TPU v7x, 1024 devices: a whole 4x8x16 slice. The times are simulated.
1024 devices in a mesh: dp: 4 (over y_lo), ctx: 32 (over y_hi, z), tp: 8 (over x, core).
Axes of the slice: x: 4, y: 8 (y_hi: 2, y_lo: 4; y = y_hi * 4 + y_lo), z: 16, core: 2. Of those that a mesh axis runs over, the one named last changes fastest.
Arguments:
- layer_input: bfloat16 [4, 4096, 8192], P('dp', 'ctx'), may hold values from -6 to 6
- queries: bfloat16 [4, 4096, 16384], P('dp', 'ctx', 'tp'), may hold values from -6 to 6
- key_heads: bfloat16 [4, 4096, 1024], P('dp', 'ctx', 'tp'), may hold values from -6 to 6
- value_heads: bfloat16 [4, 4096, 1024], P('dp', 'ctx', 'tp'), may hold values from -6 to 6
- attn_out: bfloat16 [4, 4096, 16384], P('dp', 'ctx', 'tp'), may hold values from -6 to 6
- out_grad: bfloat16 [4, 4096, 16384], P('dp', 'ctx', 'tp'), may hold values from -6 to 6
- log_sums: float32 [4, 128, 4096], P('dp', 'tp', 'ctx'), may hold values from 4 to 7
- doc_ids: int32 [4, 4096], P('dp'), may hold values from 0 to 63, never falling along the last dimension, each value on 1 to 193 neighbouring positions
Outputs:
- query_grad: bfloat16 [4, 4096, 16384], P('dp', 'ctx', 'tp')
- key_grad: bfloat16 [4, 4096, 1024], P('dp', 'ctx', 'tp')
- value_grad: bfloat16 [4, 4096, 1024], P('dp', 'ctx', 'tp')
- weight_grad: float32 [8192, 1024], P(('dp', 'ctx'), 'tp')
Inputs may be any that keep to these rules, and one draw needn't show every extreme that they name: `doc_ids`: along each sequence's positions the document ids never fall; every id names 1 to 193 positions, and one names exactly 193.
All inputs are finite; a program needn't handle non-finite values.
Results may differ from a plain program's by a relative error of at most 0.0061.
Values may be sent and summed in bfloat16 or wider, within the bound.
No kernel may reach another device: no remote copies, remote signals or barrier semaphores. Data moves between devices by JAX's collectives and lax.ppermute only.
A program may use at most 64 MiB of HBM per device.

v0:
```python
import jax
import jax.numpy as jnp
from jax import lax
from jax.sharding import Mesh
from jax.sharding import PartitionSpec as P

REACH = 4
HD = 128
CTX = ("ctx_0", "ctx_1")
DP_CTX = ("dp", "ctx_0", "ctx_1")


def with_halo(cells, sides, width):
    for axis, dim in sides:
        count = lax.axis_size(axis)
        ends = count - 1
        head = lax.slice_in_dim(cells, 0, width, axis=dim)
        tail = lax.slice_in_dim(cells, cells.shape[dim] - width, cells.shape[dim], axis=dim)
        cells = jnp.concatenate(
            [
                lax.ppermute(tail, axis, [(i, (i + 1) % count) for i in range(ends)]),
                cells,
                lax.ppermute(head, axis, [((i + 1) % count, i) for i in range(ends)]),
            ],
            axis=dim,
        )
    return cells


def sum_in_order(tiles, axes, turns):
    lengths = [lax.axis_size(a) for a in axes]
    tiles = tiles.reshape(*lengths, *tiles.shape[1:])
    tiles = tiles.transpose(*turns, *range(len(axes), tiles.ndim))
    tiles = tiles.reshape(-1, *tiles.shape[len(axes) :])
    for k in turns:
        tiles = lax.psum_scatter(tiles, axes[k], scatter_dimension=0, tiled=True)
    return tiles[0]


def cut_along(value, dim, length):
    before, after = (value.shape[:dim], value.shape[dim + 1 :])
    return jnp.moveaxis(value.reshape(*before, length, -1, *after), dim, 0)


def sum_by_axis(value, axes, turns, dim):
    length = lax.axis_size(axes)
    return sum_in_order(cut_along(value, dim, length), axes, turns)


def tile_terms(query_rows, grad_rows, lse_rows, row_delta, key_value, live_mask):
    groups = query_rows.shape[1]
    score_scale = HD ** (-0.5)
    key_rows = key_value[:, : groups * HD].reshape(-1, groups, HD)
    value_rows = key_value[:, groups * HD :].reshape(-1, groups, HD)
    scores = (
        jnp.einsum("qgrd,kgd->grqk", query_rows, key_rows, preferred_element_type=jnp.float32)
        * score_scale
    )
    soft_probs = jnp.where(live_mask, jnp.exp(scores - lse_rows[..., None]), 0.0)
    grad_value = jnp.einsum(
        "grqk,qgrd->kgd",
        soft_probs.astype(jnp.bfloat16),
        grad_rows,
        preferred_element_type=jnp.float32,
    )
    grad_probs = jnp.einsum(
        "qgrd,kgd->grqk", grad_rows, value_rows, preferred_element_type=jnp.float32
    )
    grad_scores = (soft_probs * (grad_probs - row_delta[..., None])).astype(jnp.bfloat16)
    grad_query = (
        jnp.einsum("grqk,kgd->qgrd", grad_scores, key_rows, preferred_element_type=jnp.float32)
        * score_scale
    )
    grad_key = (
        jnp.einsum("grqk,qgrd->kgd", grad_scores, query_rows, preferred_element_type=jnp.float32)
        * score_scale
    )
    key_count = key_value.shape[0]
    joined = jnp.concatenate(
        [grad_key.reshape(key_count, groups * HD), grad_value.reshape(key_count, groups * HD)],
        axis=1,
    )
    return (grad_query, joined)


def block_terms(
    reach_step,
    query_block,
    key_block,
    doc_seq,
    block_rows,
    query_rows,
    grad_rows,
    lse_rows,
    row_delta,
    key_value,
):
    query_doc = lax.dynamic_slice_in_dim(doc_seq, query_block * block_rows, block_rows)
    key_doc = lax.dynamic_slice_in_dim(doc_seq, jnp.maximum(key_block, 0) * block_rows, block_rows)
    offsets = jnp.arange(block_rows, dtype=jnp.int32)
    query_pos = query_block * block_rows + offsets
    key_pos = key_block * block_rows + offsets
    live_mask = (
        (key_pos[None, :] <= query_pos[:, None])
        & (key_doc[None, :] == query_doc[:, None])
        & (key_block >= 0)
    )
    operands = (query_rows, grad_rows, lse_rows, row_delta, key_value, live_mask)
    if reach_step == 0:
        return tile_terms(*operands)

    def compute(packed):
        return tile_terms(*packed)

    def skipped(packed):
        return (jnp.zeros(packed[0].shape, jnp.float32), jnp.zeros(packed[4].shape, jnp.float32))

    live_tile = (key_block >= 0) & (key_doc[block_rows - 1] == query_doc[0])
    return lax.cond(live_tile, compute, skipped, operands)


def body(layer_input, queries, key_heads, value_heads, attn_out, out_grad, log_sums, doc_ids):
    ctx_index = lax.axis_index(CTX)
    ctx_count = lax.axis_size(CTX)
    block_rows = queries.shape[1] // 2
    kv_width = key_heads.shape[2]
    groups = kv_width // HD
    head_count = queries.shape[2] // HD
    per_group = head_count // groups
    query_rows = queries[0].reshape(2, block_rows, groups, per_group, HD)
    grad_rows = out_grad[0].reshape(2, block_rows, groups, per_group, HD)
    out_rows = attn_out[0].reshape(2, block_rows, groups, per_group, HD)
    row_delta = jnp.sum(
        grad_rows.astype(jnp.float32) * out_rows.astype(jnp.float32), axis=-1
    ).transpose(0, 2, 3, 1)
    lse_rows = log_sums[0].reshape(groups, per_group, 2, block_rows).transpose(2, 0, 1, 3)
    doc_seq = doc_ids[0]
    own_blocks = (ctx_index, 2 * ctx_count - 1 - ctx_index)
    key_value = jnp.concatenate([key_heads[0], value_heads[0]], axis=1)
    current = (key_value[:block_rows], key_value[block_rows:])
    last_device = ctx_index == ctx_count - 1
    query_accum = [
        jnp.zeros(query_rows.shape[1:], jnp.float32),
        jnp.zeros(query_rows.shape[1:], jnp.float32),
    ]
    pieces = []
    for reach_step in range(REACH):
        if reach_step > 0:
            stacked = jnp.concatenate([current[1], current[0]], axis=0)
            padded = with_halo(stacked, ((CTX, 0),), block_rows)
            current = (
                padded[:block_rows],
                jnp.where(last_device, current[0], padded[3 * block_rows :]),
            )
        grad_terms = []
        for which_half in range(2):
            query_block = own_blocks[which_half]
            grad_query, joined = block_terms(
                reach_step,
                query_block,
                query_block - reach_step,
                doc_seq,
                block_rows,
                query_rows[which_half],
                grad_rows[which_half],
                lse_rows[which_half],
                row_delta[which_half],
                current[which_half],
            )
            query_accum[which_half] = query_accum[which_half] + grad_query
            grad_terms.append(joined)
        pieces.append(grad_terms)
    accum_first, accum_second = pieces[REACH - 1]
    for reach_step in range(REACH - 1, 0, -1):
        stacked = jnp.concatenate([accum_first, accum_second], axis=0)
        padded = with_halo(stacked, ((CTX, 0),), block_rows)
        accum_first, accum_second = (
            jnp.where(last_device, accum_second, padded[3 * block_rows :])
            + pieces[reach_step - 1][0],
            padded[:block_rows] + pieces[reach_step - 1][1],
        )
    kv_grad = jnp.concatenate([accum_first, accum_second], axis=0)
    key_grad = kv_grad[:, :kv_width].astype(jnp.bfloat16)
    value_grad = kv_grad[:, kv_width:].astype(jnp.bfloat16)
    query_grad = (
        jnp.concatenate(query_accum, axis=0)
        .reshape(1, 2 * block_rows, head_count * HD)
        .astype(jnp.bfloat16)
    )
    tokens = layer_input[0]
    weight_scale = (lax.axis_size("dp") * doc_seq.shape[0]) ** (-0.5)
    weight_grad = sum_by_axis(
        jnp.einsum("td,tc->dc", tokens, value_grad, preferred_element_type=jnp.float32)
        * weight_scale,
        DP_CTX,
        (2, 0, 1),
        0,
    )
    return (query_grad, key_grad[None], value_grad[None], weight_grad)


def solution(mesh):
    split = Mesh(
        mesh.devices.reshape(mesh.shape["dp"], 2, 16, mesh.shape["tp"]),
        ("dp", "ctx_0", "ctx_1", "tp"),
    )
    in_specs = (
        P("dp", CTX, None),
        P("dp", CTX, "tp"),
        P("dp", CTX, "tp"),
        P("dp", CTX, "tp"),
        P("dp", CTX, "tp"),
        P("dp", CTX, "tp"),
        P("dp", "tp", CTX),
        P("dp", None),
    )
    out_specs = (P("dp", CTX, "tp"), P("dp", CTX, "tp"), P("dp", CTX, "tp"), P(DP_CTX, "tp"))
    return jax.shard_map(body, mesh=split, in_specs=in_specs, out_specs=out_specs, check_vma=False)
```

profile of v0, /device:TPU:1, one launch (start us, length us, event | category | flops | bytes accessed | tf_op | source)
XLA Modules:
  0.0 324.5 jit_solution(3092280668861813501)
XLA Ops:
  7.2 1.5 pad_maximum_fusion.7
  16.4 1.5 constant_dynamic-slice_fusion.7
  19.6 2.2 fusion.162
  22.5 5.5 %collective-permute-start = (bf16[64,256]{1,0:T(8,128)(2,1)S(1)}, bf16[64,256]{1,0:T(8,128)(2,1)S(1)}, u32[]{:S(2)}, u32[]{:S(2)}) collective-permute-start(bf16[64,256]{1,0:T(8,128)(2,1)S(1)} %get-tuple-element.532), channel_id=1, source_target_pairs={{0,8},{8,16},{16,24},{24,32},{32,40},{40,48},{48,56},{56,64},{64,7... | collective-permute-start | bytes 98312 | tf_op jit(solution)/shard_map/ppermute | solution.py:21
  29.7 5.2 %collective-permute-start.1 = (bf16[64,256]{1,0:T(8,128)(2,1)S(1)}, bf16[64,256]{1,0:T(8,128)(2,1)}, u32[]{:S(2)}, u32[]{:S(2)}) collective-permute-start(bf16[64,256]{1,0:T(8,128)(2,1)S(1)} %collective-permute-done), channel_id=1, source_target_pairs={{0,8},{8,16},{16,24},{24,32},{32,40},{40,48},{48,56},{56,64},{64,7... | collective-permute-start | bytes 98312 | tf_op jit(solution)/shard_map/ppermute | solution.py:21
  34.9 1.8 fusion.170
  39.4 3.4 %collective-permute-start.2 = (bf16[64,256]{1,0:T(8,128)(2,1)}, bf16[64,256]{1,0:T(8,128)(2,1)S(1)}, u32[]{:S(2)}, u32[]{:S(2)}) collective-permute-start(bf16[64,256]{1,0:T(8,128)(2,1)} %collective-permute-done.1), channel_id=1, source_target_pairs={{0,8},{8,16},{16,24},{24,32},{32,40},{40,48},{48,56},{56,64},{64,7... | collective-permute-start | bytes 98312 | tf_op jit(solution)/shard_map/ppermute | solution.py:21
  46.3 1.5 conditional.8
  58.1 15.6 %collective-permute-start.6 = (f32[64,256]{1,0:T(8,128)}, f32[64,256]{1,0:T(8,128)}, u32[]{:S(2)}, u32[]{:S(2)}) collective-permute-start(f32[64,256]{1,0:T(8,128)} %get-tuple-element.305), channel_id=1, source_target_pairs={{0,8},{8,16},{16,24},{24,32},{32,40},{40,48},{48,56},{56,64},{64,7... | collective-permute-start | bytes 196616 | tf_op jit(solution)/shard_map/ppermute | solution.py:21
  74.6 1.5 select_add_fusion.1
  77.4 1.8 fusion.171
  84.9 1.5 select_add_fusion
  87.7 15.8 %collective-permute-start.7 = (f32[64,256]{1,0:T(8,128)}, f32[64,256]{1,0:T(8,128)}, u32[]{:S(2)}, u32[]{:S(2)}) collective-permute-start(f32[64,256]{1,0:T(8,128)} %get-tuple-element.530), channel_id=1, source_target_pairs={{0,8},{8,16},{16,24},{24,32},{32,40},{40,48},{48,56},{56,64},{64,7... | collective-permute-start | bytes 196616 | tf_op jit(solution)/shard_map/ppermute | solution.py:21
  103.5 1.9 convolution_bitcast_fusion.22
  107.2 5.7 %conditional.9 = (f32[64,1,16,128]{3,0,2,1:T(8,128)S(1)}, f32[64,256]{1,0:T(8,128)S(1)}) conditional(s32[]{:T(128)} %convert_element_type.119, () %tuple.62, (s32[]{:T(128)}, s32[1,64]{1,0:T(1,128)}, s32[64,64]{0,1:T(8,128)S(1)}, s32[1,64]{1,0:T(1,128)S(1)}, s32[64,64]{0,1:T(8,128)S(1)}, /*index=5*/pred[]{:T(512)}, bf16[64,256]{1,0:T(8,128)(2,1)}, ...), branch_computations={%region_7.8_spmd, %region_8.9_spmd} | conditional | flops 84516928 | bytes 3056673 | solution.py:119
  114.0 2.9 collective-permute-start.11
  118.9 2.7 fusion.150
  121.6 5.6 %copy.139 = f32[8192,128]{1,0:T(8,128)} copy(f32[8192,128]{0,1:T(8,128)} %fusion.150) | data formatting | bytes 8388608 | tf_op jit(solution)/shard_map/mul | solution.py:193
  127.2 4.8 %copy.140 = f32[16,4,2,64,128]{4,3,2,1,0:T(8,128)} copy(f32[16,4,2,64,128]{4,3,0,2,1:T(8,128)} %bitcast.590) | data formatting | bytes 8388608 | tf_op jit(solution)/shard_map/transpose | solution.py:33
  133.5 110.4 %reduce-scatter.4.cloned.1.call-done = f32[8,64,128]{2,1,0:T(8,128)} async-done(((f32[128,64,128]{2,1,0:T(8,128)}), f32[8,64,128]{2,1,0:T(8,128)}) %reduce-scatter.4.cloned.1.call-update) | async-done | bytes 262160 | tf_op jit(solution)/shard_map/reduce_scatter | solution.py:36
  243.9 1.5 add_convert_fusion
  245.4 1.5 add_convert_fusion.1
  248.3 37.3 %reduce-scatter.6.cloned.1.call-done = f32[2,64,128]{2,1,0:T(8,128)} async-done(((f32[8,64,128]{2,1,0:T(8,128)}), f32[2,64,128]{2,1,0:T(8,128)}) %reduce-scatter.6.cloned.1.call-update) | async-done | bytes 65552 | tf_op jit(solution)/shard_map/reduce_scatter | solution.py:36
  286.2 31.8 %reduce-scatter.8.cloned.1.call-done = f32[1,64,128]{2,1,0:T(8,128)} async-done(((f32[2,64,128]{2,1,0:T(8,128)}), f32[1,64,128]{2,1,0:T(8,128)}) %reduce-scatter.8.cloned.1.call-update) | async-done | bytes 32784 | tf_op jit(solution)/shard_map/reduce_scatter | solution.py:36
  (149 shorter events, 49.8 us)
Async XLA Ops:
  7.2 111.7 %copy-start = (bf16[1,128,8192]{2,1,0:T(8,128)(2,1)S(1)}, bf16[1,128,8192]{2,1,0:T(8,128)(2,1)}, u32[]{:S(2)}) copy-start(bf16[1,128,8192]{2,1,0:T(8,128)(2,1)} %param.20) | copy-start | bytes 6291460
  7.2 236.7 %reduce-scatter.4.cloned.1.call-start = ((), (), s32[]{:S(2)}) async-start(), calls=%async_computation.3 | async-start | bytes 4456448 | tf_op jit(solution)/shard_map/reduce_scatter | solution.py:36
  8.7 13.7 %collective-permute-start.3 = (bf16[64,256]{1,0:T(8,128)(2,1)}, bf16[64,256]{1,0:T(8,128)(2,1)S(1)}, u32[]{:S(2)}, u32[]{:S(2)}) collective-permute-start(bf16[64,256]{1,0:T(8,128)(2,1)} %pad_maximum_fusion.7), channel_id=1, source_target_pairs={{8,0},{16,8},{24,16},{32,24},{40,32},{48,40},{56,48},{64,56},{72,6... | collective-permute-start | bytes 98312 | tf_op jit(solution)/shard_map/ppermute | solution.py:23
  10.9 35.4 %copy-start.18 = (f32[1,1,16,64]{3,0,2,1:T(1,128)}, f32[1,1,16,64]{3,0,2,1:T(1,128)S(1)}, u32[]{:S(2)}) copy-start(f32[1,1,16,64]{3,0,2,1:T(1,128)S(1)} %get-tuple-element.553) | copy-start | bytes 12292
  18.0 20.6 %copy-start.19 = (s32[1,64]{1,0:T(1,128)}, s32[1,64]{1,0:T(1,128)S(1)}, u32[]{:S(2)}) copy-start(s32[1,64]{1,0:T(1,128)S(1)} %get-tuple-element.545) | copy-start | bytes 772
  18.0 20.6 %copy-start.21 = (s32[1,64]{1,0:T(1,128)}, s32[1,64]{1,0:T(1,128)S(1)}, u32[]{:S(2)}) copy-start(s32[1,64]{1,0:T(1,128)S(1)} %get-tuple-element.549) | copy-start | bytes 772
  22.5 22.4 %copy-start.12 = (bf16[64,256]{1,0:T(8,128)(2,1)}, bf16[64,256]{1,0:T(8,128)(2,1)S(1)}, u32[]{:S(2)}) copy-start(bf16[64,256]{1,0:T(8,128)(2,1)S(1)} %get-tuple-element.531) | copy-start | bytes 98308
  22.5 7.2 %collective-permute-start = (bf16[64,256]{1,0:T(8,128)(2,1)S(1)}, bf16[64,256]{1,0:T(8,128)(2,1)S(1)}, u32[]{:S(2)}, u32[]{:S(2)}) collective-permute-start(bf16[64,256]{1,0:T(8,128)(2,1)S(1)} %get-tuple-element.532), channel_id=1, source_target_pairs={{0,8},{8,16},{16,24},{24,32},{32,40},{40,48},{48,56},{56,64},{64,7... | collective-permute-start | bytes 98312 | tf_op jit(solution)/shard_map/ppermute | solution.py:21
  28.4 14.5 %collective-permute-start.4 = (bf16[64,256]{1,0:T(8,128)(2,1)S(1)}, bf16[64,256]{1,0:T(8,128)(2,1)}, u32[]{:S(2)}, u32[]{:S(2)}) collective-permute-start(bf16[64,256]{1,0:T(8,128)(2,1)S(1)} %get-tuple-element.531), channel_id=1, source_target_pairs={{8,0},{16,8},{24,16},{32,24},{40,32},{48,40},{56,48},{64,56},{72,6... | collective-permute-start | bytes 98312 | tf_op jit(solution)/shard_map/ppermute | solution.py:23
  29.7 9.8 %collective-permute-start.1 = (bf16[64,256]{1,0:T(8,128)(2,1)S(1)}, bf16[64,256]{1,0:T(8,128)(2,1)}, u32[]{:S(2)}, u32[]{:S(2)}) collective-permute-start(bf16[64,256]{1,0:T(8,128)(2,1)S(1)} %collective-permute-done), channel_id=1, source_target_pairs={{0,8},{8,16},{16,24},{24,32},{32,40},{40,48},{48,56},{56,64},{64,7... | collective-permute-start | bytes 98312 | tf_op jit(solution)/shard_map/ppermute | solution.py:21
  39.4 5.5 %collective-permute-start.2 = (bf16[64,256]{1,0:T(8,128)(2,1)}, bf16[64,256]{1,0:T(8,128)(2,1)S(1)}, u32[]{:S(2)}, u32[]{:S(2)}) collective-permute-start(bf16[64,256]{1,0:T(8,128)(2,1)} %collective-permute-done.1), channel_id=1, source_target_pairs={{0,8},{8,16},{16,24},{24,32},{32,40},{40,48},{48,56},{56,64},{64,7... | collective-permute-start | bytes 98312 | tf_op jit(solution)/shard_map/ppermute | solution.py:21
  43.6 11.9 %collective-permute-start.5 = (bf16[64,256]{1,0:T(8,128)(2,1)S(1)}, bf16[64,256]{1,0:T(8,128)(2,1)}, u32[]{:S(2)}, u32[]{:S(2)}) collective-permute-start(bf16[64,256]{1,0:T(8,128)(2,1)S(1)} %broadcast_select_fusion), channel_id=1, source_target_pairs={{8,0},{16,8},{24,16},{32,24},{40,32},{48,40},{56,48},{64,56},{72,6... | collective-permute-start | bytes 98312 | tf_op jit(solution)/shard_map/ppermute | solution.py:23
  47.8 26.8 %collective-permute-start.8 = (f32[64,256]{1,0:T(8,128)}, f32[64,256]{1,0:T(8,128)}, u32[]{:S(2)}, u32[]{:S(2)}) collective-permute-start(f32[64,256]{1,0:T(8,128)} %get-tuple-element.308), channel_id=1, source_target_pairs={{8,0},{16,8},{24,16},{32,24},{40,32},{48,40},{56,48},{64,56},{72,6... | collective-permute-start | bytes 196616 | tf_op jit(solution)/shard_map/ppermute | solution.py:23
  50.5 26.8 %copy-start.6 = (bf16[16,64,64]{1,2,0:T(8,128)(2,1)}, bf16[16,64,64]{1,2,0:T(8,128)(2,1)S(1)}, u32[]{:S(2)}) copy-start(bf16[16,64,64]{1,2,0:T(8,128)(2,1)S(1)} %fusion.168) | copy-start | bytes 393220
  58.1 22.3 %copy-start.20 = (s32[1,64]{1,0:T(1,128)S(1)}, s32[1,64]{1,0:T(1,128)}, u32[]{:S(2)}) copy-start(s32[1,64]{1,0:T(1,128)} %copy-done.19) | copy-start | bytes 772
  58.1 24.3 %copy-start.22 = (s32[1,64]{1,0:T(1,128)S(1)}, s32[1,64]{1,0:T(1,128)}, u32[]{:S(2)}) copy-start(s32[1,64]{1,0:T(1,128)} %copy-done.21) | copy-start | bytes 772
  58.1 26.8 %collective-permute-start.6 = (f32[64,256]{1,0:T(8,128)}, f32[64,256]{1,0:T(8,128)}, u32[]{:S(2)}, u32[]{:S(2)}) collective-permute-start(f32[64,256]{1,0:T(8,128)} %get-tuple-element.305), channel_id=1, source_target_pairs={{0,8},{8,16},{16,24},{24,32},{32,40},{40,48},{48,56},{56,64},{64,7... | collective-permute-start | bytes 196616 | tf_op jit(solution)/shard_map/ppermute | solution.py:21
  76.1 8.9 %collective-permute-start.9 = (f32[64,256]{1,0:T(8,128)}, f32[64,256]{1,0:T(8,128)}, u32[]{:S(2)}, u32[]{:S(2)}) collective-permute-start(f32[64,256]{1,0:T(8,128)} %select_add_fusion.1), channel_id=1, source_target_pairs={{8,0},{16,8},{24,16},{32,24},{40,32},{48,40},{56,48},{64,56},{72,6... | collective-permute-start | bytes 196616 | tf_op jit(solution)/shard_map/ppermute | solution.py:23
  83.3 22.2 %copy-start.25 = (s32[1,64]{1,0:T(1,128)S(1)}, s32[1,64]{1,0:T(1,128)}, u32[]{:S(2)}) copy-start(s32[1,64]{1,0:T(1,128)} %get-tuple-element.544) | copy-start | bytes 772
  86.4 26.5 %collective-permute-start.10 = (f32[64,256]{1,0:T(8,128)}, f32[64,256]{1,0:T(8,128)}, u32[]{:S(2)}, u32[]{:S(2)}) collective-permute-start(f32[64,256]{1,0:T(8,128)} %get-tuple-element.529), channel_id=1, source_target_pairs={{8,0},{16,8},{24,16},{32,24},{40,32},{48,40},{56,48},{64,56},{72,6... | collective-permute-start | bytes 196616 | tf_op jit(solution)/shard_map/ppermute | solution.py:23
  87.7 25.2 %collective-permute-start.7 = (f32[64,256]{1,0:T(8,128)}, f32[64,256]{1,0:T(8,128)}, u32[]{:S(2)}, u32[]{:S(2)}) collective-permute-start(f32[64,256]{1,0:T(8,128)} %get-tuple-element.530), channel_id=1, source_target_pairs={{0,8},{8,16},{16,24},{24,32},{32,40},{40,48},{48,56},{56,64},{64,7... | collective-permute-start | bytes 196616 | tf_op jit(solution)/shard_map/ppermute | solution.py:21
  114.0 4.1 %collective-permute-start.11 = (f32[64,256]{1,0:T(8,128)S(1)}, f32[64,256]{1,0:T(8,128)S(1)}, u32[]{:S(2)}, u32[]{:S(2)}) collective-permute-start(f32[64,256]{1,0:T(8,128)S(1)} %get-tuple-element.528), channel_id=1, source_target_pairs={{0,8},{8,16},{16,24},{24,32},{32,40},{40,48},{48,56},{56,64},{64,7... | collective-permute-start | bytes 196616 | tf_op jit(solution)/shard_map/ppermute | solution.py:21
  132.0 153.5 %reduce-scatter.6.cloned.1.call-start = ((), (), s32[]{:S(2)}) async-start(), calls=%async_computation.4 | async-start | bytes 327680 | tf_op jit(solution)/shard_map/reduce_scatter | solution.py:36
  243.9 74.1 %reduce-scatter.8.cloned.1.call-start = ((), (), s32[]{:S(2)}) async-start(), calls=%async_computation.5 | async-start | bytes 98304 | tf_op jit(solution)/shard_map/reduce_scatter | solution.py:36
  (17 other events, 124.4 us)
Sparse Core Ops, SparseCore 0:
  132.1 111.6 reduce-scatter.3
  247.2 38.2 reduce-scatter.5
  289.8 28.1 reduce-scatter.7
where the time goes:
time: 327 us; the launch traced here: 324 us
  waiting for transfers between devices  180 us (55%)
  starting transfers between devices  56.2 us (17%)
  local copies, waits for them, and re-layouts  36.4 us (11%)
  between operations  19.6 us (6%)
  matrix products  19.1 us (6%)
  other arithmetic  12.8 us (4%)
    reduce_scatter x3, waiting for transfers between devices, sum_in_order(): tiles = lax.psum_scatter(tiles, axes[k], scatter_dimension=0, tiled=True)  179 us
    ppermute x6, starting transfers between devices, with_halo(): lax.ppermute(tail, axis, [(i, (i + 1) % count) for i in range(ends)])  48.3 us
    ppermute x6, starting transfers between devices, with_halo(): lax.ppermute(head, axis, [((i + 1) % count, i) for i in range(ends)])  7.69 us
    slice x6, local copies, waits for them, and re-layouts, block_terms(): live_tile = (key_block >= 0) & (key_doc[block_rows - 1] == query_doc[0])  6.83 us
    unnamed x60, local copies, waits for them, and re-layouts  6.66 us
  transfers between devices with their start and end apart: 15, of which 4 were waited for; matrix products, arithmetic and copies ran while one was open for 15% of the time, Pallas kernels for 0%

commit v1 on v0

v1 whole, which is shorter than its diff:
```python
import functools

import jax
import jax.numpy as jnp
from jax import lax
from jax.experimental import pallas as pl
from jax.experimental.pallas import tpu as pltpu
from jax.sharding import Mesh
from jax.sharding import PartitionSpec as P

HD = 128
C = 64
CTX = ("ctx_0", "ctx_1")
ROWS = ("dp", "ctx_0")
DP_CTX = ("dp", "ctx_0", "ctx_1")
SCALE = HD ** (-0.5)
BF = jnp.bfloat16
F32 = jnp.float32
SMEM = pl.BlockSpec(memory_space=pltpu.SMEM)
VMEM = pl.BlockSpec(memory_space=pltpu.VMEM)


def call(kernel, outs, n_in, flops, scratch=()):
    return pl.pallas_call(
        kernel,
        out_shape=outs,
        in_specs=[SMEM] + [VMEM] * (n_in - 1),
        out_specs=[VMEM] * len(outs),
        scratch_shapes=list(scratch),
        compiler_params=pltpu.CompilerParams(vmem_limit_bytes=40 * 1024 * 1024),
        cost_estimate=pl.CostEstimate(flops=flops, bytes_accessed=1 << 20, transcendentals=0),
    )


def shape(dims, dtype):
    return jax.ShapeDtypeStruct(dims, dtype)


def doc_pair(doc_ref, block):
    first = jnp.maximum(block - 1, 0)
    chunk = first // 2
    ahead = jnp.minimum(chunk + 1, doc_ref.shape[1] // 128 - 1)
    here = doc_ref[:, pl.ds(pl.multiple_of(chunk * 128, 128), 128)]
    after = doc_ref[:, pl.ds(pl.multiple_of(ahead * 128, 128), 128)]
    lane = lax.broadcasted_iota(jnp.int32, (1, 128), 1)
    crossing = jnp.where(lane < C, pltpu.roll(here, C, 1), pltpu.roll(after, C, 1))
    start = jnp.where(block - 1 < 0, pltpu.roll(here, C, 1), here)
    return jnp.where(first % 2 == 0, start, crossing)


def live_pair(doc_ref, query_block, key_block):
    row = lax.broadcasted_iota(jnp.int32, (C, 128), 0)
    lane = lax.broadcasted_iota(jnp.int32, (C, 128), 1)
    own = doc_pair(doc_ref, query_block)
    query_doc = jnp.sum(jnp.where(lane == row + C, own, 0), axis=1, keepdims=True)
    key_doc = doc_pair(doc_ref, key_block)
    key_pos = (key_block - 1) * C + lane
    query_pos = query_block * C + row
    return (key_doc == query_doc) & (key_pos <= query_pos) & (key_pos >= 0)


def attend(q_ref, g_ref, o_ref, lse_ref, keys, values, live, kv_acc, write_query):
    heads = q_ref.shape[1] // HD
    group = min(4, heads)
    row = lax.broadcasted_iota(jnp.int32, (C, 128), 0)
    lane = lax.broadcasted_iota(jnp.int32, (C, 128), 1)

    def step(at, carry):
        lanes = pl.ds(pl.multiple_of(at * group * HD, group * HD), group * HD)
        for half in range(2):
            rows = slice(half * C, half * C + C)

            def stacked(ref):
                wide = ref[rows, lanes]
                return jnp.concatenate([wide[:, i * HD : (i + 1) * HD] for i in range(group)], axis=0)

            q, g, o = stacked(q_ref), stacked(g_ref), stacked(o_ref)
            delta = jnp.sum(g.astype(F32) * o.astype(F32), axis=1, keepdims=True)
            lse = jnp.concatenate(
                [
                    jnp.sum(
                        jnp.where(lane == row + half * C, lse_ref[pl.ds(at * group + i, 1), :], 0.0),
                        axis=1,
                        keepdims=True,
                    )
                    for i in range(group)
                ],
                axis=0,
            )
            k, v = keys[half], values[half]
            dims = (((1,), (1,)), ((), ()))
            s = lax.dot_general(q, k, dims, preferred_element_type=F32)
            mask = jnp.concatenate([live[half]] * group, axis=0)
            p = jnp.where(mask > 0.0, jnp.exp(s * SCALE - lse), 0.0)
            dp = lax.dot_general(g, v, dims, preferred_element_type=F32)
            ds = (p * (dp - delta)).astype(BF)
            dq = jnp.dot(ds, k, preferred_element_type=F32) * SCALE
            tdims = (((0,), (0,)), ((), ()))
            dk = lax.dot_general(ds, q, tdims, preferred_element_type=F32) * SCALE
            dv = lax.dot_general(p.astype(BF), g, tdims, preferred_element_type=F32)
            kv_acc[half, :, :HD] += dk
            kv_acc[half, :, HD:] += dv
            wide = jnp.concatenate([dq[i * C : (i + 1) * C] for i in range(group)], axis=1)
            write_query(rows, lanes, wide)
        return carry

    kv_acc[...] = jnp.zeros_like(kv_acc)
    lax.fori_loop(0, heads // group, step, 0)


def pick(where, a, b):
    return jnp.where(where, a.astype(F32), b.astype(F32))


def pack_kernel(k_ref, v_ref, out_ref):
    out_ref[:, :HD] = k_ref[0]
    out_ref[:, HD:] = v_ref[0]


def widen_kernel(count, idx_ref, own_ref, left_ref, right_ref, low_ref, high_ref):
    last = idx_ref[0] == count - 1
    low_ref[:C] = left_ref[:C]
    low_ref[C:] = own_ref[:C]
    high_ref[:C] = pick(last, own_ref[:C], right_ref[C:]).astype(BF)
    high_ref[C:] = own_ref[C:]


def near_kernel(
    count, idx_ref, q_ref, g_ref, o_ref, lse_ref, doc_ref, low_ref, high_ref, dq_ref, kv_ref, live_ref
):
    place = idx_ref[0]
    for half, block in enumerate((place, 2 * count - 1 - place)):
        live_ref[half] = live_pair(doc_ref, block, block).astype(F32)
    keys = (low_ref[:, :HD], high_ref[:, :HD])
    values = (low_ref[:, HD:], high_ref[:, HD:])

    def write(rows, lanes, value):
        dq_ref[rows, lanes] = value

    attend(q_ref, g_ref, o_ref, lse_ref, keys, values, live_ref, kv_ref, write)


def far_kernel(
    count,
    idx_ref,
    q_ref,
    g_ref,
    o_ref,
    lse_ref,
    doc_ref,
    own_ref,
    left_ref,
    right_ref,
    left2_ref,
    right2_ref,
    near_ref,
    dq_ref,
    low_ref,
    high_ref,
    live_ref,
    acc_ref,
):
    place = idx_ref[0]
    last, before = place == count - 1, place == count - 2
    for half, block in enumerate((place, 2 * count - 1 - place)):
        live_ref[half] = live_pair(doc_ref, block, block - 2).astype(F32)
    third = pick(before, own_ref[:C], pick(last, left2_ref[C:], right2_ref[:C])).astype(BF)
    second = pick(before, right_ref[:C], pick(last, left_ref[:C], right2_ref[C:])).astype(BF)
    upper = jnp.concatenate([third, second], axis=0)
    keys = (left2_ref[:, :HD], upper[:, :HD])
    values = (left2_ref[:, HD:], upper[:, HD:])

    def write(rows, lanes, value):
        dq_ref[0, rows, lanes] = (value + near_ref[rows, lanes]).astype(BF)

    attend(q_ref, g_ref, o_ref, lse_ref, keys, values, live_ref, acc_ref, write)
    low_ref[:C] = acc_ref[0, :C].astype(BF)
    low_ref[C:] = (acc_ref[0, C:] + jnp.where(last, acc_ref[1, :C], 0.0)).astype(BF)
    high_ref[...] = acc_ref[1].astype(BF)


def turn_kernel(count, idx_ref, kv_ref, high_ref, low2_ref, high2_ref, left_ref, right_ref):
    last = idx_ref[0] == count - 1
    mine = jnp.where(last, high_ref[C:].astype(F32), 0.0)
    left_ref[...] = (kv_ref[0, :C] + low2_ref[:C].astype(F32) + mine).astype(BF)
    right_ref[:C] = (kv_ref[1, :C] + high2_ref[:C].astype(F32)).astype(BF)
    right_ref[C:] = high_ref[C:]


def close_kernel(
    count,
    idx_ref,
    kv_ref,
    high_ref,
    low2_ref,
    high2_ref,
    right_ref,
    low1_ref,
    high1_ref,
    dk_ref,
    dv_ref,
    spread_ref,
):
    place = idx_ref[0]
    last, before = place == count - 1, place == count - 2
    lower = kv_ref[0, C:] + low2_ref[C:].astype(F32) + low1_ref[...].astype(F32)
    lower += jnp.where(last, high1_ref[C:].astype(F32) + right_ref[:C].astype(F32), 0.0)
    lower += jnp.where(before, high_ref[:C].astype(F32), 0.0)
    upper = kv_ref[1, C:] + high2_ref[C:].astype(F32) + high1_ref[:C].astype(F32)
    both = jnp.concatenate([lower, upper], axis=0).astype(BF)
    dk_ref[0] = both[:, :HD]
    dv_ref[0] = both[:, HD:]
    for i in range(spread_ref.shape[0]):
        spread_ref[i] = both[:, HD:]


def chunk_kernel(x_ref, out_ref, sems):
    parts, _, width = out_ref.shape
    copies = [
        pltpu.make_async_copy(x_ref.at[0, :, pl.ds(i * width, width)], out_ref.at[i], sems.at[i])
        for i in range(parts)
    ]
    for copy in copies:
        copy.start()
    for copy in copies:
        copy.wait()


def weight_kernel(scale, x_ref, dv_ref, out_ref):
    parts, tokens, width = x_ref.shape
    x = x_ref[...].reshape(parts * tokens, width)
    dv = dv_ref[...].reshape(parts * tokens, HD)
    flat = lax.dot_general(dv, x, (((0,), (0,)), ((), ())), preferred_element_type=F32) * scale
    out_ref[...] = flat.T.astype(BF).reshape(out_ref.shape)


def shift(value, by):
    count = lax.axis_size(CTX)
    if by > 0:
        pairs = [(i, i + by) for i in range(count - by)]
    else:
        pairs = [(i - by, i) for i in range(count + by)]
    return lax.ppermute(value, CTX, pairs)


def body(layer_input, queries, key_heads, value_heads, attn_out, out_grad, log_sums, doc_ids):
    count = lax.axis_size(CTX)
    place = lax.axis_index(CTX).astype(jnp.int32).reshape(1)
    width = queries.shape[2]
    rows = 2 * C
    groups = lax.axis_size(ROWS)
    steps = lax.axis_size("ctx_1")
    heads = width // HD
    attend_flops = 10 * rows * 128 * HD * heads
    q, g, o, lse = queries[0], out_grad[0], attn_out[0], log_sums[0]
    at = functools.partial

    kv = pl.pallas_call(
        pack_kernel, out_shape=shape((rows, 2 * HD), BF), in_specs=[VMEM] * 2, out_specs=VMEM
    )(key_heads, value_heads)
    left = shift(kv, 1)
    right = shift(kv, -1)
    chunks = pl.pallas_call(
        chunk_kernel,
        out_shape=shape((groups, rows, layer_input.shape[2] // groups), BF),
        in_specs=[pl.BlockSpec(memory_space=pl.ANY)],
        out_specs=pl.BlockSpec(memory_space=pl.ANY),
        scratch_shapes=[pltpu.SemaphoreType.DMA((groups,))],
    )(layer_input)
    tokens = lax.all_to_all(chunks, ROWS, 0, 0, tiled=True)
    pair = shape((rows, 2 * HD), BF)
    low, high = call(at(widen_kernel, count), [pair, pair], 4, 0)(place, kv, left, right)
    left2 = shift(low, 2)
    right2 = shift(high, -2)
    near_query, near_kv = call(
        at(near_kernel, count),
        [shape((rows, width), F32), shape((2, 128, 2 * HD), F32)],
        8,
        attend_flops,
        [pltpu.VMEM((2, C, 128), F32)],
    )(place, q, g, o, lse, doc_ids, low, high)
    query_grad, far_low, far_high = call(
        at(far_kernel, count),
        [shape((1, rows, width), BF), pair, pair],
        12,
        attend_flops,
        [pltpu.VMEM((2, C, 128), F32), pltpu.VMEM((2, 128, 2 * HD), F32)],
    )(place, q, g, o, lse, doc_ids, kv, left, right, left2, right2, near_query)
    low2 = shift(far_low, -2)
    high2 = shift(far_high, 2)
    to_left, to_right = call(at(turn_kernel, count), [shape((C, 2 * HD), BF), pair], 5, 0)(
        place, near_kv, far_high, low2, high2
    )
    low1 = shift(to_left, -1)
    high1 = shift(to_right, 1)
    key_grad, value_grad, spread = call(
        at(close_kernel, count),
        [shape((1, rows, HD), BF), shape((1, rows, HD), BF), shape((groups, rows, HD), BF)],
        8,
        0,
    )(place, near_kv, far_high, low2, high2, to_right, low1, high1)
    spread, tokens = lax.optimization_barrier((spread, tokens))
    everyone = lax.all_to_all(spread, ROWS, 0, 0, tiled=True)
    weight_scale = (lax.axis_size("dp") * doc_ids.shape[1]) ** (-0.5)
    part = pl.pallas_call(
        at(weight_kernel, weight_scale),
        out_shape=shape((steps, tokens.shape[2] // steps, HD), BF),
        in_specs=[VMEM] * 2,
        out_specs=VMEM,
        compiler_params=pltpu.CompilerParams(vmem_limit_bytes=40 * 1024 * 1024),
    )(tokens, everyone)
    parts = lax.all_to_all(part, "ctx_1", 0, 0, tiled=True)
    weight_grad = jnp.sum(parts.astype(F32), axis=0)
    return (query_grad, key_grad, value_grad, weight_grad)


def solution(mesh):
    tall = 2 if mesh.shape["ctx"] % 2 == 0 else 1
    split = Mesh(
        mesh.devices.reshape(mesh.shape["dp"], tall, mesh.shape["ctx"] // tall, mesh.shape["tp"]),
        ("dp", "ctx_0", "ctx_1", "tp"),
    )
    in_specs = (
        P("dp", CTX, None),
        P("dp", CTX, "tp"),
        P("dp", CTX, "tp"),
        P("dp", CTX, "tp"),
        P("dp", CTX, "tp"),
        P("dp", CTX, "tp"),
        P("dp", "tp", CTX),
        P("dp", None),
    )
    out_specs = (P("dp", CTX, "tp"), P("dp", CTX, "tp"), P("dp", CTX, "tp"), P(DP_CTX, "tp"))
    return jax.shard_map(body, mesh=split, in_specs=in_specs, out_specs=out_specs, check_vma=False)
```

time: 327 us -> 205 us (0.63)
  the two profiles are of different devices: /device:TPU:1 before, /device:TPU:78 now
where the time goes in v1:
time: 205 us
  blocking collectives  74.4 us (36%)
  Pallas kernels  74.3 us (36%)
  starting transfers between devices  39.4 us (19%)
  waiting for transfers between devices  11.5 us (6%)
  local copies, waits for them, and re-layouts  3.78 us (2%)
    pallas_call x1, Pallas kernels, body(): pl.pallas_call(chunk_kernel, out_shape=shape((groups, rows, layer_input.s...  64.7 us
    all_to_all x1, blocking collectives, body(): everyone = lax.all_to_all(spread, ROWS, 0, 0, tiled=True)  45.2 us
    ppermute x8, starting transfers between devices, shift(): return lax.ppermute(value, CTX, pairs)  31.7 us
    all_to_all x1, blocking collectives, body(): parts = lax.all_to_all(part, 'ctx_1', 0, 0, tiled=True)  29.2 us
    ppermute x8, waiting for transfers between devices, shift(): return lax.ppermute(value, CTX, pairs)  11.5 us
    all_to_all x1, starting transfers between devices, body(): tokens = lax.all_to_all(chunks, ROWS, 0, 0, tiled=True)  7.69 us
  transfers between devices with their start and end apart: 9, of which 6 were waited for; matrix products, arithmetic and copies ran while one was open for 0% of the time, Pallas kernels for 4%

profile of v1, /device:TPU:78, one launch (start us, length us, event | category | flops | bytes accessed | tf_op | source)
XLA Modules:
  0.0 204.8 jit_solution(12250342908619636183)
XLA Ops:
  0.6 64.7 %shard_map.117 = bf16[8,128,1024]{2,1,0:T(8,128)(2,1)} custom-call(bf16[1,128,8192]{2,1,0:T(8,128)(2,1)} %x_ref.1), custom_call_target="tpu_custom_call" | custom-call | tf_op jit(solution)/shard_map/pallas_call | solution.py:263
  65.4 7.7 %all-to-all-start = ((bf16[8,128,1024]{2,1,0:T(8,128)(2,1)}), bf16[8,128,1024]{2,1,0:T(8,128)(2,1)S(1)}, u32[]{:S(2)}, u32[]{:S(2)}) async-start(bf16[8,128,1024]{2,1,0:T(8,128)(2,1)} %shard_map.117), calls=%async_computation | async-start | bytes 4194304 | tf_op jit(solution)/shard_map/all_to_all | solution.py:270
  73.1 1.4 shard_map.111.own_ref
  74.5 1.9 collective-permute-start.1
  76.4 4.3 %collective-permute-start = (bf16[128,256]{1,0:T(8,128)(2,1)}, bf16[128,256]{1,0:T(8,128)(2,1)S(1)}, u32[]{:S(2)}, u32[]{:S(2)}) collective-permute-start(bf16[128,256]{1,0:T(8,128)(2,1)} %shard_map.111.own_ref), channel_id=1, source_target_pairs={{0,8},{8,16},{16,24},{24,32},{32,40},{40,48},{48,56},{56,64},{64,7... | collective-permute-start | bytes 196616 | tf_op jit(solution)/shard_map/ppermute | solution.py:243
  81.2 1.7 collective-permute-done.left_ref
  82.9 0.8 copy-done.4
  83.8 7.3 %collective-permute-start.2 = (bf16[128,256]{1,0:T(8,128)(2,1)S(1)}, bf16[128,256]{1,0:T(8,128)(2,1)S(1)}, u32[]{:S(2)}, u32[]{:S(2)}) collective-permute-start(bf16[128,256]{1,0:T(8,128)(2,1)S(1)} %get-tuple-element.18.low_ref), channel_id=1, source_target_pairs={{0,16},{8,24},{16,32},{24,40},{32,48},{40,56},{48,64},{56,72},{64,... | collective-permute-start | bytes 196616 | tf_op jit(solution)/shard_map/ppermute | solution.py:243
  91.1 1.3 collective-permute-start.3
  92.4 1.0 copy-done.2
  93.4 3.1 %shard_map.113 = (f32[128,2048]{1,0:T(8,128)S(1)}, f32[2,128,256]{2,1,0:T(8,128)S(1)}) custom-call(s32[1]{0:T(128)} %bitcast.idx_ref, bf16[128,2048]{1,0:T(8,128)(2,1)S(1)} %bitcast.5, bf16[128,2048]{1,0:T(8,128)(2,1)S(1)} %bitcast.7, bf16[128,2048]{1,0:T(8,128)(2,1)S(1)} %bitcast.9, f32[16,128]{1,0:T(8,128)S(1)} %bitcast.11, s32[1,4096]{1,0:T(1,128)S(1)} %copy-done.6, ...), custom_call_target="tpu_custom_call" | custom-call | flops 335544320 | bytes 1048576 | tf_op jit(solution)/shard_map/pallas_call | solution.py:275
  96.6 3.5 %collective-permute-done.3.right2_ref = bf16[128,256]{1,0:T(8,128)(2,1)S(1)} collective-permute-done((bf16[128,256]{1,0:T(8,128)(2,1)S(1)}, bf16[128,256]{1,0:T(8,128)(2,1)S(1)}, u32[]{:S(2)}, u32[]{:S(2)}) %collective-permute-start.3) | collective-permute-done | bytes 65568 | tf_op jit(solution)/shard_map/ppermute | solution.py:243
  100.1 1.0 copy-done.3
  101.1 0.8 copy-done.5
  102.0 3.8 %shard_map.114 = (bf16[1,128,2048]{2,1,0:T(8,128)(2,1)}, bf16[128,256]{1,0:T(8,128)(2,1)S(1)}, bf16[128,256]{1,0:T(8,128)(2,1)S(1)}) custom-call(s32[1]{0:T(128)} %bitcast.idx_ref, bf16[128,2048]{1,0:T(8,128)(2,1)S(1)} %bitcast.6, bf16[128,2048]{1,0:T(8,128)(2,1)S(1)} %bitcast.8, bf16[128,2048]{1,0:T(8,128)(2,1)S(1)} %bitcast.10, f32[16,128]{1,0:T(8,128)S(1)} %bitcast.12, ...), custom_call_target="tpu_custom_call" | custom-call | flops 335544320 | bytes 1048576 | tf_op jit(solution)/shard_map/pallas_call | solution.py:282
  105.8 1.3 collective-permute-start.4
  107.1 7.3 %collective-permute-start.5 = (bf16[128,256]{1,0:T(8,128)(2,1)S(1)}, bf16[128,256]{1,0:T(8,128)(2,1)S(1)}, u32[]{:S(2)}, u32[]{:S(2)}) collective-permute-start(bf16[128,256]{1,0:T(8,128)(2,1)S(1)} %get-tuple-element.23.high_ref), channel_id=1, source_target_pairs={{0,16},{8,24},{16,32},{24,40},{32,48},{40,56},{48,64},{56,72},{64,... | collective-permute-start | bytes 196616 | tf_op jit(solution)/shard_map/ppermute | solution.py:243
  114.7 1.6 collective-permute-done.5.high2_ref
  116.3 6.4 %collective-permute-start.7 = (bf16[128,256]{1,0:T(8,128)(2,1)S(1)}, bf16[128,256]{1,0:T(8,128)(2,1)S(1)}, u32[]{:S(2)}, u32[]{:S(2)}) collective-permute-start(bf16[128,256]{1,0:T(8,128)(2,1)S(1)} %get-tuple-element.25.right_ref), channel_id=1, source_target_pairs={{0,8},{8,16},{16,24},{24,32},{32,40},{40,48},{48,56},{56,64},{64,7... | collective-permute-start | bytes 196616 | tf_op jit(solution)/shard_map/ppermute | solution.py:243
  122.7 1.9 collective-permute-start.6
  124.7 3.9 %collective-permute-done.6.low1_ref = bf16[64,256]{1,0:T(8,128)(2,1)S(1)} collective-permute-done((bf16[64,256]{1,0:T(8,128)(2,1)S(1)}, bf16[64,256]{1,0:T(8,128)(2,1)S(1)}, u32[]{:S(2)}, u32[]{:S(2)}) %collective-permute-start.6) | collective-permute-done | bytes 32800 | tf_op jit(solution)/shard_map/ppermute | solution.py:243
  128.5 0.7 shard_map.116
  129.2 45.2 %all_to_all.15.dv_ref = bf16[8,128,128]{2,1,0:T(8,128)(2,1)S(1)} all-to-all(bf16[8,128,128]{2,1,0:T(8,128)(2,1)S(1)} %get-tuple-element.31), channel_id=1, replica_groups=mesh['dp'=4,'ctx_0'=2,'ctx_1'=16,'tp'=8] {'dp','ctx_0'}, dimensions={0} | all-to-all | bytes 524288 | tf_op jit(solution)/shard_map/all_to_all | solution.py:303
  174.9 29.2 %all_to_all.16 = bf16[16,64,128]{2,1,0:T(8,128)(2,1)S(1)} all-to-all(bf16[16,64,128]{2,1,0:T(8,128)(2,1)S(1)} %shard_map.118), channel_id=1, replica_groups=mesh['dp'=4,'ctx_0'=2,'ctx_1'=16,'tp'=8] {'ctx_1'}, dimensions={0} | all-to-all | bytes 524288 | tf_op jit(solution)/shard_map/all_to_all | solution.py:312
  (21 shorter events, 2.1 us)
Async XLA Ops:
  65.3 27.0 %copy-start = (bf16[1,128,2048]{2,1,0:T(8,128)(2,1)S(1)}, bf16[1,128,2048]{2,1,0:T(8,128)(2,1)}, u32[]{:S(2)}) copy-start(bf16[1,128,2048]{2,1,0:T(8,128)(2,1)} %param.9) | copy-start | bytes 1572868
  65.4 27.0 %copy-start.1 = (bf16[1,128,2048]{2,1,0:T(8,128)(2,1)S(1)}, bf16[1,128,2048]{2,1,0:T(8,128)(2,1)}, u32[]{:S(2)}) copy-start(bf16[1,128,2048]{2,1,0:T(8,128)(2,1)} %param.13) | copy-start | bytes 1572868
  65.4 27.0 %copy-start.6 = (s32[1,4096]{1,0:T(1,128)S(1)}, s32[1,4096]{1,0:T(1,128)}, u32[]{:S(2)}) copy-start(s32[1,4096]{1,0:T(1,128)} %doc_ref.3) | copy-start | bytes 49156
  65.4 27.0 %copy-start.7 = (f32[1,16,128]{2,1,0:T(8,128)S(1)}, f32[1,16,128]{2,1,0:T(8,128)}, u32[]{:S(2)}) copy-start(f32[1,16,128]{2,1,0:T(8,128)} %param.14) | copy-start | bytes 24580
  65.4 63.8 %all-to-all-start = ((bf16[8,128,1024]{2,1,0:T(8,128)(2,1)}), bf16[8,128,1024]{2,1,0:T(8,128)(2,1)S(1)}, u32[]{:S(2)}, u32[]{:S(2)}) async-start(bf16[8,128,1024]{2,1,0:T(8,128)(2,1)} %shard_map.117), calls=%async_computation | async-start | bytes 4194304 | tf_op jit(solution)/shard_map/all_to_all | solution.py:270
  74.5 6.7 %collective-permute-start.1 = (bf16[128,256]{1,0:T(8,128)(2,1)}, bf16[128,256]{1,0:T(8,128)(2,1)S(1)}, u32[]{:S(2)}, u32[]{:S(2)}) collective-permute-start(bf16[128,256]{1,0:T(8,128)(2,1)} %shard_map.111.own_ref), channel_id=1, source_target_pairs={{8,0},{16,8},{24,16},{32,24},{40,32},{48,40},{56,48},{64,56},{72,6... | collective-permute-start | bytes 196616 | tf_op jit(solution)/shard_map/ppermute | solution.py:243
  76.4 6.5 %collective-permute-start = (bf16[128,256]{1,0:T(8,128)(2,1)}, bf16[128,256]{1,0:T(8,128)(2,1)S(1)}, u32[]{:S(2)}, u32[]{:S(2)}) collective-permute-start(bf16[128,256]{1,0:T(8,128)(2,1)} %shard_map.111.own_ref), channel_id=1, source_target_pairs={{0,8},{8,16},{16,24},{24,32},{32,40},{40,48},{48,56},{56,64},{64,7... | collective-permute-start | bytes 196616 | tf_op jit(solution)/shard_map/ppermute | solution.py:243
  82.9 0.8 copy-start.4
  83.8 12.8 %collective-permute-start.2 = (bf16[128,256]{1,0:T(8,128)(2,1)S(1)}, bf16[128,256]{1,0:T(8,128)(2,1)S(1)}, u32[]{:S(2)}, u32[]{:S(2)}) collective-permute-start(bf16[128,256]{1,0:T(8,128)(2,1)S(1)} %get-tuple-element.18.low_ref), channel_id=1, source_target_pairs={{0,16},{8,24},{16,32},{24,40},{32,48},{40,56},{48,64},{56,72},{64,... | collective-permute-start | bytes 196616 | tf_op jit(solution)/shard_map/ppermute | solution.py:243
  91.1 9.0 %collective-permute-start.3 = (bf16[128,256]{1,0:T(8,128)(2,1)S(1)}, bf16[128,256]{1,0:T(8,128)(2,1)S(1)}, u32[]{:S(2)}, u32[]{:S(2)}) collective-permute-start(bf16[128,256]{1,0:T(8,128)(2,1)S(1)} %get-tuple-element.19.high_ref), channel_id=1, source_target_pairs={{16,0},{24,8},{32,16},{40,24},{48,32},{56,40},{64,48},{72,56},{80,... | collective-permute-start | bytes 196616 | tf_op jit(solution)/shard_map/ppermute | solution.py:243
  92.4 1.0 copy-start.2
  100.1 1.0 copy-start.3
  101.1 0.8 copy-start.5
  105.8 8.9 %collective-permute-start.4 = (bf16[128,256]{1,0:T(8,128)(2,1)S(1)}, bf16[128,256]{1,0:T(8,128)(2,1)S(1)}, u32[]{:S(2)}, u32[]{:S(2)}) collective-permute-start(bf16[128,256]{1,0:T(8,128)(2,1)S(1)} %get-tuple-element.24), channel_id=1, source_target_pairs={{16,0},{24,8},{32,16},{40,24},{48,32},{56,40},{64,48},{72,56},{80,... | collective-permute-start | bytes 196616 | tf_op jit(solution)/shard_map/ppermute | solution.py:243
  107.1 9.2 %collective-permute-start.5 = (bf16[128,256]{1,0:T(8,128)(2,1)S(1)}, bf16[128,256]{1,0:T(8,128)(2,1)S(1)}, u32[]{:S(2)}, u32[]{:S(2)}) collective-permute-start(bf16[128,256]{1,0:T(8,128)(2,1)S(1)} %get-tuple-element.23.high_ref), channel_id=1, source_target_pairs={{0,16},{8,24},{16,32},{24,40},{32,48},{40,56},{48,64},{56,72},{64,... | collective-permute-start | bytes 196616 | tf_op jit(solution)/shard_map/ppermute | solution.py:243
  116.3 12.3 %collective-permute-start.7 = (bf16[128,256]{1,0:T(8,128)(2,1)S(1)}, bf16[128,256]{1,0:T(8,128)(2,1)S(1)}, u32[]{:S(2)}, u32[]{:S(2)}) collective-permute-start(bf16[128,256]{1,0:T(8,128)(2,1)S(1)} %get-tuple-element.25.right_ref), channel_id=1, source_target_pairs={{0,8},{8,16},{16,24},{24,32},{32,40},{40,48},{48,56},{56,64},{64,7... | collective-permute-start | bytes 196616 | tf_op jit(solution)/shard_map/ppermute | solution.py:243
  122.7 5.8 %collective-permute-start.6 = (bf16[64,256]{1,0:T(8,128)(2,1)S(1)}, bf16[64,256]{1,0:T(8,128)(2,1)S(1)}, u32[]{:S(2)}, u32[]{:S(2)}) collective-permute-start(bf16[64,256]{1,0:T(8,128)(2,1)S(1)} %get-tuple-element.26), channel_id=1, source_target_pairs={{8,0},{16,8},{24,16},{32,24},{40,32},{48,40},{56,48},{64,56},{72,6... | collective-permute-start | bytes 98312 | tf_op jit(solution)/shard_map/ppermute | solution.py:243

commit v2 on v1

--- a/solution.py
+++ b/solution.py
@@ -59,11 +59,9 @@
     return (key_doc == query_doc) & (key_pos <= query_pos) & (key_pos >= 0)
 
 
-def attend(q_ref, g_ref, o_ref, lse_ref, keys, values, live, kv_acc, write_query):
+def attend(q_ref, g_ref, keys, values, live, kv_acc, lse_rows, delta_rows, write_query):
     heads = q_ref.shape[1] // HD
     group = min(4, heads)
-    row = lax.broadcasted_iota(jnp.int32, (C, 128), 0)
-    lane = lax.broadcasted_iota(jnp.int32, (C, 128), 1)
 
     def step(at, carry):
         lanes = pl.ds(pl.multiple_of(at * group * HD, group * HD), group * HD)
@@ -74,19 +72,8 @@
                 wide = ref[rows, lanes]
                 return jnp.concatenate([wide[:, i * HD : (i + 1) * HD] for i in range(group)], axis=0)
 
-            q, g, o = stacked(q_ref), stacked(g_ref), stacked(o_ref)
-            delta = jnp.sum(g.astype(F32) * o.astype(F32), axis=1, keepdims=True)
-            lse = jnp.concatenate(
-                [
-                    jnp.sum(
-                        jnp.where(lane == row + half * C, lse_ref[pl.ds(at * group + i, 1), :], 0.0),
-                        axis=1,
-                        keepdims=True,
-                    )
-                    for i in range(group)
-                ],
-                axis=0,
-            )
+            q, g = stacked(q_ref), stacked(g_ref)
+            lse, delta = lse_rows[half, at], delta_rows[half, at]
             k, v = keys[half], values[half]
             dims = (((1,), (1,)), ((), ()))
             s = lax.dot_general(q, k, dims, preferred_element_type=F32)
@@ -117,27 +104,50 @@
     out_ref[:, HD:] = v_ref[0]
 
 
-def widen_kernel(count, idx_ref, own_ref, left_ref, right_ref, low_ref, high_ref):
+def widen_kernel(count, idx_ref, k_ref, v_ref, left_ref, right_ref, low_ref, high_ref):
     last = idx_ref[0] == count - 1
     low_ref[:C] = left_ref[:C]
-    low_ref[C:] = own_ref[:C]
-    high_ref[:C] = pick(last, own_ref[:C], right_ref[C:]).astype(BF)
-    high_ref[C:] = own_ref[C:]
-
-
-def near_kernel(
-    count, idx_ref, q_ref, g_ref, o_ref, lse_ref, doc_ref, low_ref, high_ref, dq_ref, kv_ref, live_ref
-):
+    for own_ref, lanes in ((k_ref, slice(0, HD)), (v_ref, slice(HD, 2 * HD))):
+        low_ref[C:, lanes] = own_ref[0, :C]
+        high_ref[:C, lanes] = pick(last, own_ref[0, :C], right_ref[C:, lanes]).astype(BF)
+        high_ref[C:, lanes] = own_ref[0, C:]
+
+
+def prepare_kernel(count, idx_ref, g_ref, o_ref, lse_ref, doc_ref, lse_rows, delta_rows, live_ref):
     place = idx_ref[0]
     for half, block in enumerate((place, 2 * count - 1 - place)):
-        live_ref[half] = live_pair(doc_ref, block, block).astype(F32)
+        live_ref[0, half] = live_pair(doc_ref, block, block).astype(F32)
+        live_ref[1, half] = live_pair(doc_ref, block, block - 2).astype(F32)
+    row = lax.broadcasted_iota(jnp.int32, (C, 128), 0)
+    lane = lax.broadcasted_iota(jnp.int32, (C, 128), 1)
+    group = lse_rows.shape[2] // C
+
+    def step(at, carry):
+        for half in range(2):
+            rows = slice(half * C, half * C + C)
+            for i in range(group):
+                head = at * group + i
+                lanes = pl.ds(pl.multiple_of(head * HD, HD), HD)
+                g, o = g_ref[rows, lanes].astype(F32), o_ref[rows, lanes].astype(F32)
+                delta = jnp.sum(g * o, axis=1, keepdims=True)
+                mine = jnp.where(lane == row + half * C, lse_ref[pl.ds(head, 1), :], 0.0)
+                lse = jnp.sum(mine, axis=1, keepdims=True)
+                into = slice(i * C, i * C + C)
+                delta_rows[half, at, into] = jnp.broadcast_to(delta, (C, 128))
+                lse_rows[half, at, into] = jnp.broadcast_to(lse, (C, 128))
+        return carry
+
+    lax.fori_loop(0, lse_rows.shape[1], step, 0)
+
+
+def near_kernel(idx_ref, q_ref, g_ref, low_ref, high_ref, lse_rows, delta_rows, live_ref, dq_ref, kv_ref):
     keys = (low_ref[:, :HD], high_ref[:, :HD])
     values = (low_ref[:, HD:], high_ref[:, HD:])
 
     def write(rows, lanes, value):
         dq_ref[rows, lanes] = value
 
-    attend(q_ref, g_ref, o_ref, lse_ref, keys, values, live_ref, kv_ref, write)
+    attend(q_ref, g_ref, keys, values, live_ref[0], kv_ref, lse_rows, delta_rows, write)
 
 
 def far_kernel(
@@ -145,27 +155,23 @@
     idx_ref,
     q_ref,
     g_ref,
-    o_ref,
-    lse_ref,
-    doc_ref,
-    own_ref,
-    left_ref,
+    near_low_ref,
     right_ref,
     left2_ref,
     right2_ref,
     near_ref,
+    lse_rows,
+    delta_rows,
+    live_ref,
     dq_ref,
     low_ref,
     high_ref,
-    live_ref,
     acc_ref,
 ):
     place = idx_ref[0]
     last, before = place == count - 1, place == count - 2
-    for half, block in enumerate((place, 2 * count - 1 - place)):
-        live_ref[half] = live_pair(doc_ref, block, block - 2).astype(F32)
-    third = pick(before, own_ref[:C], pick(last, left2_ref[C:], right2_ref[:C])).astype(BF)
-    second = pick(before, right_ref[:C], pick(last, left_ref[:C], right2_ref[C:])).astype(BF)
+    third = pick(before, near_low_ref[C:], pick(last, left2_ref[C:], right2_ref[:C])).astype(BF)
+    second = pick(before, right_ref[:C], pick(last, near_low_ref[:C], right2_ref[C:])).astype(BF)
     upper = jnp.concatenate([third, second], axis=0)
     keys = (left2_ref[:, :HD], upper[:, :HD])
     values = (left2_ref[:, HD:], upper[:, HD:])
@@ -173,7 +179,7 @@
     def write(rows, lanes, value):
         dq_ref[0, rows, lanes] = (value + near_ref[rows, lanes]).astype(BF)
 
-    attend(q_ref, g_ref, o_ref, lse_ref, keys, values, live_ref, acc_ref, write)
+    attend(q_ref, g_ref, keys, values, live_ref[1], acc_ref, lse_rows, delta_rows, write)
     low_ref[:C] = acc_ref[0, :C].astype(BF)
     low_ref[C:] = (acc_ref[0, C:] + jnp.where(last, acc_ref[1, :C], 0.0)).astype(BF)
     high_ref[...] = acc_ref[1].astype(BF)
@@ -214,24 +220,32 @@
         spread_ref[i] = both[:, HD:]
 
 
-def chunk_kernel(x_ref, out_ref, sems):
+def chunk_kernel(tp_ref, x_ref, out_ref, sems):
     parts, _, width = out_ref.shape
-    copies = [
-        pltpu.make_async_copy(x_ref.at[0, :, pl.ds(i * width, width)], out_ref.at[i], sems.at[i])
-        for i in range(parts)
-    ]
+    stride = x_ref.shape[2] // parts
+    copies = []
+    for i in range(parts):
+        lanes = pl.ds(pl.multiple_of(i * stride + tp_ref[0] * width, 128), width)
+        copies.append(pltpu.make_async_copy(x_ref.at[0, :, lanes], out_ref.at[i], sems.at[i]))
     for copy in copies:
         copy.start()
     for copy in copies:
         copy.wait()
 
 
+def repeat_kernel(x_ref, out_ref):
+    for i in range(out_ref.shape[0]):
+        out_ref[i] = x_ref[...]
+
+
 def weight_kernel(scale, x_ref, dv_ref, out_ref):
-    parts, tokens, width = x_ref.shape
-    x = x_ref[...].reshape(parts * tokens, width)
-    dv = dv_ref[...].reshape(parts * tokens, HD)
-    flat = lax.dot_general(dv, x, (((0,), (0,)), ((), ())), preferred_element_type=F32) * scale
-    out_ref[...] = flat.T.astype(BF).reshape(out_ref.shape)
+    pieces, parts, tokens, width = x_ref.shape
+    each = out_ref.shape[0] // pieces
+    dv = dv_ref[...].reshape(parts * tokens, HD).T
+    for i in range(pieces):
+        x = x_ref[i].reshape(parts * tokens, width)
+        flat = jnp.dot(dv, x, preferred_element_type=F32) * scale
+        out_ref[i * each : (i + 1) * each] = flat.T.astype(BF).reshape(each, width // each, HD)
 
 
 def shift(value, by):
@@ -260,32 +274,44 @@
     )(key_heads, value_heads)
     left = shift(kv, 1)
     right = shift(kv, -1)
+    group = min(4, heads)
+    row_terms = shape((2, heads // group, group * C, 128), F32)
+    lse_rows, delta_rows, live = call(
+        at(prepare_kernel, count), [row_terms, row_terms, shape((2, 2, C, 128), F32)], 5, attend_flops
+    )(place, g, o, lse, doc_ids)
+    left, lse_rows = lax.optimization_barrier((left, lse_rows))
+    pieces = lax.axis_size("tp")
+    piece = layer_input.shape[2] // (groups * pieces)
     chunks = pl.pallas_call(
         chunk_kernel,
-        out_shape=shape((groups, rows, layer_input.shape[2] // groups), BF),
-        in_specs=[pl.BlockSpec(memory_space=pl.ANY)],
-        out_specs=pl.BlockSpec(memory_space=pl.ANY),
+        out_shape=shape((groups, rows, piece), BF),
+        in_specs=[SMEM, pl.BlockSpec(memory_space=pl.ANY)],
+        out_specs=VMEM,
         scratch_shapes=[pltpu.SemaphoreType.DMA((groups,))],
-    )(layer_input)
-    tokens = lax.all_to_all(chunks, ROWS, 0, 0, tiled=True)
+    )(lax.axis_index("tp").astype(jnp.int32).reshape(1), layer_input)
+    mine = lax.all_to_all(chunks, ROWS, 0, 0, tiled=True)
     pair = shape((rows, 2 * HD), BF)
-    low, high = call(at(widen_kernel, count), [pair, pair], 4, 0)(place, kv, left, right)
+    low, high = call(at(widen_kernel, count), [pair, pair], 5, 0)(place, key_heads, value_heads, left, right)
     left2 = shift(low, 2)
     right2 = shift(high, -2)
+    low, high, mine = lax.optimization_barrier((low, high, mine))
+    repeated = pl.pallas_call(
+        repeat_kernel, out_shape=shape((pieces, groups, rows, piece), BF), in_specs=[VMEM], out_specs=VMEM
+    )(mine)
+    tokens = lax.all_to_all(repeated, "tp", 0, 0, tiled=True)
     near_query, near_kv = call(
-        at(near_kernel, count),
+        near_kernel,
         [shape((rows, width), F32), shape((2, 128, 2 * HD), F32)],
         8,
         attend_flops,
-        [pltpu.VMEM((2, C, 128), F32)],
-    )(place, q, g, o, lse, doc_ids, low, high)
+    )(place, q, g, low, high, lse_rows, delta_rows, live)
     query_grad, far_low, far_high = call(
         at(far_kernel, count),
         [shape((1, rows, width), BF), pair, pair],
-        12,
+        11,
         attend_flops,
-        [pltpu.VMEM((2, C, 128), F32), pltpu.VMEM((2, 128, 2 * HD), F32)],
-    )(place, q, g, o, lse, doc_ids, kv, left, right, left2, right2, near_query)
+        [pltpu.VMEM((2, 128, 2 * HD), F32)],
+    )(place, q, g, low, right, left2, right2, near_query, lse_rows, delta_rows, live)
     low2 = shift(far_low, -2)
     high2 = shift(far_high, 2)
     to_left, to_right = call(at(turn_kernel, count), [shape((C, 2 * HD), BF), pair], 5, 0)(
@@ -304,7 +330,7 @@
     weight_scale = (lax.axis_size("dp") * doc_ids.shape[1]) ** (-0.5)
     part = pl.pallas_call(
         at(weight_kernel, weight_scale),
-        out_shape=shape((steps, tokens.shape[2] // steps, HD), BF),
+        out_shape=shape((steps, piece * pieces // steps, HD), BF),
         in_specs=[VMEM] * 2,
         out_specs=VMEM,
         compiler_params=pltpu.CompilerParams(vmem_limit_bytes=40 * 1024 * 1024),

time: 205 us -> 141 us (0.69)
  the two profiles are of different devices: /device:TPU:78 before, /device:TPU:8 now
where the time goes in v2:
time: 141 us; the launch traced here: 140 us
  blocking collectives  65.8 us (47%)
  starting transfers between devices  43.1 us (31%)
  Pallas kernels  14.6 us (10%)
  waiting for transfers between devices  10.5 us (7%)
  local copies, waits for them, and re-layouts  5.01 us (4%)
    all_to_all x1, blocking collectives, body(): everyone = lax.all_to_all(spread, ROWS, 0, 0, tiled=True)  42.6 us
    all_to_all x1, blocking collectives, body(): parts = lax.all_to_all(part, 'ctx_1', 0, 0, tiled=True)  23.1 us
    ppermute x8, starting transfers between devices, shift(): return lax.ppermute(value, CTX, pairs)  23 us
    all_to_all x1, starting transfers between devices, body(): mine = lax.all_to_all(chunks, ROWS, 0, 0, tiled=True)  16.4 us
    ppermute x8, waiting for transfers between devices, shift(): return lax.ppermute(value, CTX, pairs)  10.5 us
    unnamed x22, local copies, waits for them, and re-layouts  5.01 us
    all_to_all x1, starting transfers between devices, body(): tokens = lax.all_to_all(repeated, 'tp', 0, 0, tiled=True)  3.6 us
    pallas_call x1, Pallas kernels, body(): call(at(far_kernel, count), [shape((1, rows, width), BF), pair, pair], 11...  3.48 us
  transfers between devices with their start and end apart: 10, of which 5 were waited for; matrix products, arithmetic and copies ran while one was open for 0% of the time, Pallas kernels for 7%

profile of v2, /device:TPU:8, one launch (start us, length us, event | category | flops | bytes accessed | tf_op | source)
XLA Modules:
  0.0 140.4 jit_solution(2982042737143684501)
XLA Ops:
  0.7 1.7 %shard_map.114 = bf16[8,128,128]{2,1,0:T(8,128)(2,1)} custom-call(s32[1]{0:T(128)} %bitcast.5.tp_ref, bf16[1,128,8192]{2,1,0:T(8,128)(2,1)} %x_ref.1), custom_call_target="tpu_custom_call" | custom-call | tf_op jit(solution)/shard_map/pallas_call | solution.py:285
  2.4 16.4 %all-to-all-start = ((bf16[8,128,128]{2,1,0:T(8,128)(2,1)}), bf16[8,128,128]{2,1,0:T(8,128)(2,1)S(1)}, u32[]{:S(2)}, u32[]{:S(2)}) async-start(bf16[8,128,128]{2,1,0:T(8,128)(2,1)} %shard_map.114), calls=%async_computation | async-start | bytes 524288 | tf_op jit(solution)/shard_map/all_to_all | solution.py:292
  18.9 1.4 %shard_map.111 = bf16[128,256]{1,0:T(8,128)(2,1)} custom-call(bf16[1,128,128]{2,1,0:T(8,128)(2,1)} %k_ref.3, bf16[1,128,128]{2,1,0:T(8,128)(2,1)} %v_ref.3), custom_call_target="tpu_custom_call" | custom-call | tf_op jit(solution)/shard_map/pallas_call | solution.py:272
  20.3 1.3 collective-permute-start
  21.6 1.3 collective-permute-start.1
  22.9 1.1 shard_map.112
  25.1 2.9 %collective-permute-done.1.right_ref = bf16[128,256]{1,0:T(8,128)(2,1)S(1)} collective-permute-done((bf16[128,256]{1,0:T(8,128)(2,1)}, bf16[128,256]{1,0:T(8,128)(2,1)S(1)}, u32[]{:S(2)}, u32[]{:S(2)}) %collective-permute-start.1) | collective-permute-done | bytes 65568 | tf_op jit(solution)/shard_map/ppermute | solution.py:257
  28.7 2.5 %shard_map.119 = bf16[8,8,128,128]{3,2,1,0:T(8,128)(2,1)} custom-call(bf16[8,128,128]{2,1,0:T(8,128)(2,1)} %copy-done.10), custom_call_target="tpu_custom_call" | custom-call | tf_op jit(solution)/shard_map/pallas_call | solution.py:298
  31.2 3.6 %all-to-all-start.1 = ((bf16[8,8,128,128]{3,2,1,0:T(8,128)(2,1)}), bf16[8,8,128,128]{3,2,1,0:T(8,128)(2,1)S(1)}, u32[]{:S(2)}, u32[]{:S(2)}) async-start(bf16[8,8,128,128]{3,2,1,0:T(8,128)(2,1)} %shard_map.119), calls=%async_computation.1 | async-start | bytes 4194304 | tf_op jit(solution)/shard_map/all_to_all | solution.py:301
  34.9 2.4 %collective-permute-start.2 = (bf16[128,256]{1,0:T(8,128)(2,1)S(1)}, bf16[128,256]{1,0:T(8,128)(2,1)S(1)}, u32[]{:S(2)}, u32[]{:S(2)}) collective-permute-start(bf16[128,256]{1,0:T(8,128)(2,1)S(1)} %get-tuple-element.30.low_ref.near_low_ref), channel_id=1, source_target_pairs={{0,16},{8,24},{16,32},{24,40},{32,48},{40,56},{48,64},{56,72},{64,... | collective-permute-start | bytes 196616 | tf_op jit(solution)/shard_map/ppermute | solution.py:257
  37.3 1.3 collective-permute-start.3
  38.6 1.2 copy-done.1
  39.8 1.0 copy-done.2
  41.9 2.8 %shard_map.115 = (f32[128,2048]{1,0:T(8,128)S(1)}, f32[2,128,256]{2,1,0:T(8,128)S(1)}) custom-call(s32[1]{0:T(128)} %bitcast.idx_ref, bf16[128,2048]{1,0:T(8,128)(2,1)S(1)} %bitcast.6, bf16[128,2048]{1,0:T(8,128)(2,1)S(1)} %bitcast.9, bf16[128,256]{1,0:T(8,128)(2,1)S(1)} %get-tuple-element.30.low_ref.near_low_ref, ...), custom_call_target="tpu_custom_call" | custom-call | flops 335544320 | bytes 1048576 | tf_op jit(solution)/shard_map/pallas_call | solution.py:302
  44.7 1.2 collective-permute-done.3.right2_ref
  45.9 3.5 %shard_map.116 = (bf16[1,128,2048]{2,1,0:T(8,128)(2,1)}, bf16[128,256]{1,0:T(8,128)(2,1)S(1)}, bf16[128,256]{1,0:T(8,128)(2,1)S(1)}) custom-call(s32[1]{0:T(128)} %bitcast.idx_ref, bf16[128,2048]{1,0:T(8,128)(2,1)S(1)} %bitcast.7, bf16[128,2048]{1,0:T(8,128)(2,1)S(1)} %bitcast.10, bf16[128,256]{1,0:T(8,128)(2,1)S(1)} %get-tuple-element.30.low_ref.near_low_ref, ...), custom_call_target="tpu_custom_call" | custom-call | flops 335544320 | bytes 1048576 | tf_op jit(solution)/shard_map/pallas_call | solution.py:308
  49.3 1.3 collective-permute-start.4
  50.6 7.9 %collective-permute-start.5 = (bf16[128,256]{1,0:T(8,128)(2,1)S(1)}, bf16[128,256]{1,0:T(8,128)(2,1)S(1)}, u32[]{:S(2)}, u32[]{:S(2)}) collective-permute-start(bf16[128,256]{1,0:T(8,128)(2,1)S(1)} %get-tuple-element.38.high_ref), channel_id=1, source_target_pairs={{0,16},{8,24},{16,32},{24,40},{32,48},{40,56},{48,64},{56,72},{64,... | collective-permute-start | bytes 196616 | tf_op jit(solution)/shard_map/ppermute | solution.py:257
  58.9 1.6 %collective-permute-done.5.high2_ref = bf16[128,256]{1,0:T(8,128)(2,1)S(1)} collective-permute-done((bf16[128,256]{1,0:T(8,128)(2,1)S(1)}, bf16[128,256]{1,0:T(8,128)(2,1)S(1)}, u32[]{:S(2)}, u32[]{:S(2)}) %collective-permute-start.5) | collective-permute-done | bytes 65568 | tf_op jit(solution)/shard_map/ppermute | solution.py:257
  60.5 6.2 %collective-permute-start.7 = (bf16[128,256]{1,0:T(8,128)(2,1)S(1)}, bf16[128,256]{1,0:T(8,128)(2,1)S(1)}, u32[]{:S(2)}, u32[]{:S(2)}) collective-permute-start(bf16[128,256]{1,0:T(8,128)(2,1)S(1)} %get-tuple-element.40.right_ref), channel_id=1, source_target_pairs={{0,8},{8,16},{16,24},{24,32},{32,40},{40,48},{48,56},{56,64},{64,7... | collective-permute-start | bytes 196616 | tf_op jit(solution)/shard_map/ppermute | solution.py:257
  66.7 1.3 collective-permute-start.6
  68.0 4.5 %collective-permute-done.6.low1_ref = bf16[64,256]{1,0:T(8,128)(2,1)S(1)} collective-permute-done((bf16[64,256]{1,0:T(8,128)(2,1)S(1)}, bf16[64,256]{1,0:T(8,128)(2,1)S(1)}, u32[]{:S(2)}, u32[]{:S(2)}) %collective-permute-start.6) | collective-permute-done | bytes 32800 | tf_op jit(solution)/shard_map/ppermute | solution.py:257
  73.2 42.6 %all_to_all.20.dv_ref = bf16[8,128,128]{2,1,0:T(8,128)(2,1)S(1)} all-to-all(bf16[8,128,128]{2,1,0:T(8,128)(2,1)S(1)} %get-tuple-element.47), channel_id=1, replica_groups=mesh['dp'=4,'ctx_0'=2,'ctx_1'=16,'tp'=8] {'dp','ctx_0'}, dimensions={0} | all-to-all | bytes 524288 | tf_op jit(solution)/shard_map/all_to_all | solution.py:329
  116.7 23.1 %all_to_all.21 = bf16[16,64,128]{2,1,0:T(8,128)(2,1)S(1)} all-to-all(bf16[16,64,128]{2,1,0:T(8,128)(2,1)S(1)} %shard_map.120), channel_id=1, replica_groups=mesh['dp'=4,'ctx_0'=2,'ctx_1'=16,'tp'=8] {'ctx_1'}, dimensions={0} | all-to-all | bytes 524288 | tf_op jit(solution)/shard_map/all_to_all | solution.py:338
  (31 shorter events, 5.3 us)
Async XLA Ops:
  0.6 22.3 %copy-start.8 = (s32[1,4096]{1,0:T(1,128)S(1)}, s32[1,4096]{1,0:T(1,128)}, u32[]{:S(2)}) copy-start(s32[1,4096]{1,0:T(1,128)} %doc_ref.1) | copy-start | bytes 49156
  0.6 22.3 %copy-start.9 = (f32[1,16,128]{2,1,0:T(8,128)S(1)}, f32[1,16,128]{2,1,0:T(8,128)}, u32[]{:S(2)}) copy-start(f32[1,16,128]{2,1,0:T(8,128)} %param.14) | copy-start | bytes 24580
  0.7 22.3 %copy-start.3 = (bf16[1,128,2048]{2,1,0:T(8,128)(2,1)S(1)}, bf16[1,128,2048]{2,1,0:T(8,128)(2,1)}, u32[]{:S(2)}) copy-start(bf16[1,128,2048]{2,1,0:T(8,128)(2,1)} %param.13) | copy-start | bytes 1572868
  0.7 22.2 %copy-start.7 = (bf16[1,128,2048]{2,1,0:T(8,128)(2,1)S(1)}, bf16[1,128,2048]{2,1,0:T(8,128)(2,1)}, u32[]{:S(2)}) copy-start(bf16[1,128,2048]{2,1,0:T(8,128)(2,1)} %param.12) | copy-start | bytes 1572868
  0.7 27.3 %copy-start.5 = (bf16[1,128,128]{2,1,0:T(8,128)(2,1)S(1)}, bf16[1,128,128]{2,1,0:T(8,128)(2,1)}, u32[]{:S(2)}) copy-start(bf16[1,128,128]{2,1,0:T(8,128)(2,1)} %k_ref.3) | copy-start | bytes 98308
  0.7 27.3 %copy-start.6 = (bf16[1,128,128]{2,1,0:T(8,128)(2,1)S(1)}, bf16[1,128,128]{2,1,0:T(8,128)(2,1)}, u32[]{:S(2)}) copy-start(bf16[1,128,128]{2,1,0:T(8,128)(2,1)} %v_ref.3) | copy-start | bytes 98308
  2.4 25.5 %all-to-all-start = ((bf16[8,128,128]{2,1,0:T(8,128)(2,1)}), bf16[8,128,128]{2,1,0:T(8,128)(2,1)S(1)}, u32[]{:S(2)}, u32[]{:S(2)}) async-start(bf16[8,128,128]{2,1,0:T(8,128)(2,1)} %shard_map.114), calls=%async_computation | async-start | bytes 524288 | tf_op jit(solution)/shard_map/all_to_all | solution.py:292
  20.3 4.8 %collective-permute-start = (bf16[128,256]{1,0:T(8,128)(2,1)}, bf16[128,256]{1,0:T(8,128)(2,1)S(1)}, u32[]{:S(2)}, u32[]{:S(2)}) collective-permute-start(bf16[128,256]{1,0:T(8,128)(2,1)} %shard_map.111), channel_id=1, source_target_pairs={{0,8},{8,16},{16,24},{24,32},{32,40},{40,48},{48,56},{56,64},{64,7... | collective-permute-start | bytes 196616 | tf_op jit(solution)/shard_map/ppermute | solution.py:257
  21.6 6.4 %collective-permute-start.1 = (bf16[128,256]{1,0:T(8,128)(2,1)}, bf16[128,256]{1,0:T(8,128)(2,1)S(1)}, u32[]{:S(2)}, u32[]{:S(2)}) collective-permute-start(bf16[128,256]{1,0:T(8,128)(2,1)} %shard_map.111), channel_id=1, source_target_pairs={{8,0},{16,8},{24,16},{32,24},{40,32},{48,40},{56,48},{64,56},{72,6... | collective-permute-start | bytes 196616 | tf_op jit(solution)/shard_map/ppermute | solution.py:257
  24.1 1.0 copy-start
  28.0 0.7 copy-start.10
  31.2 42.0 %all-to-all-start.1 = ((bf16[8,8,128,128]{3,2,1,0:T(8,128)(2,1)}), bf16[8,8,128,128]{3,2,1,0:T(8,128)(2,1)S(1)}, u32[]{:S(2)}, u32[]{:S(2)}) async-start(bf16[8,8,128,128]{3,2,1,0:T(8,128)(2,1)} %shard_map.119), calls=%async_computation.1 | async-start | bytes 4194304 | tf_op jit(solution)/shard_map/all_to_all | solution.py:301
  34.9 9.8 %collective-permute-start.2 = (bf16[128,256]{1,0:T(8,128)(2,1)S(1)}, bf16[128,256]{1,0:T(8,128)(2,1)S(1)}, u32[]{:S(2)}, u32[]{:S(2)}) collective-permute-start(bf16[128,256]{1,0:T(8,128)(2,1)S(1)} %get-tuple-element.30.low_ref.near_low_ref), channel_id=1, source_target_pairs={{0,16},{8,24},{16,32},{24,40},{32,48},{40,56},{48,64},{56,72},{64,... | collective-permute-start | bytes 196616 | tf_op jit(solution)/shard_map/ppermute | solution.py:257
  37.3 8.6 %collective-permute-start.3 = (bf16[128,256]{1,0:T(8,128)(2,1)S(1)}, bf16[128,256]{1,0:T(8,128)(2,1)S(1)}, u32[]{:S(2)}, u32[]{:S(2)}) collective-permute-start(bf16[128,256]{1,0:T(8,128)(2,1)S(1)} %get-tuple-element.31.high_ref), channel_id=1, source_target_pairs={{16,0},{24,8},{32,16},{40,24},{48,32},{56,40},{64,48},{72,56},{80,... | collective-permute-start | bytes 196616 | tf_op jit(solution)/shard_map/ppermute | solution.py:257
  38.6 1.2 copy-start.1
  39.8 1.0 copy-start.2
  40.9 1.0 copy-start.4
  49.3 9.5 %collective-permute-start.4 = (bf16[128,256]{1,0:T(8,128)(2,1)S(1)}, bf16[128,256]{1,0:T(8,128)(2,1)S(1)}, u32[]{:S(2)}, u32[]{:S(2)}) collective-permute-start(bf16[128,256]{1,0:T(8,128)(2,1)S(1)} %get-tuple-element.39), channel_id=1, source_target_pairs={{16,0},{24,8},{32,16},{40,24},{48,32},{56,40},{64,48},{72,56},{80,... | collective-permute-start | bytes 196616 | tf_op jit(solution)/shard_map/ppermute | solution.py:257
  50.6 9.8 %collective-permute-start.5 = (bf16[128,256]{1,0:T(8,128)(2,1)S(1)}, bf16[128,256]{1,0:T(8,128)(2,1)S(1)}, u32[]{:S(2)}, u32[]{:S(2)}) collective-permute-start(bf16[128,256]{1,0:T(8,128)(2,1)S(1)} %get-tuple-element.38.high_ref), channel_id=1, source_target_pairs={{0,16},{8,24},{16,32},{24,40},{32,48},{40,56},{48,64},{56,72},{64,... | collective-permute-start | bytes 196616 | tf_op jit(solution)/shard_map/ppermute | solution.py:257
  60.5 12.1 %collective-permute-start.7 = (bf16[128,256]{1,0:T(8,128)(2,1)S(1)}, bf16[128,256]{1,0:T(8,128)(2,1)S(1)}, u32[]{:S(2)}, u32[]{:S(2)}) collective-permute-start(bf16[128,256]{1,0:T(8,128)(2,1)S(1)} %get-tuple-element.40.right_ref), channel_id=1, source_target_pairs={{0,8},{8,16},{16,24},{24,32},{32,40},{40,48},{48,56},{56,64},{64,7... | collective-permute-start | bytes 196616 | tf_op jit(solution)/shard_map/ppermute | solution.py:257
  66.7 5.8 %collective-permute-start.6 = (bf16[64,256]{1,0:T(8,128)(2,1)S(1)}, bf16[64,256]{1,0:T(8,128)(2,1)S(1)}, u32[]{:S(2)}, u32[]{:S(2)}) collective-permute-start(bf16[64,256]{1,0:T(8,128)(2,1)S(1)} %get-tuple-element.41), channel_id=1, source_target_pairs={{8,0},{16,8},{24,16},{32,24},{40,32},{48,40},{56,48},{64,56},{72,6... | collective-permute-start | bytes 98312 | tf_op jit(solution)/shard_map/ppermute | solution.py:257

commit v3 on v2

--- a/solution.py
+++ b/solution.py
@@ -18,17 +18,19 @@
 F32 = jnp.float32
 SMEM = pl.BlockSpec(memory_space=pltpu.SMEM)
 VMEM = pl.BlockSpec(memory_space=pltpu.VMEM)
-
-
-def call(kernel, outs, n_in, flops, scratch=()):
+COST = {"prepare": 1, "widen": 0.1, "near": 3, "far": 3, "turn": 10, "close": 10}
+
+
+def call(kernel, outs, in_specs, us, scratch=(), mib=8):
     return pl.pallas_call(
         kernel,
+        name=getattr(kernel, "func", kernel).__name__,
         out_shape=outs,
-        in_specs=[SMEM] + [VMEM] * (n_in - 1),
+        in_specs=in_specs,
         out_specs=[VMEM] * len(outs),
         scratch_shapes=list(scratch),
-        compiler_params=pltpu.CompilerParams(vmem_limit_bytes=40 * 1024 * 1024),
-        cost_estimate=pl.CostEstimate(flops=flops, bytes_accessed=1 << 20, transcendentals=0),
+        compiler_params=pltpu.CompilerParams(vmem_limit_bytes=mib * 1024 * 1024),
+        cost_estimate=pl.CostEstimate(flops=int(us * 1e9), bytes_accessed=0, transcendentals=0),
     )
 
 
@@ -59,20 +61,14 @@
     return (key_doc == query_doc) & (key_pos <= query_pos) & (key_pos >= 0)
 
 
-def attend(q_ref, g_ref, keys, values, live, kv_acc, lse_rows, delta_rows, write_query):
-    heads = q_ref.shape[1] // HD
-    group = min(4, heads)
+def attend(q_rows, g_rows, keys, values, live, kv_acc, lse_rows, delta_rows, write_query):
+    steps, group = q_rows.shape[1], q_rows.shape[2] // C
 
     def step(at, carry):
         lanes = pl.ds(pl.multiple_of(at * group * HD, group * HD), group * HD)
         for half in range(2):
             rows = slice(half * C, half * C + C)
-
-            def stacked(ref):
-                wide = ref[rows, lanes]
-                return jnp.concatenate([wide[:, i * HD : (i + 1) * HD] for i in range(group)], axis=0)
-
-            q, g = stacked(q_ref), stacked(g_ref)
+            q, g = q_rows[half, at], g_rows[half, at]
             lse, delta = lse_rows[half, at], delta_rows[half, at]
             k, v = keys[half], values[half]
             dims = (((1,), (1,)), ((), ()))
@@ -92,7 +88,7 @@
         return carry
 
     kv_acc[...] = jnp.zeros_like(kv_acc)
-    lax.fori_loop(0, heads // group, step, 0)
+    lax.fori_loop(0, steps, step, 0)
 
 
 def pick(where, a, b):
@@ -113,7 +109,9 @@
         high_ref[C:, lanes] = own_ref[0, C:]
 
 
-def prepare_kernel(count, idx_ref, g_ref, o_ref, lse_ref, doc_ref, lse_rows, delta_rows, live_ref):
+def prepare_kernel(
+    count, idx_ref, q_ref, g_ref, o_ref, lse_ref, doc_ref, q_rows, g_rows, lse_rows, delta_rows, live_ref
+):
     place = idx_ref[0]
     for half, block in enumerate((place, 2 * count - 1 - place)):
         live_ref[0, half] = live_pair(doc_ref, block, block).astype(F32)
@@ -128,11 +126,13 @@
             for i in range(group):
                 head = at * group + i
                 lanes = pl.ds(pl.multiple_of(head * HD, HD), HD)
-                g, o = g_ref[rows, lanes].astype(F32), o_ref[rows, lanes].astype(F32)
-                delta = jnp.sum(g * o, axis=1, keepdims=True)
+                g = g_ref[rows, lanes]
+                delta = jnp.sum(g.astype(F32) * o_ref[rows, lanes].astype(F32), axis=1, keepdims=True)
                 mine = jnp.where(lane == row + half * C, lse_ref[pl.ds(head, 1), :], 0.0)
                 lse = jnp.sum(mine, axis=1, keepdims=True)
                 into = slice(i * C, i * C + C)
+                q_rows[half, at, into] = q_ref[rows, lanes]
+                g_rows[half, at, into] = g
                 delta_rows[half, at, into] = jnp.broadcast_to(delta, (C, 128))
                 lse_rows[half, at, into] = jnp.broadcast_to(lse, (C, 128))
         return carry
@@ -140,21 +140,21 @@
     lax.fori_loop(0, lse_rows.shape[1], step, 0)
 
 
-def near_kernel(idx_ref, q_ref, g_ref, low_ref, high_ref, lse_rows, delta_rows, live_ref, dq_ref, kv_ref):
+def near_kernel(idx_ref, q_rows, g_rows, low_ref, high_ref, lse_rows, delta_rows, live_ref, dq_ref, kv_ref):
     keys = (low_ref[:, :HD], high_ref[:, :HD])
     values = (low_ref[:, HD:], high_ref[:, HD:])
 
     def write(rows, lanes, value):
         dq_ref[rows, lanes] = value
 
-    attend(q_ref, g_ref, keys, values, live_ref[0], kv_ref, lse_rows, delta_rows, write)
+    attend(q_rows, g_rows, keys, values, live_ref[0], kv_ref, lse_rows, delta_rows, write)
 
 
 def far_kernel(
     count,
     idx_ref,
-    q_ref,
-    g_ref,
+    q_rows,
+    g_rows,
     near_low_ref,
     right_ref,
     left2_ref,
@@ -179,7 +179,7 @@
     def write(rows, lanes, value):
         dq_ref[0, rows, lanes] = (value + near_ref[rows, lanes]).astype(BF)
 
-    attend(q_ref, g_ref, keys, values, live_ref[1], acc_ref, lse_rows, delta_rows, write)
+    attend(q_rows, g_rows, keys, values, live_ref[1], acc_ref, lse_rows, delta_rows, write)
     low_ref[:C] = acc_ref[0, :C].astype(BF)
     low_ref[C:] = (acc_ref[0, C:] + jnp.where(last, acc_ref[1, :C], 0.0)).astype(BF)
     high_ref[...] = acc_ref[1].astype(BF)
@@ -264,76 +264,80 @@
     rows = 2 * C
     groups = lax.axis_size(ROWS)
     steps = lax.axis_size("ctx_1")
+    pieces = lax.axis_size("tp")
+    piece = layer_input.shape[2] // (groups * pieces)
     heads = width // HD
-    attend_flops = 10 * rows * 128 * HD * heads
-    q, g, o, lse = queries[0], out_grad[0], attn_out[0], log_sums[0]
+    group = min(4, heads)
+    row_terms = shape((2, heads // group, group * C, 128), F32)
+    head_rows = shape(row_terms.shape, BF)
+    pair = shape((rows, 2 * HD), BF)
     at = functools.partial
 
-    kv = pl.pallas_call(
-        pack_kernel, out_shape=shape((rows, 2 * HD), BF), in_specs=[VMEM] * 2, out_specs=VMEM
-    )(key_heads, value_heads)
+    (kv,) = call(pack_kernel, [pair], [VMEM] * 2, 1, mib=56)(key_heads, value_heads)
     left = shift(kv, 1)
     right = shift(kv, -1)
-    group = min(4, heads)
-    row_terms = shape((2, heads // group, group * C, 128), F32)
-    lse_rows, delta_rows, live = call(
-        at(prepare_kernel, count), [row_terms, row_terms, shape((2, 2, C, 128), F32)], 5, attend_flops
-    )(place, g, o, lse, doc_ids)
-    left, lse_rows = lax.optimization_barrier((left, lse_rows))
-    pieces = lax.axis_size("tp")
-    piece = layer_input.shape[2] // (groups * pieces)
-    chunks = pl.pallas_call(
+    q_rows, g_rows, lse_rows, delta_rows, live = call(
+        at(prepare_kernel, count),
+        [head_rows, head_rows, row_terms, row_terms, shape((2, 2, C, 128), F32)],
+        [SMEM] + [VMEM] * 5,
+        COST["prepare"],
+        mib=12,
+    )(place, queries[0], out_grad[0], attn_out[0], log_sums[0], doc_ids)
+    left, live = lax.optimization_barrier((left, live))
+    (chunks,) = call(
         chunk_kernel,
-        out_shape=shape((groups, rows, piece), BF),
-        in_specs=[SMEM, pl.BlockSpec(memory_space=pl.ANY)],
-        out_specs=VMEM,
-        scratch_shapes=[pltpu.SemaphoreType.DMA((groups,))],
+        [shape((groups, rows, piece), BF)],
+        [SMEM, pl.BlockSpec(memory_space=pl.ANY)],
+        2,
+        [pltpu.SemaphoreType.DMA((groups,))],
     )(lax.axis_index("tp").astype(jnp.int32).reshape(1), layer_input)
     mine = lax.all_to_all(chunks, ROWS, 0, 0, tiled=True)
-    pair = shape((rows, 2 * HD), BF)
-    low, high = call(at(widen_kernel, count), [pair, pair], 5, 0)(place, key_heads, value_heads, left, right)
+    low, high = call(at(widen_kernel, count), [pair, pair], [SMEM] + [VMEM] * 4, COST["widen"])(
+        place, key_heads, value_heads, left, right
+    )
     left2 = shift(low, 2)
     right2 = shift(high, -2)
-    low, high, mine = lax.optimization_barrier((low, high, mine))
-    repeated = pl.pallas_call(
-        repeat_kernel, out_shape=shape((pieces, groups, rows, piece), BF), in_specs=[VMEM], out_specs=VMEM
-    )(mine)
-    tokens = lax.all_to_all(repeated, "tp", 0, 0, tiled=True)
     near_query, near_kv = call(
         near_kernel,
         [shape((rows, width), F32), shape((2, 128, 2 * HD), F32)],
-        8,
-        attend_flops,
-    )(place, q, g, low, high, lse_rows, delta_rows, live)
+        [SMEM] + [VMEM] * 7,
+        COST["near"],
+        mib=12,
+    )(place, q_rows, g_rows, low, high, lse_rows, delta_rows, live)
     query_grad, far_low, far_high = call(
         at(far_kernel, count),
         [shape((1, rows, width), BF), pair, pair],
-        11,
-        attend_flops,
+        [SMEM] + [VMEM] * 10,
+        COST["far"],
         [pltpu.VMEM((2, 128, 2 * HD), F32)],
-    )(place, q, g, low, right, left2, right2, near_query, lse_rows, delta_rows, live)
+        mib=12,
+    )(place, q_rows, g_rows, low, right, left2, right2, near_query, lse_rows, delta_rows, live)
     low2 = shift(far_low, -2)
     high2 = shift(far_high, 2)
-    to_left, to_right = call(at(turn_kernel, count), [shape((C, 2 * HD), BF), pair], 5, 0)(
-        place, near_kv, far_high, low2, high2
-    )
+    low2, mine = lax.optimization_barrier((low2, mine))
+    (repeated,) = call(repeat_kernel, [shape((pieces, groups, rows, piece), BF)], [VMEM], 2)(mine)
+    tokens = lax.all_to_all(repeated, "tp", 0, 0, tiled=True)
+    to_left, to_right = call(
+        at(turn_kernel, count), [shape((C, 2 * HD), BF), pair], [SMEM] + [VMEM] * 4, COST["turn"]
+    )(place, near_kv, far_high, low2, high2)
     low1 = shift(to_left, -1)
     high1 = shift(to_right, 1)
+    grad = shape((1, rows, HD), BF)
     key_grad, value_grad, spread = call(
         at(close_kernel, count),
-        [shape((1, rows, HD), BF), shape((1, rows, HD), BF), shape((groups, rows, HD), BF)],
-        8,
-        0,
+        [grad, grad, shape((groups, rows, HD), BF)],
+        [SMEM] + [VMEM] * 7,
+        COST["close"],
     )(place, near_kv, far_high, low2, high2, to_right, low1, high1)
     spread, tokens = lax.optimization_barrier((spread, tokens))
     everyone = lax.all_to_all(spread, ROWS, 0, 0, tiled=True)
     weight_scale = (lax.axis_size("dp") * doc_ids.shape[1]) ** (-0.5)
-    part = pl.pallas_call(
+    (part,) = call(
         at(weight_kernel, weight_scale),
-        out_shape=shape((steps, piece * pieces // steps, HD), BF),
-        in_specs=[VMEM] * 2,
-        out_specs=VMEM,
-        compiler_params=pltpu.CompilerParams(vmem_limit_bytes=40 * 1024 * 1024),
+        [shape((steps, piece * pieces // steps, HD), BF)],
+        [VMEM] * 2,
+        1,
+        mib=12,
     )(tokens, everyone)
     parts = lax.all_to_all(part, "ctx_1", 0, 0, tiled=True)
     weight_grad = jnp.sum(parts.astype(F32), axis=0)

time: 141 us -> 142 us (level)
  waiting for transfers between devices: 10.5 us -> 27.2 us
  blocking collectives: 65.8 us -> 54.6 us
  Pallas kernels: 14.6 us -> 11.8 us
  local copies, waits for them, and re-layouts: 5.01 us -> 2.41 us
    all_to_all x1, waiting for transfers between devices: 0.01 us -> 17.7 us  [body(): tokens = lax.all_to_all(repeated, 'tp', 0, 0, tiled=True)]
    all_to_all x1, blocking collectives: 42.6 us -> 29.3 us  [body(): everyone = lax.all_to_all(spread, ROWS, 0, 0, tiled=True)]
    ppermute x8, starting transfers between devices: 23 us -> 17.5 us  [shift(): return lax.ppermute(value, CTX, pairs)]
    all_to_all x1, starting transfers between devices: 16.4 us -> 22 us  [body(): mine = lax.all_to_all(chunks, ROWS, 0, 0, tiled=True)]
    pallas_call x9, Pallas kernels: 11.8 us -> 9.03 us  [the longest x1 3.47 us: body(): call(at(far_kernel, count), [shape((1, rows, width), BF), pair, pair], [S...]
    unnamed x22 -> x18, local copies, waits for them, and re-layouts: 5.01 us -> 2.41 us
    all_to_all x1, blocking collectives: 23.1 us -> 25.4 us  [body(): parts = lax.all_to_all(part, 'ctx_1', 0, 0, tiled=True)]
  transfers between devices with their start and end apart: 10 -> 10, of which waited for: 5 -> 4; matrix products, arithmetic and copies ran while one was open for 0% -> 0% of each run, Pallas kernels for 7% -> 7%
where the time goes in v3:
time: 142 us; the launch traced here: 141 us
  blocking collectives  54.6 us (38%)
  starting transfers between devices  43.8 us (31%)
  waiting for transfers between devices  27.2 us (19%)
  Pallas kernels  11.8 us (8%)
  local copies, waits for them, and re-layouts  2.41 us (2%)
    all_to_all x1, blocking collectives, body(): everyone = lax.all_to_all(spread, ROWS, 0, 0, tiled=True)  29.3 us
    all_to_all x1, blocking collectives, body(): parts = lax.all_to_all(part, 'ctx_1', 0, 0, tiled=True)  25.4 us
    all_to_all x1, starting transfers between devices, body(): mine = lax.all_to_all(chunks, ROWS, 0, 0, tiled=True)  22 us
    all_to_all x1, waiting for transfers between devices, body(): tokens = lax.all_to_all(repeated, 'tp', 0, 0, tiled=True)  17.7 us
    ppermute x8, starting transfers between devices, shift(): return lax.ppermute(value, CTX, pairs)  17.5 us
    ppermute x8, waiting for transfers between devices, shift(): return lax.ppermute(value, CTX, pairs)  9.46 us
    all_to_all x1, starting transfers between devices, body(): tokens = lax.all_to_all(repeated, 'tp', 0, 0, tiled=True)  4.3 us
    pallas_call x1, Pallas kernels, body(): call(at(far_kernel, count), [shape((1, rows, width), BF), pair, pair], [S...  3.47 us
  transfers between devices with their start and end apart: 10, of which 4 were waited for; matrix products, arithmetic and copies ran while one was open for 0% of the time, Pallas kernels for 7%

profile of v3, /device:TPU:8, one launch (start us, length us, event | category | flops | bytes accessed | tf_op | source)
XLA Modules:
  0.0 141.3 jit_solution(7449643549437982733)
XLA Ops:
  0.6 1.6 %pack_kernel.1 = bf16[128,256]{1,0:T(8,128)(2,1)} custom-call(bf16[1,128,128]{2,1,0:T(8,128)(2,1)} %k_ref.3, bf16[1,128,128]{2,1,0:T(8,128)(2,1)} %v_ref.3), custom_call_target="tpu_custom_call" | custom-call | flops 1000000000 | tf_op jit(solution)/shard_map/pack_kernel/pallas_call | solution.py:276
  2.2 4.3 %collective-permute-start = (bf16[128,256]{1,0:T(8,128)(2,1)}, bf16[128,256]{1,0:T(8,128)(2,1)S(1)}, u32[]{:S(2)}, u32[]{:S(2)}) collective-permute-start(bf16[128,256]{1,0:T(8,128)(2,1)} %pack_kernel.1), channel_id=1, source_target_pairs={{0,8},{8,16},{16,24},{24,32},{32,40},{40,48},{48,56},{56,64},{64,7... | collective-permute-start | bytes 196616 | tf_op jit(solution)/shard_map/ppermute | solution.py:257
  6.5 1.3 collective-permute-start.1
  7.8 0.9 chunk_kernel.1
  8.8 22.0 %all-to-all-start = ((bf16[8,128,128]{2,1,0:T(8,128)(2,1)}), bf16[8,128,128]{2,1,0:T(8,128)(2,1)S(1)}, u32[]{:S(2)}, u32[]{:S(2)}) async-start(bf16[8,128,128]{2,1,0:T(8,128)(2,1)} %chunk_kernel.1), calls=%async_computation | async-start | bytes 524288 | tf_op jit(solution)/shard_map/all_to_all | solution.py:294
  30.8 1.0 copy-done.4
  31.9 1.3 prepare_kernel.1
  33.2 1.3 collective-permute-start.2
  34.5 1.3 collective-permute-start.3
  35.8 2.7 %near_kernel.1 = (f32[128,2048]{1,0:T(8,128)S(1)}, f32[2,128,256]{2,1,0:T(8,128)S(1)}) custom-call(s32[1]{0:T(128)} %bitcast.idx_ref, bf16[2,4,256,128]{3,2,1,0:T(8,128)(2,1)S(1)} %get-tuple-element.27.q_rows, bf16[2,4,256,128]{3,2,1,0:T(8,128)(2,1)S(1)} %get-tuple-element.28.g_rows, bf16[128,256]{1,0:T(8,128)(2,1)S(1)} %get-tuple-element.31.low_ref.near_low_ref, ...), custom_call_target="tpu_custom_call" | custom-call | flops 3000000000 | tf_op jit(solution)/shard_map/near_kernel/pallas_call | solution.py:300
  38.6 3.0 %collective-permute-done.3.right2_ref = bf16[128,256]{1,0:T(8,128)(2,1)S(1)} collective-permute-done((bf16[128,256]{1,0:T(8,128)(2,1)S(1)}, bf16[128,256]{1,0:T(8,128)(2,1)S(1)}, u32[]{:S(2)}, u32[]{:S(2)}) %collective-permute-start.3) | collective-permute-done | bytes 65568 | tf_op jit(solution)/shard_map/ppermute | solution.py:257
  41.6 3.5 %far_kernel.1 = (bf16[1,128,2048]{2,1,0:T(8,128)(2,1)}, bf16[128,256]{1,0:T(8,128)(2,1)S(1)}, bf16[128,256]{1,0:T(8,128)(2,1)S(1)}) custom-call(s32[1]{0:T(128)} %bitcast.idx_ref, bf16[2,4,256,128]{3,2,1,0:T(8,128)(2,1)S(1)} %get-tuple-element.27.q_rows, bf16[2,4,256,128]{3,2,1,0:T(8,128)(2,1)S(1)} %get-tuple-element.28.g_rows, ...), custom_call_target="tpu_custom_call" | custom-call | flops 3000000000 | tf_op jit(solution)/shard_map/far_kernel/pallas_call | solution.py:307
  45.0 1.3 collective-permute-start.4
  46.3 5.4 %collective-permute-start.5 = (bf16[128,256]{1,0:T(8,128)(2,1)S(1)}, bf16[128,256]{1,0:T(8,128)(2,1)S(1)}, u32[]{:S(2)}, u32[]{:S(2)}) collective-permute-start(bf16[128,256]{1,0:T(8,128)(2,1)S(1)} %get-tuple-element.39.high_ref), channel_id=1, source_target_pairs={{0,16},{8,24},{16,32},{24,40},{32,48},{40,56},{48,64},{56,72},{64,... | collective-permute-start | bytes 196616 | tf_op jit(solution)/shard_map/ppermute | solution.py:257
  52.4 1.3 copy-done
  53.7 4.3 %all-to-all-start.1 = ((bf16[8,8,128,128]{3,2,1,0:T(8,128)(2,1)}), bf16[8,8,128,128]{3,2,1,0:T(8,128)(2,1)S(1)}, u32[]{:S(2)}, u32[]{:S(2)}) async-start(bf16[8,8,128,128]{3,2,1,0:T(8,128)(2,1)} %copy-done), calls=%async_computation.1 | async-start | bytes 4194304 | tf_op jit(solution)/shard_map/all_to_all | solution.py:319
  58.1 1.3 collective-permute-start.7
  59.4 1.3 collective-permute-start.6
  60.7 6.1 %collective-permute-done.6.low1_ref = bf16[64,256]{1,0:T(8,128)(2,1)S(1)} collective-permute-done((bf16[64,256]{1,0:T(8,128)(2,1)S(1)}, bf16[64,256]{1,0:T(8,128)(2,1)S(1)}, u32[]{:S(2)}, u32[]{:S(2)}) %collective-permute-start.6) | collective-permute-done | bytes 32800 | tf_op jit(solution)/shard_map/ppermute | solution.py:257
  66.8 0.7 close_kernel.1
  67.5 17.7 %all-to-all-done.1.x_ref = bf16[8,8,128,128]{3,2,1,0:T(8,128)(2,1)S(1)} async-done(((bf16[8,8,128,128]{3,2,1,0:T(8,128)(2,1)}), bf16[8,8,128,128]{3,2,1,0:T(8,128)(2,1)S(1)}, u32[]{:S(2)}, u32[]{:S(2)}) %all-to-all-start.1) | async-done | bytes 2097184 | tf_op jit(solution)/shard_map/all_to_all | solution.py:319
  85.2 29.3 %all_to_all.20.dv_ref = bf16[8,128,128]{2,1,0:T(8,128)(2,1)S(1)} all-to-all(bf16[8,128,128]{2,1,0:T(8,128)(2,1)S(1)} %get-tuple-element.49), channel_id=1, replica_groups=mesh['dp'=4,'ctx_0'=2,'ctx_1'=16,'tp'=8] {'dp','ctx_0'}, dimensions={0} | all-to-all | bytes 524288 | tf_op jit(solution)/shard_map/all_to_all | solution.py:333
  114.5 0.8 weight_kernel.1
  115.3 25.4 %all_to_all.21 = bf16[16,64,128]{2,1,0:T(8,128)(2,1)S(1)} all-to-all(bf16[16,64,128]{2,1,0:T(8,128)(2,1)S(1)} %weight_kernel.1), channel_id=1, replica_groups=mesh['dp'=4,'ctx_0'=2,'ctx_1'=16,'tp'=8] {'ctx_1'}, dimensions={0} | all-to-all | bytes 524288 | tf_op jit(solution)/shard_map/all_to_all | solution.py:342
  (27 shorter events, 1.3 us)
Async XLA Ops:
  0.6 7.2 %copy-start.1 = (bf16[1,128,8192]{2,1,0:T(8,128)(2,1)S(1)}, bf16[1,128,8192]{2,1,0:T(8,128)(2,1)}, u32[]{:S(2)}) copy-start(bf16[1,128,8192]{2,1,0:T(8,128)(2,1)} %x_ref.1) | copy-start | bytes 6291460
  2.2 30.9 %collective-permute-start = (bf16[128,256]{1,0:T(8,128)(2,1)}, bf16[128,256]{1,0:T(8,128)(2,1)S(1)}, u32[]{:S(2)}, u32[]{:S(2)}) collective-permute-start(bf16[128,256]{1,0:T(8,128)(2,1)} %pack_kernel.1), channel_id=1, source_target_pairs={{0,8},{8,16},{16,24},{24,32},{32,40},{40,48},{48,56},{56,64},{64,7... | collective-permute-start | bytes 196616 | tf_op jit(solution)/shard_map/ppermute | solution.py:257
  6.5 26.7 %collective-permute-start.1 = (bf16[128,256]{1,0:T(8,128)(2,1)}, bf16[128,256]{1,0:T(8,128)(2,1)S(1)}, u32[]{:S(2)}, u32[]{:S(2)}) collective-permute-start(bf16[128,256]{1,0:T(8,128)(2,1)} %pack_kernel.1), channel_id=1, source_target_pairs={{8,0},{16,8},{24,16},{32,24},{40,32},{48,40},{56,48},{64,56},{72,6... | collective-permute-start | bytes 196616 | tf_op jit(solution)/shard_map/ppermute | solution.py:257
  7.8 23.0 %copy-start.2 = (bf16[1,128,2048]{2,1,0:T(8,128)(2,1)S(1)}, bf16[1,128,2048]{2,1,0:T(8,128)(2,1)}, u32[]{:S(2)}) copy-start(bf16[1,128,2048]{2,1,0:T(8,128)(2,1)} %param.9) | copy-start | bytes 1572868
  7.8 23.0 %copy-start.3 = (bf16[1,128,2048]{2,1,0:T(8,128)(2,1)S(1)}, bf16[1,128,2048]{2,1,0:T(8,128)(2,1)}, u32[]{:S(2)}) copy-start(bf16[1,128,2048]{2,1,0:T(8,128)(2,1)} %param.13) | copy-start | bytes 1572868
  7.8 23.0 %copy-start.7 = (s32[1,4096]{1,0:T(1,128)S(1)}, s32[1,4096]{1,0:T(1,128)}, u32[]{:S(2)}) copy-start(s32[1,4096]{1,0:T(1,128)} %doc_ref.1) | copy-start | bytes 49156
  7.8 23.0 %copy-start.8 = (f32[1,16,128]{2,1,0:T(8,128)S(1)}, f32[1,16,128]{2,1,0:T(8,128)}, u32[]{:S(2)}) copy-start(f32[1,16,128]{2,1,0:T(8,128)} %param.14) | copy-start | bytes 24580
  8.7 24.4 %copy-start.5 = (bf16[1,128,128]{2,1,0:T(8,128)(2,1)S(1)}, bf16[1,128,128]{2,1,0:T(8,128)(2,1)}, u32[]{:S(2)}) copy-start(bf16[1,128,128]{2,1,0:T(8,128)(2,1)} %k_ref.3) | copy-start | bytes 98308
  8.7 24.4 %copy-start.6 = (bf16[1,128,128]{2,1,0:T(8,128)(2,1)S(1)}, bf16[1,128,128]{2,1,0:T(8,128)(2,1)}, u32[]{:S(2)}) copy-start(bf16[1,128,128]{2,1,0:T(8,128)(2,1)} %v_ref.3) | copy-start | bytes 98308
  8.8 43.3 %all-to-all-start = ((bf16[8,128,128]{2,1,0:T(8,128)(2,1)}), bf16[8,128,128]{2,1,0:T(8,128)(2,1)S(1)}, u32[]{:S(2)}, u32[]{:S(2)}) async-start(bf16[8,128,128]{2,1,0:T(8,128)(2,1)} %chunk_kernel.1), calls=%async_computation | async-start | bytes 524288 | tf_op jit(solution)/shard_map/all_to_all | solution.py:294
  30.8 1.0 copy-start.4
  33.2 5.4 %collective-permute-start.2 = (bf16[128,256]{1,0:T(8,128)(2,1)S(1)}, bf16[128,256]{1,0:T(8,128)(2,1)S(1)}, u32[]{:S(2)}, u32[]{:S(2)}) collective-permute-start(bf16[128,256]{1,0:T(8,128)(2,1)S(1)} %get-tuple-element.31.low_ref.near_low_ref), channel_id=1, source_target_pairs={{0,16},{8,24},{16,32},{24,40},{32,48},{40,56},{48,64},{56,72},{64,... | collective-permute-start | bytes 196616 | tf_op jit(solution)/shard_map/ppermute | solution.py:257
  34.5 7.1 %collective-permute-start.3 = (bf16[128,256]{1,0:T(8,128)(2,1)S(1)}, bf16[128,256]{1,0:T(8,128)(2,1)S(1)}, u32[]{:S(2)}, u32[]{:S(2)}) collective-permute-start(bf16[128,256]{1,0:T(8,128)(2,1)S(1)} %get-tuple-element.32.high_ref), channel_id=1, source_target_pairs={{16,0},{24,8},{32,16},{40,24},{48,32},{56,40},{64,48},{72,56},{80,... | collective-permute-start | bytes 196616 | tf_op jit(solution)/shard_map/ppermute | solution.py:257
  45.0 7.0 %collective-permute-start.4 = (bf16[128,256]{1,0:T(8,128)(2,1)S(1)}, bf16[128,256]{1,0:T(8,128)(2,1)S(1)}, u32[]{:S(2)}, u32[]{:S(2)}) collective-permute-start(bf16[128,256]{1,0:T(8,128)(2,1)S(1)} %get-tuple-element.40), channel_id=1, source_target_pairs={{16,0},{24,8},{32,16},{40,24},{48,32},{56,40},{64,48},{72,56},{80,... | collective-permute-start | bytes 196616 | tf_op jit(solution)/shard_map/ppermute | solution.py:257
  46.3 11.7 %collective-permute-start.5 = (bf16[128,256]{1,0:T(8,128)(2,1)S(1)}, bf16[128,256]{1,0:T(8,128)(2,1)S(1)}, u32[]{:S(2)}, u32[]{:S(2)}) collective-permute-start(bf16[128,256]{1,0:T(8,128)(2,1)S(1)} %get-tuple-element.39.high_ref), channel_id=1, source_target_pairs={{0,16},{8,24},{16,32},{24,40},{32,48},{40,56},{48,64},{56,72},{64,... | collective-permute-start | bytes 196616 | tf_op jit(solution)/shard_map/ppermute | solution.py:257
  52.4 1.3 copy-start
  53.7 31.5 %all-to-all-start.1 = ((bf16[8,8,128,128]{3,2,1,0:T(8,128)(2,1)}), bf16[8,8,128,128]{3,2,1,0:T(8,128)(2,1)S(1)}, u32[]{:S(2)}, u32[]{:S(2)}) async-start(bf16[8,8,128,128]{3,2,1,0:T(8,128)(2,1)} %copy-done), calls=%async_computation.1 | async-start | bytes 4194304 | tf_op jit(solution)/shard_map/all_to_all | solution.py:319
  58.1 8.8 %collective-permute-start.7 = (bf16[128,256]{1,0:T(8,128)(2,1)S(1)}, bf16[128,256]{1,0:T(8,128)(2,1)S(1)}, u32[]{:S(2)}, u32[]{:S(2)}) collective-permute-start(bf16[128,256]{1,0:T(8,128)(2,1)S(1)} %get-tuple-element.42.right_ref), channel_id=1, source_target_pairs={{0,8},{8,16},{16,24},{24,32},{32,40},{40,48},{48,56},{56,64},{64,7... | collective-permute-start | bytes 196616 | tf_op jit(solution)/shard_map/ppermute | solution.py:257
  59.4 7.4 %collective-permute-start.6 = (bf16[64,256]{1,0:T(8,128)(2,1)S(1)}, bf16[64,256]{1,0:T(8,128)(2,1)S(1)}, u32[]{:S(2)}, u32[]{:S(2)}) collective-permute-start(bf16[64,256]{1,0:T(8,128)(2,1)S(1)} %get-tuple-element.43), channel_id=1, source_target_pairs={{8,0},{16,8},{24,16},{32,24},{40,32},{48,40},{56,48},{64,56},{72,6... | collective-permute-start | bytes 98312 | tf_op jit(solution)/shard_map/ppermute | solution.py:257

commit v4 on v3

--- a/solution.py
+++ b/solution.py
@@ -13,12 +13,14 @@
 CTX = ("ctx_0", "ctx_1")
 ROWS = ("dp", "ctx_0")
 DP_CTX = ("dp", "ctx_0", "ctx_1")
+TP = ("tp_x", "core")
 SCALE = HD ** (-0.5)
 BF = jnp.bfloat16
 F32 = jnp.float32
 SMEM = pl.BlockSpec(memory_space=pltpu.SMEM)
 VMEM = pl.BlockSpec(memory_space=pltpu.VMEM)
-COST = {"prepare": 1, "widen": 0.1, "near": 3, "far": 3, "turn": 10, "close": 10}
+ANY = pl.BlockSpec(memory_space=pl.ANY)
+COST = {"prepare": 2, "widen": 0.1, "near": 0.3, "far": 0.3, "turn": 10, "close": 5, "finish": 0.5}
 
 
 def call(kernel, outs, in_specs, us, scratch=(), mib=8):
@@ -95,18 +97,47 @@
     return jnp.where(where, a.astype(F32), b.astype(F32))
 
 
-def pack_kernel(k_ref, v_ref, out_ref):
-    out_ref[:, :HD] = k_ref[0]
-    out_ref[:, HD:] = v_ref[0]
-
-
-def widen_kernel(count, idx_ref, k_ref, v_ref, left_ref, right_ref, low_ref, high_ref):
-    last = idx_ref[0] == count - 1
-    low_ref[:C] = left_ref[:C]
-    for own_ref, lanes in ((k_ref, slice(0, HD)), (v_ref, slice(HD, 2 * HD))):
-        low_ref[C:, lanes] = own_ref[0, :C]
-        high_ref[:C, lanes] = pick(last, own_ref[0, :C], right_ref[C:, lanes]).astype(BF)
-        high_ref[C:, lanes] = own_ref[0, C:]
+def pack_kernel(count, idx_ref, k_ref, v_ref, kv_ref, cross_ref, k_buf, v_buf, sems):
+    copies = [
+        pltpu.make_async_copy(k_ref.at[0], k_buf, sems.at[0]),
+        pltpu.make_async_copy(v_ref.at[0], v_buf, sems.at[1]),
+    ]
+    for copy in copies:
+        copy.start()
+    for copy in copies:
+        copy.wait()
+    kv_ref[:, :HD] = k_buf[...]
+    kv_ref[:, HD:] = v_buf[...]
+    first = idx_ref[0] < count // 2
+    cross_ref[:, :HD] = pick(first, k_buf[:C], k_buf[C:]).astype(BF)
+    cross_ref[:, HD:] = pick(first, v_buf[:C], v_buf[C:]).astype(BF)
+
+
+def first_kernel(count, idx_ref, kv_ref, cross_ref, left_ref, right_ref):
+    place = idx_ref[0]
+    left_ref[:C] = pick(place == count - 1, cross_ref[...], kv_ref[:C]).astype(BF)
+    left_ref[C:] = cross_ref[...]
+    right_ref[:C] = kv_ref[:C]
+    right_ref[C : 2 * C] = pick(place == 0, cross_ref[...], kv_ref[C:]).astype(BF)
+    right_ref[2 * C :] = cross_ref[...]
+
+
+def widen_kernel(
+    count, idx_ref, kv_ref, cross_ref, left_ref, right_ref, low_ref, high_ref, send_low_ref, send_high_ref
+):
+    place = idx_ref[0]
+    lower, upper, other = kv_ref[:C], kv_ref[C:], cross_ref[...]
+    before_lower = left_ref[:C]
+    before_upper = pick(place == count - 1, lower, right_ref[C : 2 * C]).astype(BF)
+    low_ref[:C] = before_lower
+    low_ref[C:] = lower
+    high_ref[:C] = before_upper
+    high_ref[C:] = upper
+    end, start = place >= count - 2, place < 2
+    send_low_ref[:C] = pick(end, left_ref[C:], before_lower).astype(BF)
+    send_low_ref[C:] = pick(end, other, lower).astype(BF)
+    send_high_ref[:C] = pick(start, right_ref[2 * C :], before_upper).astype(BF)
+    send_high_ref[C:] = pick(start, other, upper).astype(BF)
 
 
 def prepare_kernel(
@@ -186,11 +217,15 @@
 
 
 def turn_kernel(count, idx_ref, kv_ref, high_ref, low2_ref, high2_ref, left_ref, right_ref):
-    last = idx_ref[0] == count - 1
-    mine = jnp.where(last, high_ref[C:].astype(F32), 0.0)
-    left_ref[...] = (kv_ref[0, :C] + low2_ref[:C].astype(F32) + mine).astype(BF)
-    right_ref[:C] = (kv_ref[1, :C] + high2_ref[:C].astype(F32)).astype(BF)
-    right_ref[C:] = high_ref[C:]
+    place = idx_ref[0]
+    end, start = place >= count - 2, place < 2
+    low2, high2 = low2_ref[:C].astype(F32), high2_ref[:C].astype(F32)
+    mine = jnp.where(place == count - 1, high_ref[C:].astype(F32), 0.0)
+    left_ref[:C] = (kv_ref[0, :C] + jnp.where(end, 0.0, low2) + mine).astype(BF)
+    left_ref[C:] = jnp.where(end, low2, 0.0).astype(BF)
+    right_ref[:C] = (kv_ref[1, :C] + jnp.where(start, 0.0, high2)).astype(BF)
+    right_ref[C : 2 * C] = high_ref[C:]
+    right_ref[2 * C :] = jnp.where(start, high2, 0.0).astype(BF)
 
 
 def close_kernel(
@@ -203,21 +238,44 @@
     right_ref,
     low1_ref,
     high1_ref,
-    dk_ref,
-    dv_ref,
+    own_ref,
+    cross_ref,
     spread_ref,
 ):
     place = idx_ref[0]
     last, before = place == count - 1, place == count - 2
-    lower = kv_ref[0, C:] + low2_ref[C:].astype(F32) + low1_ref[...].astype(F32)
-    lower += jnp.where(last, high1_ref[C:].astype(F32) + right_ref[:C].astype(F32), 0.0)
+    end, start = place >= count - 2, place < 2
+    low2, high2 = low2_ref[C:].astype(F32), high2_ref[C:].astype(F32)
+    low1, high1 = low1_ref[:C].astype(F32), high1_ref[:C].astype(F32)
+    lower = kv_ref[0, C:] + jnp.where(end, 0.0, low2) + jnp.where(last, 0.0, low1)
+    lower += jnp.where(last, high1_ref[C : 2 * C].astype(F32) + right_ref[:C].astype(F32), 0.0)
     lower += jnp.where(before, high_ref[:C].astype(F32), 0.0)
-    upper = kv_ref[1, C:] + high2_ref[C:].astype(F32) + high1_ref[:C].astype(F32)
-    both = jnp.concatenate([lower, upper], axis=0).astype(BF)
-    dk_ref[0] = both[:, :HD]
-    dv_ref[0] = both[:, HD:]
+    upper = kv_ref[1, C:] + jnp.where(start, 0.0, high2) + jnp.where(place == 0, 0.0, high1)
+    own_ref[:C] = lower
+    own_ref[C:] = upper
+    near_end = before | (place == count - 3)
+    near_start = (place == 1) | (place == 2)
+    back = jnp.where(end, low2, 0.0) + jnp.where(last, low1, 0.0)
+    back += jnp.where(near_end, low1_ref[C:].astype(F32), 0.0)
+    forth = jnp.where(start, high2, 0.0) + jnp.where(place == 0, high1, 0.0)
+    forth += jnp.where(near_start, high1_ref[2 * C :].astype(F32), 0.0)
+    cross = jnp.where(place >= count // 2, back, forth).astype(BF)
+    cross_ref[...] = cross
     for i in range(spread_ref.shape[0]):
-        spread_ref[i] = both[:, HD:]
+        spread_ref[i, :C] = lower[:, HD:].astype(BF)
+        spread_ref[i, C : 2 * C] = upper[:, HD:].astype(BF)
+        spread_ref[i, 2 * C :] = cross[:, HD:]
+
+
+def finish_kernel(count, idx_ref, own_ref, cross_ref, dk_ref, dv_ref):
+    first = idx_ref[0] < count // 2
+    cross = cross_ref[...].astype(F32)
+    lower = own_ref[:C] + jnp.where(first, cross, 0.0)
+    upper = own_ref[C:] + jnp.where(first, 0.0, cross)
+    dk_ref[0, :C] = lower[:, :HD].astype(BF)
+    dk_ref[0, C:] = upper[:, :HD].astype(BF)
+    dv_ref[0, :C] = lower[:, HD:].astype(BF)
+    dv_ref[0, C:] = upper[:, HD:].astype(BF)
 
 
 def chunk_kernel(tp_ref, x_ref, out_ref, sems):
@@ -238,23 +296,42 @@
         out_ref[i] = x_ref[...]
 
 
-def weight_kernel(scale, x_ref, dv_ref, out_ref):
-    pieces, parts, tokens, width = x_ref.shape
-    each = out_ref.shape[0] // pieces
-    dv = dv_ref[...].reshape(parts * tokens, HD).T
+def weight_kernel(scale, core_ref, mine_ref, theirs_ref, dv_ref, out_ref):
+    pieces, parts, tokens, width = mine_ref.shape
+    each = out_ref.shape[0] // (2 * pieces)
+    rows = []
+    for i in range(parts):
+        lower, upper = dv_ref[i, :C].astype(F32), dv_ref[i, C : 2 * C].astype(F32)
+        cross = dv_ref[i ^ 1, 2 * C :].astype(F32)
+        if i % 2 == 0:
+            lower += cross
+        else:
+            upper += cross
+        rows += [lower.astype(BF), upper.astype(BF)]
+    dv = jnp.concatenate(rows, axis=0).T
     for i in range(pieces):
-        x = x_ref[i].reshape(parts * tokens, width)
-        flat = jnp.dot(dv, x, preferred_element_type=F32) * scale
-        out_ref[i * each : (i + 1) * each] = flat.T.astype(BF).reshape(each, width // each, HD)
-
-
-def shift(value, by):
-    count = lax.axis_size(CTX)
-    if by > 0:
-        pairs = [(i, i + by) for i in range(count - by)]
-    else:
-        pairs = [(i - by, i) for i in range(count + by)]
+        for x_ref, core in ((mine_ref, core_ref[0]), (theirs_ref, 1 - core_ref[0])):
+            x = x_ref[i].reshape(parts * tokens, width)
+            flat = jnp.dot(dv, x, preferred_element_type=F32) * scale
+            flat = flat.T.astype(BF).reshape(each, width // each, HD)
+            out_ref[pl.ds((2 * i + core) * each, each)] = flat
+
+
+def shift(value, by, wrap_half):
+    length = lax.axis_size("ctx_1")
+    pairs = [
+        (h * length + z, h * length + (z + by) % length)
+        for h in range(2)
+        for z in range(length)
+        if h == wrap_half or 0 <= z + by < length
+    ]
     return lax.ppermute(value, CTX, pairs)
+
+
+def swap(value, back):
+    length = lax.axis_size("ctx_1")
+    pairs = [(z, length + z) for z in range(length - 3, length)] + [(length + z, z) for z in range(3)]
+    return lax.ppermute(value, CTX, [(b, a) for a, b in pairs] if back else pairs)
 
 
 def body(layer_input, queries, key_heads, value_heads, attn_out, out_grad, log_sums, doc_ids):
@@ -264,18 +341,25 @@
     rows = 2 * C
     groups = lax.axis_size(ROWS)
     steps = lax.axis_size("ctx_1")
-    pieces = lax.axis_size("tp")
+    pieces = lax.axis_size(TP)
     piece = layer_input.shape[2] // (groups * pieces)
     heads = width // HD
     group = min(4, heads)
     row_terms = shape((2, heads // group, group * C, 128), F32)
     head_rows = shape(row_terms.shape, BF)
-    pair = shape((rows, 2 * HD), BF)
+    pair, block, three = (shape((n * C, 2 * HD), BF) for n in (2, 1, 3))
     at = functools.partial
 
-    (kv,) = call(pack_kernel, [pair], [VMEM] * 2, 1, mib=56)(key_heads, value_heads)
-    left = shift(kv, 1)
-    right = shift(kv, -1)
+    kv, cross = call(
+        at(pack_kernel, count),
+        [pair, block],
+        [SMEM, ANY, ANY],
+        1,
+        [pltpu.VMEM((rows, HD), BF), pltpu.VMEM((rows, HD), BF), pltpu.SemaphoreType.DMA((2,))],
+        mib=56,
+    )(place, key_heads, value_heads)
+    kv, part_of = lax.optimization_barrier((kv, lax.axis_index(TP).astype(jnp.int32).reshape(1)))
+    cross = swap(cross, False)
     q_rows, g_rows, lse_rows, delta_rows, live = call(
         at(prepare_kernel, count),
         [head_rows, head_rows, row_terms, row_terms, shape((2, 2, C, 128), F32)],
@@ -283,20 +367,25 @@
         COST["prepare"],
         mib=12,
     )(place, queries[0], out_grad[0], attn_out[0], log_sums[0], doc_ids)
-    left, live = lax.optimization_barrier((left, live))
+    cross, live = lax.optimization_barrier((cross, live))
     (chunks,) = call(
         chunk_kernel,
         [shape((groups, rows, piece), BF)],
-        [SMEM, pl.BlockSpec(memory_space=pl.ANY)],
+        [SMEM, ANY],
         2,
         [pltpu.SemaphoreType.DMA((groups,))],
-    )(lax.axis_index("tp").astype(jnp.int32).reshape(1), layer_input)
+    )(part_of, layer_input)
     mine = lax.all_to_all(chunks, ROWS, 0, 0, tiled=True)
-    low, high = call(at(widen_kernel, count), [pair, pair], [SMEM] + [VMEM] * 4, COST["widen"])(
-        place, key_heads, value_heads, left, right
+    to_left, to_right = call(at(first_kernel, count), [pair, three], [SMEM] + [VMEM] * 2, COST["widen"])(
+        place, kv, cross
     )
-    left2 = shift(low, 2)
-    right2 = shift(high, -2)
+    left = shift(to_left, 1, 1)
+    right = shift(to_right, -1, 0)
+    low, high, send_low, send_high = call(
+        at(widen_kernel, count), [pair] * 4, [SMEM] + [VMEM] * 4, COST["widen"]
+    )(place, kv, cross, left, right)
+    left2 = shift(send_low, 2, 1)
+    right2 = shift(send_high, -2, 0)
     near_query, near_kv = call(
         near_kernel,
         [shape((rows, width), F32), shape((2, 128, 2 * HD), F32)],
@@ -312,53 +401,59 @@
         [pltpu.VMEM((2, 128, 2 * HD), F32)],
         mib=12,
     )(place, q_rows, g_rows, low, right, left2, right2, near_query, lse_rows, delta_rows, live)
-    low2 = shift(far_low, -2)
-    high2 = shift(far_high, 2)
+    low2 = shift(far_low, -2, 1)
+    high2 = shift(far_high, 2, 0)
     low2, mine = lax.optimization_barrier((low2, mine))
-    (repeated,) = call(repeat_kernel, [shape((pieces, groups, rows, piece), BF)], [VMEM], 2)(mine)
-    tokens = lax.all_to_all(repeated, "tp", 0, 0, tiled=True)
+    (repeated,) = call(repeat_kernel, [shape((pieces // 2, groups, rows, piece), BF)], [VMEM], 1)(mine)
+    tokens = lax.all_to_all(repeated, "tp_x", 0, 0, tiled=True)
     to_left, to_right = call(
-        at(turn_kernel, count), [shape((C, 2 * HD), BF), pair], [SMEM] + [VMEM] * 4, COST["turn"]
+        at(turn_kernel, count), [pair, three], [SMEM] + [VMEM] * 4, COST["turn"]
     )(place, near_kv, far_high, low2, high2)
-    low1 = shift(to_left, -1)
-    high1 = shift(to_right, 1)
-    grad = shape((1, rows, HD), BF)
-    key_grad, value_grad, spread = call(
+    low1 = shift(to_left, -1, 1)
+    high1 = shift(to_right, 1, 0)
+    own, cross, spread = call(
         at(close_kernel, count),
-        [grad, grad, shape((groups, rows, HD), BF)],
+        [shape((rows, 2 * HD), F32), block, shape((groups, 3 * C, HD), BF)],
         [SMEM] + [VMEM] * 7,
         COST["close"],
     )(place, near_kv, far_high, low2, high2, to_right, low1, high1)
     spread, tokens = lax.optimization_barrier((spread, tokens))
+    tokens_2 = lax.ppermute(tokens, "core", [(0, 1), (1, 0)])
     everyone = lax.all_to_all(spread, ROWS, 0, 0, tiled=True)
     weight_scale = (lax.axis_size("dp") * doc_ids.shape[1]) ** (-0.5)
     (part,) = call(
         at(weight_kernel, weight_scale),
         [shape((steps, piece * pieces // steps, HD), BF)],
-        [VMEM] * 2,
+        [SMEM] + [VMEM] * 3,
         1,
         mib=12,
-    )(tokens, everyone)
+    )(lax.axis_index("core").astype(jnp.int32).reshape(1), tokens, tokens_2, everyone)
+    part, cross = lax.optimization_barrier((part, cross))
     parts = lax.all_to_all(part, "ctx_1", 0, 0, tiled=True)
+    cross = swap(cross, True)
+    grad = shape((1, rows, HD), BF)
+    key_grad, value_grad = call(at(finish_kernel, count), [grad, grad], [SMEM] + [VMEM] * 2, COST["finish"])(
+        place, own, cross
+    )
     weight_grad = jnp.sum(parts.astype(F32), axis=0)
     return (query_grad, key_grad, value_grad, weight_grad)
 
 
 def solution(mesh):
-    tall = 2 if mesh.shape["ctx"] % 2 == 0 else 1
+    sizes = mesh.shape
     split = Mesh(
-        mesh.devices.reshape(mesh.shape["dp"], tall, mesh.shape["ctx"] // tall, mesh.shape["tp"]),
-        ("dp", "ctx_0", "ctx_1", "tp"),
+        mesh.devices.reshape(sizes["dp"], 2, sizes["ctx"] // 2, sizes["tp"] // 2, 2),
+        ("dp", "ctx_0", "ctx_1", "tp_x", "core"),
     )
     in_specs = (
         P("dp", CTX, None),
-        P("dp", CTX, "tp"),
-        P("dp", CTX, "tp"),
-        P("dp", CTX, "tp"),
-        P("dp", CTX, "tp"),
-        P("dp", CTX, "tp"),
-        P("dp", "tp", CTX),
+        P("dp", CTX, TP),
+        P("dp", CTX, TP),
+        P("dp", CTX, TP),
+        P("dp", CTX, TP),
+        P("dp", CTX, TP),
+        P("dp", TP, CTX),
         P("dp", None),
     )
-    out_specs = (P("dp", CTX, "tp"), P("dp", CTX, "tp"), P("dp", CTX, "tp"), P(DP_CTX, "tp"))
+    out_specs = (P("dp", CTX, TP), P("dp", CTX, TP), P("dp", CTX, TP), P(DP_CTX, TP))
     return jax.shard_map(body, mesh=split, in_specs=in_specs, out_specs=out_specs, check_vma=False)

time: 142 us -> 130 us (0.915)
  blocking collectives: 54.6 us -> 21 us
  starting transfers between devices: 43.8 us -> 68.3 us
  waiting for transfers between devices: 27.2 us -> 23.7 us
  Pallas kernels: 11.8 us -> 13.5 us
    all_to_all x1 -> x0, blocking collectives: 25.4 us -> none  [body(): parts = lax.all_to_all(part, 'ctx_1', 0, 0, tiled=True)]
    ppermute x8, starting transfers between devices: 17.5 us -> 27.1 us  [shift(): return lax.ppermute(value, CTX, pairs)]
    all_to_all x1 -> x2, starting transfers between devices: 4.3 us -> 13.5 us  [the longest x1 9.17 us: body(): parts = lax.all_to_all(part, 'ctx_1', 0, 0, tiled=True)]
    all_to_all x1, blocking collectives: 29.3 us -> 21 us  [body(): everyone = lax.all_to_all(spread, ROWS, 0, 0, tiled=True)]
    ppermute x0 -> x3, starting transfers between devices: none -> 6.75 us  [the longest x2 4.84 us: swap(): lax.ppermute(value, CTX, [(b, a) for a, b in pairs] if back else pairs)]
    all_to_all x1 -> x2, waiting for transfers between devices: 17.7 us -> 15 us  [the longest x1 12.6 us: body(): parts = lax.all_to_all(part, 'ctx_1', 0, 0, tiled=True)]
    ppermute x8, waiting for transfers between devices: 9.46 us -> 7.06 us  [shift(): return lax.ppermute(value, CTX, pairs)]
    ppermute x0 -> x3, waiting for transfers between devices: none -> 1.58 us  [the longest x2 1.58 us: swap(): lax.ppermute(value, CTX, [(b, a) for a, b in pairs] if back else pairs)]
  transfers between devices with their start and end apart: 10 -> 14, of which waited for: 4 -> 6; matrix products, arithmetic and copies ran while one was open for 0% -> 0% of each run, Pallas kernels for 7% -> 8%
where the time goes in v4:
time: 130 us; the launch traced here: 129 us
  starting transfers between devices  68.3 us (53%)
  waiting for transfers between devices  23.7 us (18%)
  blocking collectives  21 us (16%)
  Pallas kernels  13.5 us (10%)
    ppermute x8, starting transfers between devices, shift(): return lax.ppermute(value, CTX, pairs)  27.1 us
    all_to_all x1, blocking collectives, body(): everyone = lax.all_to_all(spread, ROWS, 0, 0, tiled=True)  21 us
    all_to_all x1, starting transfers between devices, body(): mine = lax.all_to_all(chunks, ROWS, 0, 0, tiled=True)  20.9 us
    all_to_all x1, waiting for transfers between devices, body(): parts = lax.all_to_all(part, 'ctx_1', 0, 0, tiled=True)  12.6 us
    all_to_all x1, starting transfers between devices, body(): parts = lax.all_to_all(part, 'ctx_1', 0, 0, tiled=True)  9.17 us
    ppermute x8, waiting for transfers between devices, shift(): return lax.ppermute(value, CTX, pairs)  7.06 us
    ppermute x2, starting transfers between devices, swap(): lax.ppermute(value, CTX, [(b, a) for a, b in pairs] if back else pairs)  4.84 us
    all_to_all x1, starting transfers between devices, body(): tokens = lax.all_to_all(repeated, 'tp_x', 0, 0, tiled=True)  4.3 us
  transfers between devices with their start and end apart: 14, of which 6 were waited for; matrix products, arithmetic and copies ran while one was open for 0% of the time, Pallas kernels for 8%

profile of v4, /device:TPU:8, one launch (start us, length us, event | category | flops | bytes accessed | tf_op | source)
XLA Modules:
  0.0 129.0 jit_solution(12996955229744838439)
XLA Ops:
  0.6 1.6 %pack_kernel.1 = (bf16[128,256]{1,0:T(8,128)(2,1)}, bf16[64,256]{1,0:T(8,128)(2,1)}) custom-call(s32[1]{0:T(128)} %bitcast.idx_ref, bf16[1,128,128]{2,1,0:T(8,128)(2,1)} %k_ref.1, bf16[1,128,128]{2,1,0:T(8,128)(2,1)} %v_ref.1), custom_call_target="tpu_custom_call" | custom-call | flops 1000000000 | tf_op jit(solution)/shard_map/pack_kernel/pallas_call | solution.py:353
  2.2 1.3 %collective-permute-start = (bf16[64,256]{1,0:T(8,128)(2,1)}, bf16[64,256]{1,0:T(8,128)(2,1)S(1)}, u32[]{:S(2)}, u32[]{:S(2)}) collective-permute-start(bf16[64,256]{1,0:T(8,128)(2,1)} %get-tuple-element.43), channel_id=1, source_target_pairs={{104,232},{112,240},{120,248},{128,0},{136,8},{144,16},{105,233},{... | collective-permute-start | bytes 98312 | tf_op jit(solution)/shard_map/ppermute | solution.py:334
  4.5 20.9 %all-to-all-start = ((bf16[8,128,128]{2,1,0:T(8,128)(2,1)}), bf16[8,128,128]{2,1,0:T(8,128)(2,1)S(1)}, u32[]{:S(2)}, u32[]{:S(2)}) async-start(bf16[8,128,128]{2,1,0:T(8,128)(2,1)} %chunk_kernel.1), calls=%async_computation | async-start | bytes 524288 | tf_op jit(solution)/shard_map/all_to_all | solution.py:378
  26.5 1.3 prepare_kernel.1
  27.8 7.5 %collective-permute-start.2 = (bf16[192,256]{1,0:T(8,128)(2,1)S(1)}, bf16[192,256]{1,0:T(8,128)(2,1)S(1)}, u32[]{:S(2)}, u32[]{:S(2)}) collective-permute-start(bf16[192,256]{1,0:T(8,128)(2,1)S(1)} %get-tuple-element.47), channel_id=1, source_target_pairs={{0,120},{8,0},{16,8},{24,16},{32,24},{40,32},{48,40},{56,48},{64,5... | collective-permute-start | bytes 294920 | tf_op jit(solution)/shard_map/ppermute | solution.py:328
  35.4 1.3 %collective-permute-start.1 = (bf16[128,256]{1,0:T(8,128)(2,1)S(1)}, bf16[128,256]{1,0:T(8,128)(2,1)S(1)}, u32[]{:S(2)}, u32[]{:S(2)}) collective-permute-start(bf16[128,256]{1,0:T(8,128)(2,1)S(1)} %get-tuple-element.46), channel_id=1, source_target_pairs={{0,8},{8,16},{16,24},{24,32},{32,40},{40,48},{48,56},{56,64},{64,7... | collective-permute-start | bytes 196616 | tf_op jit(solution)/shard_map/ppermute | solution.py:328
  36.7 1.9 %collective-permute-done.1.left_ref = bf16[128,256]{1,0:T(8,128)(2,1)S(1)} collective-permute-done((bf16[128,256]{1,0:T(8,128)(2,1)S(1)}, bf16[128,256]{1,0:T(8,128)(2,1)S(1)}, u32[]{:S(2)}, u32[]{:S(2)}) %collective-permute-start.1) | collective-permute-done | bytes 65568 | tf_op jit(solution)/shard_map/ppermute | solution.py:328
  38.6 1.3 %collective-permute-start.3 = (bf16[128,256]{1,0:T(8,128)(2,1)S(1)}, bf16[128,256]{1,0:T(8,128)(2,1)S(1)}, u32[]{:S(2)}, u32[]{:S(2)}) collective-permute-start(bf16[128,256]{1,0:T(8,128)(2,1)S(1)} %get-tuple-element.49), channel_id=1, source_target_pairs={{0,16},{8,24},{16,32},{24,40},{32,48},{40,56},{48,64},{56,72},{64,... | collective-permute-start | bytes 196616 | tf_op jit(solution)/shard_map/ppermute | solution.py:328
  39.9 5.4 %collective-permute-start.4 = (bf16[128,256]{1,0:T(8,128)(2,1)S(1)}, bf16[128,256]{1,0:T(8,128)(2,1)S(1)}, u32[]{:S(2)}, u32[]{:S(2)}) collective-permute-start(bf16[128,256]{1,0:T(8,128)(2,1)S(1)} %get-tuple-element.50), channel_id=1, source_target_pairs={{0,112},{8,120},{16,0},{24,8},{32,16},{40,24},{48,32},{56,40},{64,... | collective-permute-start | bytes 196616 | tf_op jit(solution)/shard_map/ppermute | solution.py:328
  45.3 2.8 %near_kernel.1 = (f32[128,2048]{1,0:T(8,128)S(1)}, f32[2,128,256]{2,1,0:T(8,128)S(1)}) custom-call(s32[1]{0:T(128)} %bitcast.idx_ref, bf16[2,4,256,128]{3,2,1,0:T(8,128)(2,1)S(1)} %get-tuple-element.39.q_rows, bf16[2,4,256,128]{3,2,1,0:T(8,128)(2,1)S(1)} %get-tuple-element.40.g_rows, bf16[128,256]{1,0:T(8,128)(2,1)S(1)} %get-tuple-element.48.low_ref.near_low_ref, ...), custom_call_target="tpu_custom_call" | custom-call | flops 300000000 | tf_op jit(solution)/shard_map/near_kernel/pallas_call | solution.py:389
  48.1 3.5 %far_kernel.1 = (bf16[1,128,2048]{2,1,0:T(8,128)(2,1)}, bf16[128,256]{1,0:T(8,128)(2,1)S(1)}, bf16[128,256]{1,0:T(8,128)(2,1)S(1)}) custom-call(s32[1]{0:T(128)} %bitcast.idx_ref, bf16[2,4,256,128]{3,2,1,0:T(8,128)(2,1)S(1)} %get-tuple-element.39.q_rows, bf16[2,4,256,128]{3,2,1,0:T(8,128)(2,1)S(1)} %get-tuple-element.40.g_rows, ...), custom_call_target="tpu_custom_call" | custom-call | flops 300000000 | tf_op jit(solution)/shard_map/far_kernel/pallas_call | solution.py:396
  52.9 5.4 %collective-permute-start.6 = (bf16[128,256]{1,0:T(8,128)(2,1)S(1)}, bf16[128,256]{1,0:T(8,128)(2,1)S(1)}, u32[]{:S(2)}, u32[]{:S(2)}) collective-permute-start(bf16[128,256]{1,0:T(8,128)(2,1)S(1)} %get-tuple-element.58.high_ref), channel_id=1, source_target_pairs={{0,16},{8,24},{16,32},{24,40},{32,48},{40,56},{48,64},{56,72},{64,... | collective-permute-start | bytes 196616 | tf_op jit(solution)/shard_map/ppermute | solution.py:328
  59.8 4.3 %all-to-all-start.1 = ((bf16[4,8,128,128]{3,2,1,0:T(8,128)(2,1)}), bf16[4,8,128,128]{3,2,1,0:T(8,128)(2,1)S(1)}, u32[]{:S(2)}, u32[]{:S(2)}) async-start(bf16[4,8,128,128]{3,2,1,0:T(8,128)(2,1)} %repeat_kernel.1), calls=%async_computation.1 | async-start | bytes 2097152 | tf_op jit(solution)/shard_map/all_to_all | solution.py:408
  64.1 3.6 %collective-permute-start.8 = (bf16[192,256]{1,0:T(8,128)(2,1)S(1)}, bf16[192,256]{1,0:T(8,128)(2,1)S(1)}, u32[]{:S(2)}, u32[]{:S(2)}) collective-permute-start(bf16[192,256]{1,0:T(8,128)(2,1)S(1)} %get-tuple-element.62.right_ref), channel_id=1, source_target_pairs={{0,8},{8,16},{16,24},{24,32},{32,40},{40,48},{48,56},{56,64},{64,7... | collective-permute-start | bytes 294920 | tf_op jit(solution)/shard_map/ppermute | solution.py:328
  67.7 1.3 %collective-permute-start.7 = (bf16[128,256]{1,0:T(8,128)(2,1)S(1)}, bf16[128,256]{1,0:T(8,128)(2,1)S(1)}, u32[]{:S(2)}, u32[]{:S(2)}) collective-permute-start(bf16[128,256]{1,0:T(8,128)(2,1)S(1)} %get-tuple-element.63), channel_id=1, source_target_pairs={{8,0},{16,8},{24,16},{32,24},{40,32},{48,40},{56,48},{64,56},{72,6... | collective-permute-start | bytes 196616 | tf_op jit(solution)/shard_map/ppermute | solution.py:328
  69.0 4.9 %collective-permute-done.7.low1_ref = bf16[128,256]{1,0:T(8,128)(2,1)S(1)} collective-permute-done((bf16[128,256]{1,0:T(8,128)(2,1)S(1)}, bf16[128,256]{1,0:T(8,128)(2,1)S(1)}, u32[]{:S(2)}, u32[]{:S(2)}) %collective-permute-start.7) | collective-permute-done | bytes 65568 | tf_op jit(solution)/shard_map/ppermute | solution.py:328
  73.9 2.4 %all-to-all-done.1.mine_ref = bf16[4,8,128,128]{3,2,1,0:T(8,128)(2,1)S(1)} async-done(((bf16[4,8,128,128]{3,2,1,0:T(8,128)(2,1)}), bf16[4,8,128,128]{3,2,1,0:T(8,128)(2,1)S(1)}, u32[]{:S(2)}, u32[]{:S(2)}) %all-to-all-start.1) | async-done | bytes 1048608 | tf_op jit(solution)/shard_map/all_to_all | solution.py:408
  76.3 1.9 %collective-permute-start.9 = (bf16[4,8,128,128]{3,2,1,0:T(8,128)(2,1)S(1)}, bf16[4,8,128,128]{3,2,1,0:T(8,128)(2,1)S(1)}, u32[]{:S(2)}, u32[]{:S(2)}) collective-permute-start(bf16[4,8,128,128]{3,2,1,0:T(8,128)(2,1)S(1)} %all-to-all-done.1.mine_ref), channel_id=1, source_target_pairs={{0,1},{1,0},{2,3},{3,2},{4,5},{5,4},{6,7},{7,6},{8,9},{9,8},{10,11... | collective-permute-start | bytes 3145736 | tf_op jit(solution)/shard_map/ppermute | solution.py:421
  78.2 21.0 %all_to_all.20.dv_ref = bf16[8,192,128]{2,1,0:T(8,128)(2,1)S(1)} all-to-all(bf16[8,192,128]{2,1,0:T(8,128)(2,1)S(1)} %get-tuple-element.68), channel_id=1, replica_groups=mesh['dp'=4,'ctx_0'=2,'ctx_1'=16,'tp_x'=4,'core'=2] {'dp','ctx_0'}, dimensions={0} | all-to-all | bytes 786432 | tf_op jit(solution)/shard_map/all_to_all | solution.py:422
  99.2 1.5 %weight_kernel.1 = bf16[16,64,128]{2,1,0:T(8,128)(2,1)} custom-call(s32[1]{0:T(128)} %bitcast.6.core_ref, bf16[4,8,128,128]{3,2,1,0:T(8,128)(2,1)S(1)} %all-to-all-done.1.mine_ref, bf16[4,8,128,128]{3,2,1,0:T(8,128)(2,1)S(1)} %collective-permute-done.9.theirs_ref, bf16[8,192,128]{2,1,0:T(8,128)(2,1)S(1)} %all_to_all.20.dv_ref), custom_call_target="tpu_custom_call" | custom-call | flops 1000000000 | tf_op jit(solution)/shard_map/weight_kernel/pallas_call | solution.py:424
  100.8 9.2 %all-to-all-start.3 = ((bf16[16,64,128]{2,1,0:T(8,128)(2,1)}), bf16[16,64,128]{2,1,0:T(8,128)(2,1)S(1)}, u32[]{:S(2)}, u32[]{:S(2)}) async-start(bf16[16,64,128]{2,1,0:T(8,128)(2,1)} %weight_kernel.1), calls=%async_computation.3 | async-start | bytes 524288 | tf_op jit(solution)/shard_map/all_to_all | solution.py:432
  110.0 3.5 %collective-permute-start.10 = (bf16[64,256]{1,0:T(8,128)(2,1)S(1)}, bf16[64,256]{1,0:T(8,128)(2,1)S(1)}, u32[]{:S(2)}, u32[]{:S(2)}) collective-permute-start(bf16[64,256]{1,0:T(8,128)(2,1)S(1)} %get-tuple-element.70), channel_id=1, source_target_pairs={{232,104},{240,112},{248,120},{0,128},{8,136},{16,144},{233,105},{... | collective-permute-start | bytes 98312 | tf_op jit(solution)/shard_map/ppermute | solution.py:334
  113.5 1.6 %collective-permute-done.10.cross_ref = bf16[64,256]{1,0:T(8,128)(2,1)S(1)} collective-permute-done((bf16[64,256]{1,0:T(8,128)(2,1)S(1)}, bf16[64,256]{1,0:T(8,128)(2,1)S(1)}, u32[]{:S(2)}, u32[]{:S(2)}) %collective-permute-start.10) | collective-permute-done | bytes 32800 | tf_op jit(solution)/shard_map/ppermute | solution.py:334
  115.7 12.6 %all-to-all-done.3 = bf16[16,64,128]{2,1,0:T(8,128)(2,1)S(1)} async-done(((bf16[16,64,128]{2,1,0:T(8,128)(2,1)}), bf16[16,64,128]{2,1,0:T(8,128)(2,1)S(1)}, u32[]{:S(2)}, u32[]{:S(2)}) %all-to-all-start.3) | async-done | bytes 262176 | tf_op jit(solution)/shard_map/all_to_all | solution.py:432
  (32 shorter events, 6.1 us)
Async XLA Ops:
  0.6 2.9 %copy-start = (bf16[1,128,8192]{2,1,0:T(8,128)(2,1)S(1)}, bf16[1,128,8192]{2,1,0:T(8,128)(2,1)}, u32[]{:S(2)}) copy-start(bf16[1,128,8192]{2,1,0:T(8,128)(2,1)} %x_ref.1) | copy-start | bytes 6291460
  2.2 25.6 %collective-permute-start = (bf16[64,256]{1,0:T(8,128)(2,1)}, bf16[64,256]{1,0:T(8,128)(2,1)S(1)}, u32[]{:S(2)}, u32[]{:S(2)}) collective-permute-start(bf16[64,256]{1,0:T(8,128)(2,1)} %get-tuple-element.43), channel_id=1, source_target_pairs={{104,232},{112,240},{120,248},{128,0},{136,8},{144,16},{105,233},{... | collective-permute-start | bytes 98312 | tf_op jit(solution)/shard_map/ppermute | solution.py:334
  3.6 21.9 %copy-start.1 = (bf16[1,128,2048]{2,1,0:T(8,128)(2,1)S(1)}, bf16[1,128,2048]{2,1,0:T(8,128)(2,1)}, u32[]{:S(2)}) copy-start(bf16[1,128,2048]{2,1,0:T(8,128)(2,1)} %param.9) | copy-start | bytes 1572868
  3.6 21.9 %copy-start.2 = (bf16[1,128,2048]{2,1,0:T(8,128)(2,1)S(1)}, bf16[1,128,2048]{2,1,0:T(8,128)(2,1)}, u32[]{:S(2)}) copy-start(bf16[1,128,2048]{2,1,0:T(8,128)(2,1)} %param.13) | copy-start | bytes 1572868
  3.6 21.8 %copy-start.4 = (s32[1,4096]{1,0:T(1,128)S(1)}, s32[1,4096]{1,0:T(1,128)}, u32[]{:S(2)}) copy-start(s32[1,4096]{1,0:T(1,128)} %doc_ref.1) | copy-start | bytes 49156
  3.6 21.8 %copy-start.5 = (f32[1,16,128]{2,1,0:T(8,128)S(1)}, f32[1,16,128]{2,1,0:T(8,128)}, u32[]{:S(2)}) copy-start(f32[1,16,128]{2,1,0:T(8,128)} %param.14) | copy-start | bytes 24580
  4.5 54.2 %all-to-all-start = ((bf16[8,128,128]{2,1,0:T(8,128)(2,1)}), bf16[8,128,128]{2,1,0:T(8,128)(2,1)S(1)}, u32[]{:S(2)}, u32[]{:S(2)}) async-start(bf16[8,128,128]{2,1,0:T(8,128)(2,1)} %chunk_kernel.1), calls=%async_computation | async-start | bytes 524288 | tf_op jit(solution)/shard_map/all_to_all | solution.py:378
  25.4 1.0 copy-start.3
  26.5 1.3 %copy-start.6 = (bf16[128,256]{1,0:T(8,128)(2,1)S(1)}, bf16[128,256]{1,0:T(8,128)(2,1)}, u32[]{:S(2)}) copy-start(bf16[128,256]{1,0:T(8,128)(2,1)} %get-tuple-element.42.kv_ref) | copy-start | bytes 196612
  27.8 10.7 %collective-permute-start.2 = (bf16[192,256]{1,0:T(8,128)(2,1)S(1)}, bf16[192,256]{1,0:T(8,128)(2,1)S(1)}, u32[]{:S(2)}, u32[]{:S(2)}) collective-permute-start(bf16[192,256]{1,0:T(8,128)(2,1)S(1)} %get-tuple-element.47), channel_id=1, source_target_pairs={{0,120},{8,0},{16,8},{24,16},{32,24},{40,32},{48,40},{56,48},{64,5... | collective-permute-start | bytes 294920 | tf_op jit(solution)/shard_map/ppermute | solution.py:328
  35.4 3.2 %collective-permute-start.1 = (bf16[128,256]{1,0:T(8,128)(2,1)S(1)}, bf16[128,256]{1,0:T(8,128)(2,1)S(1)}, u32[]{:S(2)}, u32[]{:S(2)}) collective-permute-start(bf16[128,256]{1,0:T(8,128)(2,1)S(1)} %get-tuple-element.46), channel_id=1, source_target_pairs={{0,8},{8,16},{16,24},{24,32},{32,40},{40,48},{48,56},{56,64},{64,7... | collective-permute-start | bytes 196616 | tf_op jit(solution)/shard_map/ppermute | solution.py:328
  38.6 9.5 %collective-permute-start.3 = (bf16[128,256]{1,0:T(8,128)(2,1)S(1)}, bf16[128,256]{1,0:T(8,128)(2,1)S(1)}, u32[]{:S(2)}, u32[]{:S(2)}) collective-permute-start(bf16[128,256]{1,0:T(8,128)(2,1)S(1)} %get-tuple-element.49), channel_id=1, source_target_pairs={{0,16},{8,24},{16,32},{24,40},{32,48},{40,56},{48,64},{56,72},{64,... | collective-permute-start | bytes 196616 | tf_op jit(solution)/shard_map/ppermute | solution.py:328
  39.9 8.2 %collective-permute-start.4 = (bf16[128,256]{1,0:T(8,128)(2,1)S(1)}, bf16[128,256]{1,0:T(8,128)(2,1)S(1)}, u32[]{:S(2)}, u32[]{:S(2)}) collective-permute-start(bf16[128,256]{1,0:T(8,128)(2,1)S(1)} %get-tuple-element.50), channel_id=1, source_target_pairs={{0,112},{8,120},{16,0},{24,8},{32,16},{40,24},{48,32},{56,40},{64,... | collective-permute-start | bytes 196616 | tf_op jit(solution)/shard_map/ppermute | solution.py:328
  51.6 7.0 %collective-permute-start.5 = (bf16[128,256]{1,0:T(8,128)(2,1)S(1)}, bf16[128,256]{1,0:T(8,128)(2,1)S(1)}, u32[]{:S(2)}, u32[]{:S(2)}) collective-permute-start(bf16[128,256]{1,0:T(8,128)(2,1)S(1)} %get-tuple-element.59), channel_id=1, source_target_pairs={{16,0},{24,8},{32,16},{40,24},{48,32},{56,40},{64,48},{72,56},{80,... | collective-permute-start | bytes 196616 | tf_op jit(solution)/shard_map/ppermute | solution.py:328
  52.9 11.2 %collective-permute-start.6 = (bf16[128,256]{1,0:T(8,128)(2,1)S(1)}, bf16[128,256]{1,0:T(8,128)(2,1)S(1)}, u32[]{:S(2)}, u32[]{:S(2)}) collective-permute-start(bf16[128,256]{1,0:T(8,128)(2,1)S(1)} %get-tuple-element.58.high_ref), channel_id=1, source_target_pairs={{0,16},{8,24},{16,32},{24,40},{32,48},{40,56},{48,64},{56,72},{64,... | collective-permute-start | bytes 196616 | tf_op jit(solution)/shard_map/ppermute | solution.py:328
  59.8 16.6 %all-to-all-start.1 = ((bf16[4,8,128,128]{3,2,1,0:T(8,128)(2,1)}), bf16[4,8,128,128]{3,2,1,0:T(8,128)(2,1)S(1)}, u32[]{:S(2)}, u32[]{:S(2)}) async-start(bf16[4,8,128,128]{3,2,1,0:T(8,128)(2,1)} %repeat_kernel.1), calls=%async_computation.1 | async-start | bytes 2097152 | tf_op jit(solution)/shard_map/all_to_all | solution.py:408
  64.1 9.7 %collective-permute-start.8 = (bf16[192,256]{1,0:T(8,128)(2,1)S(1)}, bf16[192,256]{1,0:T(8,128)(2,1)S(1)}, u32[]{:S(2)}, u32[]{:S(2)}) collective-permute-start(bf16[192,256]{1,0:T(8,128)(2,1)S(1)} %get-tuple-element.62.right_ref), channel_id=1, source_target_pairs={{0,8},{8,16},{16,24},{24,32},{32,40},{40,48},{48,56},{56,64},{64,7... | collective-permute-start | bytes 294920 | tf_op jit(solution)/shard_map/ppermute | solution.py:328
  67.7 6.2 %collective-permute-start.7 = (bf16[128,256]{1,0:T(8,128)(2,1)S(1)}, bf16[128,256]{1,0:T(8,128)(2,1)S(1)}, u32[]{:S(2)}, u32[]{:S(2)}) collective-permute-start(bf16[128,256]{1,0:T(8,128)(2,1)S(1)} %get-tuple-element.63), channel_id=1, source_target_pairs={{8,0},{16,8},{24,16},{32,24},{40,32},{48,40},{56,48},{64,56},{72,6... | collective-permute-start | bytes 196616 | tf_op jit(solution)/shard_map/ppermute | solution.py:328
  76.3 22.9 %collective-permute-start.9 = (bf16[4,8,128,128]{3,2,1,0:T(8,128)(2,1)S(1)}, bf16[4,8,128,128]{3,2,1,0:T(8,128)(2,1)S(1)}, u32[]{:S(2)}, u32[]{:S(2)}) collective-permute-start(bf16[4,8,128,128]{3,2,1,0:T(8,128)(2,1)S(1)} %all-to-all-done.1.mine_ref), channel_id=1, source_target_pairs={{0,1},{1,0},{2,3},{3,2},{4,5},{5,4},{6,7},{7,6},{8,9},{9,8},{10,11... | collective-permute-start | bytes 3145736 | tf_op jit(solution)/shard_map/ppermute | solution.py:421
  100.8 27.6 %all-to-all-start.3 = ((bf16[16,64,128]{2,1,0:T(8,128)(2,1)}), bf16[16,64,128]{2,1,0:T(8,128)(2,1)S(1)}, u32[]{:S(2)}, u32[]{:S(2)}) async-start(bf16[16,64,128]{2,1,0:T(8,128)(2,1)} %weight_kernel.1), calls=%async_computation.3 | async-start | bytes 524288 | tf_op jit(solution)/shard_map/all_to_all | solution.py:432
  110.0 5.1 %collective-permute-start.10 = (bf16[64,256]{1,0:T(8,128)(2,1)S(1)}, bf16[64,256]{1,0:T(8,128)(2,1)S(1)}, u32[]{:S(2)}, u32[]{:S(2)}) collective-permute-start(bf16[64,256]{1,0:T(8,128)(2,1)S(1)} %get-tuple-element.70), channel_id=1, source_target_pairs={{232,104},{240,112},{248,120},{0,128},{8,136},{16,144},{233,105},{... | collective-permute-start | bytes 98312 | tf_op jit(solution)/shard_map/ppermute | solution.py:334

commit v5 on v4

--- a/solution.py
+++ b/solution.py
@@ -20,7 +20,7 @@
 SMEM = pl.BlockSpec(memory_space=pltpu.SMEM)
 VMEM = pl.BlockSpec(memory_space=pltpu.VMEM)
 ANY = pl.BlockSpec(memory_space=pl.ANY)
-COST = {"prepare": 2, "widen": 0.1, "near": 0.3, "far": 0.3, "turn": 10, "close": 5, "finish": 0.5}
+COST = {"prepare": 4, "first": 4, "widen": 0.1, "repeat": 4, "near": 0.3, "far": 0.3, "turn": 10, "close": 5, "finish": 0.5}
 
 
 def call(kernel, outs, in_specs, us, scratch=(), mib=8):
@@ -291,13 +291,14 @@
         copy.wait()
 
 
-def repeat_kernel(x_ref, out_ref):
+def repeat_kernel(mine_ref, theirs_ref, out_ref):
     for i in range(out_ref.shape[0]):
-        out_ref[i] = x_ref[...]
-
-
-def weight_kernel(scale, core_ref, mine_ref, theirs_ref, dv_ref, out_ref):
-    pieces, parts, tokens, width = mine_ref.shape
+        out_ref[i, 0] = mine_ref[...]
+        out_ref[i, 1] = theirs_ref[...]
+
+
+def weight_kernel(scale, core_ref, x_ref, dv_ref, out_ref):
+    pieces, _, parts, tokens, width = x_ref.shape
     each = out_ref.shape[0] // (2 * pieces)
     rows = []
     for i in range(parts):
@@ -310,8 +311,8 @@
         rows += [lower.astype(BF), upper.astype(BF)]
     dv = jnp.concatenate(rows, axis=0).T
     for i in range(pieces):
-        for x_ref, core in ((mine_ref, core_ref[0]), (theirs_ref, 1 - core_ref[0])):
-            x = x_ref[i].reshape(parts * tokens, width)
+        for j, core in enumerate((core_ref[0], 1 - core_ref[0])):
+            x = x_ref[i, j].reshape(parts * tokens, width)
             flat = jnp.dot(dv, x, preferred_element_type=F32) * scale
             flat = flat.T.astype(BF).reshape(each, width // each, HD)
             out_ref[pl.ds((2 * i + core) * each, each)] = flat
@@ -360,14 +361,6 @@
     )(place, key_heads, value_heads)
     kv, part_of = lax.optimization_barrier((kv, lax.axis_index(TP).astype(jnp.int32).reshape(1)))
     cross = swap(cross, False)
-    q_rows, g_rows, lse_rows, delta_rows, live = call(
-        at(prepare_kernel, count),
-        [head_rows, head_rows, row_terms, row_terms, shape((2, 2, C, 128), F32)],
-        [SMEM] + [VMEM] * 5,
-        COST["prepare"],
-        mib=12,
-    )(place, queries[0], out_grad[0], attn_out[0], log_sums[0], doc_ids)
-    cross, live = lax.optimization_barrier((cross, live))
     (chunks,) = call(
         chunk_kernel,
         [shape((groups, rows, piece), BF)],
@@ -376,7 +369,7 @@
         [pltpu.SemaphoreType.DMA((groups,))],
     )(part_of, layer_input)
     mine = lax.all_to_all(chunks, ROWS, 0, 0, tiled=True)
-    to_left, to_right = call(at(first_kernel, count), [pair, three], [SMEM] + [VMEM] * 2, COST["widen"])(
+    to_left, to_right = call(at(first_kernel, count), [pair, three], [SMEM] + [VMEM] * 2, COST["first"])(
         place, kv, cross
     )
     left = shift(to_left, 1, 1)
@@ -384,8 +377,22 @@
     low, high, send_low, send_high = call(
         at(widen_kernel, count), [pair] * 4, [SMEM] + [VMEM] * 4, COST["widen"]
     )(place, kv, cross, left, right)
+    _, mine = lax.optimization_barrier((send_low, mine))
     left2 = shift(send_low, 2, 1)
     right2 = shift(send_high, -2, 0)
+    theirs = lax.ppermute(mine, "core", [(0, 1), (1, 0)])
+    (repeated,) = call(
+        repeat_kernel, [shape((pieces // 2, 2, groups, rows, piece), BF)], [VMEM] * 2, COST["repeat"]
+    )(mine, theirs)
+    tokens = lax.all_to_all(repeated, "tp_x", 0, 0, tiled=True)
+    docs, repeated = lax.optimization_barrier((doc_ids, repeated))
+    q_rows, g_rows, lse_rows, delta_rows, live = call(
+        at(prepare_kernel, count),
+        [head_rows, head_rows, row_terms, row_terms, shape((2, 2, C, 128), F32)],
+        [SMEM] + [VMEM] * 5,
+        COST["prepare"],
+        mib=12,
+    )(place, queries[0], out_grad[0], attn_out[0], log_sums[0], docs)
     near_query, near_kv = call(
         near_kernel,
         [shape((rows, width), F32), shape((2, 128, 2 * HD), F32)],
@@ -403,9 +410,6 @@
     )(place, q_rows, g_rows, low, right, left2, right2, near_query, lse_rows, delta_rows, live)
     low2 = shift(far_low, -2, 1)
     high2 = shift(far_high, 2, 0)
-    low2, mine = lax.optimization_barrier((low2, mine))
-    (repeated,) = call(repeat_kernel, [shape((pieces // 2, groups, rows, piece), BF)], [VMEM], 1)(mine)
-    tokens = lax.all_to_all(repeated, "tp_x", 0, 0, tiled=True)
     to_left, to_right = call(
         at(turn_kernel, count), [pair, three], [SMEM] + [VMEM] * 4, COST["turn"]
     )(place, near_kv, far_high, low2, high2)
@@ -418,16 +422,15 @@
         COST["close"],
     )(place, near_kv, far_high, low2, high2, to_right, low1, high1)
     spread, tokens = lax.optimization_barrier((spread, tokens))
-    tokens_2 = lax.ppermute(tokens, "core", [(0, 1), (1, 0)])
     everyone = lax.all_to_all(spread, ROWS, 0, 0, tiled=True)
     weight_scale = (lax.axis_size("dp") * doc_ids.shape[1]) ** (-0.5)
     (part,) = call(
         at(weight_kernel, weight_scale),
         [shape((steps, piece * pieces // steps, HD), BF)],
-        [SMEM] + [VMEM] * 3,
+        [SMEM] + [VMEM] * 2,
         1,
         mib=12,
-    )(lax.axis_index("core").astype(jnp.int32).reshape(1), tokens, tokens_2, everyone)
+    )(lax.axis_index("core").astype(jnp.int32).reshape(1), tokens, everyone)
     part, cross = lax.optimization_barrier((part, cross))
     parts = lax.all_to_all(part, "ctx_1", 0, 0, tiled=True)
     cross = swap(cross, True)

time: 130 us -> 125 us (0.962)
  the two profiles are of different devices: /device:TPU:8 before, /device:TPU:10 now
where the time goes in v5:
time: 125 us; the launch traced here: 124 us
  starting transfers between devices  70 us (56%)
  waiting for transfers between devices  22.2 us (18%)
  blocking collectives  15.2 us (12%)
  Pallas kernels  13.2 us (11%)
  local copies, waits for them, and re-layouts  2.4 us (2%)
    ppermute x8, starting transfers between devices, shift(): return lax.ppermute(value, CTX, pairs)  41.5 us
    all_to_all x1, blocking collectives, body(): everyone = lax.all_to_all(spread, ROWS, 0, 0, tiled=True)  15.2 us
    all_to_all x1, waiting for transfers between devices, body(): parts = lax.all_to_all(part, 'ctx_1', 0, 0, tiled=True)  10.7 us
    ppermute x8, waiting for transfers between devices, shift(): return lax.ppermute(value, CTX, pairs)  9.82 us
    all_to_all x1, starting transfers between devices, body(): mine = lax.all_to_all(chunks, ROWS, 0, 0, tiled=True)  8.62 us
    all_to_all x1, starting transfers between devices, body(): parts = lax.all_to_all(part, 'ctx_1', 0, 0, tiled=True)  8.15 us
    all_to_all x1, starting transfers between devices, body(): tokens = lax.all_to_all(repeated, 'tp_x', 0, 0, tiled=True)  4.97 us
    ppermute x2, starting transfers between devices, swap(): lax.ppermute(value, CTX, [(b, a) for a, b in pairs] if back else pairs)  4.89 us
  transfers between devices with their start and end apart: 14, of which 6 were waited for; matrix products, arithmetic and copies ran while one was open for 0% of the time, Pallas kernels for 8%

profile of v5, /device:TPU:10, one launch (start us, length us, event | category | flops | bytes accessed | tf_op | source)
XLA Modules:
  0.0 124.5 jit_solution(801986622945557819)
XLA Ops:
  0.6 1.6 %pack_kernel.1 = (bf16[128,256]{1,0:T(8,128)(2,1)}, bf16[64,256]{1,0:T(8,128)(2,1)}) custom-call(s32[1]{0:T(128)} %bitcast.idx_ref, bf16[1,128,128]{2,1,0:T(8,128)(2,1)} %k_ref.1, bf16[1,128,128]{2,1,0:T(8,128)(2,1)} %v_ref.1), custom_call_target="tpu_custom_call" | custom-call | flops 1000000000 | tf_op jit(solution)/shard_map/pack_kernel/pallas_call | solution.py:354
  4.4 8.6 %all-to-all-start = ((bf16[8,128,128]{2,1,0:T(8,128)(2,1)}), bf16[8,128,128]{2,1,0:T(8,128)(2,1)S(1)}, u32[]{:S(2)}, u32[]{:S(2)}) async-start(bf16[8,128,128]{2,1,0:T(8,128)(2,1)} %chunk_kernel.1), calls=%async_computation | async-start | bytes 524288 | tf_op jit(solution)/shard_map/all_to_all | solution.py:371
  13.1 19.8 %collective-permute-start.2 = (bf16[192,256]{1,0:T(8,128)(2,1)S(1)}, bf16[192,256]{1,0:T(8,128)(2,1)S(1)}, u32[]{:S(2)}, u32[]{:S(2)}) collective-permute-start(bf16[192,256]{1,0:T(8,128)(2,1)S(1)} %get-tuple-element.41), channel_id=1, source_target_pairs={{0,120},{8,0},{16,8},{24,16},{32,24},{40,32},{48,40},{56,48},{64,5... | collective-permute-start | bytes 294920 | tf_op jit(solution)/shard_map/ppermute | solution.py:329
  32.9 1.3 %collective-permute-start.1 = (bf16[128,256]{1,0:T(8,128)(2,1)S(1)}, bf16[128,256]{1,0:T(8,128)(2,1)S(1)}, u32[]{:S(2)}, u32[]{:S(2)}) collective-permute-start(bf16[128,256]{1,0:T(8,128)(2,1)S(1)} %get-tuple-element.40), channel_id=1, source_target_pairs={{0,8},{8,16},{16,24},{24,32},{32,40},{40,48},{48,56},{56,64},{64,7... | collective-permute-start | bytes 196616 | tf_op jit(solution)/shard_map/ppermute | solution.py:329
  34.2 1.9 %collective-permute-done.1.left_ref = bf16[128,256]{1,0:T(8,128)(2,1)S(1)} collective-permute-done((bf16[128,256]{1,0:T(8,128)(2,1)S(1)}, bf16[128,256]{1,0:T(8,128)(2,1)S(1)}, u32[]{:S(2)}, u32[]{:S(2)}) %collective-permute-start.1) | collective-permute-done | bytes 65568 | tf_op jit(solution)/shard_map/ppermute | solution.py:329
  36.8 1.9 %collective-permute-start.3 = (bf16[8,128,128]{2,1,0:T(8,128)(2,1)S(1)}, bf16[8,128,128]{2,1,0:T(8,128)(2,1)S(1)}, u32[]{:S(2)}, u32[]{:S(2)}) collective-permute-start(bf16[8,128,128]{2,1,0:T(8,128)(2,1)S(1)} %all-to-all-done.mine_ref), channel_id=1, source_target_pairs={{0,1},{1,0},{2,3},{3,2},{4,5},{5,4},{6,7},{7,6},{8,9},{9,8},{10,11... | collective-permute-start | bytes 786440 | tf_op jit(solution)/shard_map/ppermute | solution.py:383
  38.7 1.3 %collective-permute-start.4 = (bf16[128,256]{1,0:T(8,128)(2,1)}, bf16[128,256]{1,0:T(8,128)(2,1)S(1)}, u32[]{:S(2)}, u32[]{:S(2)}) collective-permute-start(bf16[128,256]{1,0:T(8,128)(2,1)} %get-tuple-element.42), channel_id=1, source_target_pairs={{0,16},{8,24},{16,32},{24,40},{32,48},{40,56},{48,64},{56,72},{64,... | collective-permute-start | bytes 196616 | tf_op jit(solution)/shard_map/ppermute | solution.py:329
  40.0 6.2 %collective-permute-start.5 = (bf16[128,256]{1,0:T(8,128)(2,1)}, bf16[128,256]{1,0:T(8,128)(2,1)S(1)}, u32[]{:S(2)}, u32[]{:S(2)}) collective-permute-start(bf16[128,256]{1,0:T(8,128)(2,1)} %get-tuple-element.49), channel_id=1, source_target_pairs={{0,112},{8,120},{16,0},{24,8},{32,16},{40,24},{48,32},{56,40},{64,... | collective-permute-start | bytes 196616 | tf_op jit(solution)/shard_map/ppermute | solution.py:329
  46.4 1.3 %copy-done = bf16[4,2,8,128,128]{4,3,2,1,0:T(8,128)(2,1)} copy-done((bf16[4,2,8,128,128]{4,3,2,1,0:T(8,128)(2,1)}, bf16[4,2,8,128,128]{4,3,2,1,0:T(8,128)(2,1)S(1)}, u32[]{:S(2)}) %copy-start) | copy-done | bytes 2097176
  47.8 5.0 %all-to-all-start.1 = ((bf16[4,2,8,128,128]{4,3,2,1,0:T(8,128)(2,1)}), bf16[4,2,8,128,128]{4,3,2,1,0:T(8,128)(2,1)S(1)}, u32[]{:S(2)}, u32[]{:S(2)}) async-start(bf16[4,2,8,128,128]{4,3,2,1,0:T(8,128)(2,1)} %copy-done), calls=%async_computation.1 | async-start | bytes 4194304 | tf_op jit(solution)/shard_map/all_to_all | solution.py:387
  55.1 2.8 %near_kernel.1 = (f32[128,2048]{1,0:T(8,128)S(1)}, f32[2,128,256]{2,1,0:T(8,128)S(1)}) custom-call(s32[1]{0:T(128)} %bitcast.idx_ref, bf16[2,4,256,128]{3,2,1,0:T(8,128)(2,1)S(1)} %get-tuple-element.46.q_rows, bf16[2,4,256,128]{3,2,1,0:T(8,128)(2,1)S(1)} %get-tuple-element.47.g_rows, bf16[128,256]{1,0:T(8,128)(2,1)S(1)} %get-tuple-element.48.low_ref.near_low_ref, ...), custom_call_target="tpu_custom_call" | custom-call | flops 300000000 | tf_op jit(solution)/shard_map/near_kernel/pallas_call | solution.py:396
  57.9 3.5 %far_kernel.1 = (bf16[1,128,2048]{2,1,0:T(8,128)(2,1)}, bf16[128,256]{1,0:T(8,128)(2,1)S(1)}, bf16[128,256]{1,0:T(8,128)(2,1)S(1)}) custom-call(s32[1]{0:T(128)} %bitcast.idx_ref, bf16[2,4,256,128]{3,2,1,0:T(8,128)(2,1)S(1)} %get-tuple-element.46.q_rows, bf16[2,4,256,128]{3,2,1,0:T(8,128)(2,1)S(1)} %get-tuple-element.47.g_rows, ...), custom_call_target="tpu_custom_call" | custom-call | flops 300000000 | tf_op jit(solution)/shard_map/far_kernel/pallas_call | solution.py:403
  62.7 5.4 %collective-permute-start.7 = (bf16[128,256]{1,0:T(8,128)(2,1)S(1)}, bf16[128,256]{1,0:T(8,128)(2,1)S(1)}, u32[]{:S(2)}, u32[]{:S(2)}) collective-permute-start(bf16[128,256]{1,0:T(8,128)(2,1)S(1)} %get-tuple-element.57.high_ref), channel_id=1, source_target_pairs={{0,16},{8,24},{16,32},{24,40},{32,48},{40,56},{48,64},{56,72},{64,... | collective-permute-start | bytes 196616 | tf_op jit(solution)/shard_map/ppermute | solution.py:329
  68.1 1.6 %collective-permute-done.6.low2_ref = bf16[128,256]{1,0:T(8,128)(2,1)S(1)} collective-permute-done((bf16[128,256]{1,0:T(8,128)(2,1)S(1)}, bf16[128,256]{1,0:T(8,128)(2,1)S(1)}, u32[]{:S(2)}, u32[]{:S(2)}) %collective-permute-start.6) | collective-permute-done | bytes 65568 | tf_op jit(solution)/shard_map/ppermute | solution.py:329
  69.7 1.4 %collective-permute-done.7.high2_ref = bf16[128,256]{1,0:T(8,128)(2,1)S(1)} collective-permute-done((bf16[128,256]{1,0:T(8,128)(2,1)S(1)}, bf16[128,256]{1,0:T(8,128)(2,1)S(1)}, u32[]{:S(2)}, u32[]{:S(2)}) %collective-permute-start.7) | collective-permute-done | bytes 65568 | tf_op jit(solution)/shard_map/ppermute | solution.py:329
  71.2 4.9 %collective-permute-start.9 = (bf16[192,256]{1,0:T(8,128)(2,1)S(1)}, bf16[192,256]{1,0:T(8,128)(2,1)S(1)}, u32[]{:S(2)}, u32[]{:S(2)}) collective-permute-start(bf16[192,256]{1,0:T(8,128)(2,1)S(1)} %get-tuple-element.59.right_ref), channel_id=1, source_target_pairs={{0,8},{8,16},{16,24},{24,32},{32,40},{40,48},{48,56},{56,64},{64,7... | collective-permute-start | bytes 294920 | tf_op jit(solution)/shard_map/ppermute | solution.py:329
  76.2 1.3 %collective-permute-start.8 = (bf16[128,256]{1,0:T(8,128)(2,1)S(1)}, bf16[128,256]{1,0:T(8,128)(2,1)S(1)}, u32[]{:S(2)}, u32[]{:S(2)}) collective-permute-start(bf16[128,256]{1,0:T(8,128)(2,1)S(1)} %get-tuple-element.60), channel_id=1, source_target_pairs={{8,0},{16,8},{24,16},{32,24},{40,32},{48,40},{56,48},{64,56},{72,6... | collective-permute-start | bytes 196616 | tf_op jit(solution)/shard_map/ppermute | solution.py:329
  77.5 4.9 %collective-permute-done.8.low1_ref = bf16[128,256]{1,0:T(8,128)(2,1)S(1)} collective-permute-done((bf16[128,256]{1,0:T(8,128)(2,1)S(1)}, bf16[128,256]{1,0:T(8,128)(2,1)S(1)}, u32[]{:S(2)}, u32[]{:S(2)}) %collective-permute-start.8) | collective-permute-done | bytes 65568 | tf_op jit(solution)/shard_map/ppermute | solution.py:329
  82.4 15.2 %all_to_all.20.dv_ref = bf16[8,192,128]{2,1,0:T(8,128)(2,1)S(1)} all-to-all(bf16[8,192,128]{2,1,0:T(8,128)(2,1)S(1)} %get-tuple-element.64), channel_id=1, replica_groups=mesh['dp'=4,'ctx_0'=2,'ctx_1'=16,'tp_x'=4,'core'=2] {'dp','ctx_0'}, dimensions={0} | all-to-all | bytes 786432 | tf_op jit(solution)/shard_map/all_to_all | solution.py:425
  97.6 1.5 %weight_kernel.1 = bf16[16,64,128]{2,1,0:T(8,128)(2,1)} custom-call(s32[1]{0:T(128)} %bitcast.6.core_ref, bf16[4,2,8,128,128]{4,3,2,1,0:T(8,128)(2,1)S(1)} %all-to-all-done.1.x_ref, bf16[8,192,128]{2,1,0:T(8,128)(2,1)S(1)} %all_to_all.20.dv_ref), custom_call_target="tpu_custom_call" | custom-call | flops 1000000000 | tf_op jit(solution)/shard_map/weight_kernel/pallas_call | solution.py:427
  99.1 8.1 %all-to-all-start.3 = ((bf16[16,64,128]{2,1,0:T(8,128)(2,1)}), bf16[16,64,128]{2,1,0:T(8,128)(2,1)S(1)}, u32[]{:S(2)}, u32[]{:S(2)}) async-start(bf16[16,64,128]{2,1,0:T(8,128)(2,1)} %weight_kernel.1), calls=%async_computation.3 | async-start | bytes 524288 | tf_op jit(solution)/shard_map/all_to_all | solution.py:435
  107.3 3.6 %collective-permute-start.10 = (bf16[64,256]{1,0:T(8,128)(2,1)S(1)}, bf16[64,256]{1,0:T(8,128)(2,1)S(1)}, u32[]{:S(2)}, u32[]{:S(2)}) collective-permute-start(bf16[64,256]{1,0:T(8,128)(2,1)S(1)} %get-tuple-element.66), channel_id=1, source_target_pairs={{232,104},{240,112},{248,120},{0,128},{8,136},{16,144},{233,105},{... | collective-permute-start | bytes 98312 | tf_op jit(solution)/shard_map/ppermute | solution.py:335
  110.9 1.6 %collective-permute-done.10.cross_ref = bf16[64,256]{1,0:T(8,128)(2,1)S(1)} collective-permute-done((bf16[64,256]{1,0:T(8,128)(2,1)S(1)}, bf16[64,256]{1,0:T(8,128)(2,1)S(1)}, u32[]{:S(2)}, u32[]{:S(2)}) %collective-permute-start.10) | collective-permute-done | bytes 32800 | tf_op jit(solution)/shard_map/ppermute | solution.py:335
  113.1 10.7 %all-to-all-done.3 = bf16[16,64,128]{2,1,0:T(8,128)(2,1)S(1)} async-done(((bf16[16,64,128]{2,1,0:T(8,128)(2,1)}), bf16[16,64,128]{2,1,0:T(8,128)(2,1)S(1)}, u32[]{:S(2)}, u32[]{:S(2)}) %all-to-all-start.3) | async-done | bytes 262176 | tf_op jit(solution)/shard_map/all_to_all | solution.py:435
  (34 shorter events, 8.1 us)
Async XLA Ops:
  0.6 2.9 %copy-start.1 = (bf16[1,128,8192]{2,1,0:T(8,128)(2,1)S(1)}, bf16[1,128,8192]{2,1,0:T(8,128)(2,1)}, u32[]{:S(2)}) copy-start(bf16[1,128,8192]{2,1,0:T(8,128)(2,1)} %x_ref.1) | copy-start | bytes 6291460
  2.2 10.8 %collective-permute-start = (bf16[64,256]{1,0:T(8,128)(2,1)}, bf16[64,256]{1,0:T(8,128)(2,1)S(1)}, u32[]{:S(2)}, u32[]{:S(2)}) collective-permute-start(bf16[64,256]{1,0:T(8,128)(2,1)} %get-tuple-element.39), channel_id=1, source_target_pairs={{104,232},{112,240},{120,248},{128,0},{136,8},{144,16},{105,233},{... | collective-permute-start | bytes 98312 | tf_op jit(solution)/shard_map/ppermute | solution.py:335
  3.6 9.5 %copy-start.7 = (bf16[128,256]{1,0:T(8,128)(2,1)S(1)}, bf16[128,256]{1,0:T(8,128)(2,1)}, u32[]{:S(2)}) copy-start(bf16[128,256]{1,0:T(8,128)(2,1)} %get-tuple-element.38.kv_ref) | copy-start | bytes 196612
  4.4 32.3 %all-to-all-start = ((bf16[8,128,128]{2,1,0:T(8,128)(2,1)}), bf16[8,128,128]{2,1,0:T(8,128)(2,1)S(1)}, u32[]{:S(2)}, u32[]{:S(2)}) async-start(bf16[8,128,128]{2,1,0:T(8,128)(2,1)} %chunk_kernel.1), calls=%async_computation | async-start | bytes 524288 | tf_op jit(solution)/shard_map/all_to_all | solution.py:371
  13.1 23.0 %collective-permute-start.2 = (bf16[192,256]{1,0:T(8,128)(2,1)S(1)}, bf16[192,256]{1,0:T(8,128)(2,1)S(1)}, u32[]{:S(2)}, u32[]{:S(2)}) collective-permute-start(bf16[192,256]{1,0:T(8,128)(2,1)S(1)} %get-tuple-element.41), channel_id=1, source_target_pairs={{0,120},{8,0},{16,8},{24,16},{32,24},{40,32},{48,40},{56,48},{64,5... | collective-permute-start | bytes 294920 | tf_op jit(solution)/shard_map/ppermute | solution.py:329
  32.9 3.2 %collective-permute-start.1 = (bf16[128,256]{1,0:T(8,128)(2,1)S(1)}, bf16[128,256]{1,0:T(8,128)(2,1)S(1)}, u32[]{:S(2)}, u32[]{:S(2)}) collective-permute-start(bf16[128,256]{1,0:T(8,128)(2,1)S(1)} %get-tuple-element.40), channel_id=1, source_target_pairs={{0,8},{8,16},{16,24},{24,32},{32,40},{40,48},{48,56},{56,64},{64,7... | collective-permute-start | bytes 196616 | tf_op jit(solution)/shard_map/ppermute | solution.py:329
  36.8 9.4 %collective-permute-start.3 = (bf16[8,128,128]{2,1,0:T(8,128)(2,1)S(1)}, bf16[8,128,128]{2,1,0:T(8,128)(2,1)S(1)}, u32[]{:S(2)}, u32[]{:S(2)}) collective-permute-start(bf16[8,128,128]{2,1,0:T(8,128)(2,1)S(1)} %all-to-all-done.mine_ref), channel_id=1, source_target_pairs={{0,1},{1,0},{2,3},{3,2},{4,5},{5,4},{6,7},{7,6},{8,9},{9,8},{10,11... | collective-permute-start | bytes 786440 | tf_op jit(solution)/shard_map/ppermute | solution.py:383
  38.7 19.2 %collective-permute-start.4 = (bf16[128,256]{1,0:T(8,128)(2,1)}, bf16[128,256]{1,0:T(8,128)(2,1)S(1)}, u32[]{:S(2)}, u32[]{:S(2)}) collective-permute-start(bf16[128,256]{1,0:T(8,128)(2,1)} %get-tuple-element.42), channel_id=1, source_target_pairs={{0,16},{8,24},{16,32},{24,40},{32,48},{40,56},{48,64},{56,72},{64,... | collective-permute-start | bytes 196616 | tf_op jit(solution)/shard_map/ppermute | solution.py:329
  40.0 17.9 %collective-permute-start.5 = (bf16[128,256]{1,0:T(8,128)(2,1)}, bf16[128,256]{1,0:T(8,128)(2,1)S(1)}, u32[]{:S(2)}, u32[]{:S(2)}) collective-permute-start(bf16[128,256]{1,0:T(8,128)(2,1)} %get-tuple-element.49), channel_id=1, source_target_pairs={{0,112},{8,120},{16,0},{24,8},{32,16},{40,24},{48,32},{56,40},{64,... | collective-permute-start | bytes 196616 | tf_op jit(solution)/shard_map/ppermute | solution.py:329
  46.4 1.3 %copy-start = (bf16[4,2,8,128,128]{4,3,2,1,0:T(8,128)(2,1)}, bf16[4,2,8,128,128]{4,3,2,1,0:T(8,128)(2,1)S(1)}, u32[]{:S(2)}) copy-start(bf16[4,2,8,128,128]{4,3,2,1,0:T(8,128)(2,1)S(1)} %repeat_kernel.1) | copy-start | bytes 6291460
  47.8 5.0 %copy-start.2 = (bf16[1,128,2048]{2,1,0:T(8,128)(2,1)S(1)}, bf16[1,128,2048]{2,1,0:T(8,128)(2,1)}, u32[]{:S(2)}) copy-start(bf16[1,128,2048]{2,1,0:T(8,128)(2,1)} %param.9) | copy-start | bytes 1572868
  47.8 5.0 %copy-start.3 = (bf16[1,128,2048]{2,1,0:T(8,128)(2,1)S(1)}, bf16[1,128,2048]{2,1,0:T(8,128)(2,1)}, u32[]{:S(2)}) copy-start(bf16[1,128,2048]{2,1,0:T(8,128)(2,1)} %param.13) | copy-start | bytes 1572868
  47.8 5.0 %copy-start.5 = (s32[1,4096]{1,0:T(1,128)S(1)}, s32[1,4096]{1,0:T(1,128)}, u32[]{:S(2)}) copy-start(s32[1,4096]{1,0:T(1,128)} %doc_ref) | copy-start | bytes 49156
  47.8 5.0 %copy-start.6 = (f32[1,16,128]{2,1,0:T(8,128)S(1)}, f32[1,16,128]{2,1,0:T(8,128)}, u32[]{:S(2)}) copy-start(f32[1,16,128]{2,1,0:T(8,128)} %param.14) | copy-start | bytes 24580
  47.8 34.6 %all-to-all-start.1 = ((bf16[4,2,8,128,128]{4,3,2,1,0:T(8,128)(2,1)}), bf16[4,2,8,128,128]{4,3,2,1,0:T(8,128)(2,1)S(1)}, u32[]{:S(2)}, u32[]{:S(2)}) async-start(bf16[4,2,8,128,128]{4,3,2,1,0:T(8,128)(2,1)} %copy-done), calls=%async_computation.1 | async-start | bytes 4194304 | tf_op jit(solution)/shard_map/all_to_all | solution.py:387
  52.8 1.0 copy-start.4
  61.4 8.4 %collective-permute-start.6 = (bf16[128,256]{1,0:T(8,128)(2,1)S(1)}, bf16[128,256]{1,0:T(8,128)(2,1)S(1)}, u32[]{:S(2)}, u32[]{:S(2)}) collective-permute-start(bf16[128,256]{1,0:T(8,128)(2,1)S(1)} %get-tuple-element.58), channel_id=1, source_target_pairs={{16,0},{24,8},{32,16},{40,24},{48,32},{56,40},{64,48},{72,56},{80,... | collective-permute-start | bytes 196616 | tf_op jit(solution)/shard_map/ppermute | solution.py:329
  62.7 8.5 %collective-permute-start.7 = (bf16[128,256]{1,0:T(8,128)(2,1)S(1)}, bf16[128,256]{1,0:T(8,128)(2,1)S(1)}, u32[]{:S(2)}, u32[]{:S(2)}) collective-permute-start(bf16[128,256]{1,0:T(8,128)(2,1)S(1)} %get-tuple-element.57.high_ref), channel_id=1, source_target_pairs={{0,16},{8,24},{16,32},{24,40},{32,48},{40,56},{48,64},{56,72},{64,... | collective-permute-start | bytes 196616 | tf_op jit(solution)/shard_map/ppermute | solution.py:329
  71.2 11.1 %collective-permute-start.9 = (bf16[192,256]{1,0:T(8,128)(2,1)S(1)}, bf16[192,256]{1,0:T(8,128)(2,1)S(1)}, u32[]{:S(2)}, u32[]{:S(2)}) collective-permute-start(bf16[192,256]{1,0:T(8,128)(2,1)S(1)} %get-tuple-element.59.right_ref), channel_id=1, source_target_pairs={{0,8},{8,16},{16,24},{24,32},{32,40},{40,48},{48,56},{56,64},{64,7... | collective-permute-start | bytes 294920 | tf_op jit(solution)/shard_map/ppermute | solution.py:329
  76.2 6.2 %collective-permute-start.8 = (bf16[128,256]{1,0:T(8,128)(2,1)S(1)}, bf16[128,256]{1,0:T(8,128)(2,1)S(1)}, u32[]{:S(2)}, u32[]{:S(2)}) collective-permute-start(bf16[128,256]{1,0:T(8,128)(2,1)S(1)} %get-tuple-element.60), channel_id=1, source_target_pairs={{8,0},{16,8},{24,16},{32,24},{40,32},{48,40},{56,48},{64,56},{72,6... | collective-permute-start | bytes 196616 | tf_op jit(solution)/shard_map/ppermute | solution.py:329
  99.1 24.7 %all-to-all-start.3 = ((bf16[16,64,128]{2,1,0:T(8,128)(2,1)}), bf16[16,64,128]{2,1,0:T(8,128)(2,1)S(1)}, u32[]{:S(2)}, u32[]{:S(2)}) async-start(bf16[16,64,128]{2,1,0:T(8,128)(2,1)} %weight_kernel.1), calls=%async_computation.3 | async-start | bytes 524288 | tf_op jit(solution)/shard_map/all_to_all | solution.py:435
  107.3 5.2 %collective-permute-start.10 = (bf16[64,256]{1,0:T(8,128)(2,1)S(1)}, bf16[64,256]{1,0:T(8,128)(2,1)S(1)}, u32[]{:S(2)}, u32[]{:S(2)}) collective-permute-start(bf16[64,256]{1,0:T(8,128)(2,1)S(1)} %get-tuple-element.66), channel_id=1, source_target_pairs={{232,104},{240,112},{248,120},{0,128},{8,136},{16,144},{233,105},{... | collective-permute-start | bytes 98312 | tf_op jit(solution)/shard_map/ppermute | solution.py:335

commit v6 on v5

--- a/solution.py
+++ b/solution.py
@@ -20,7 +20,7 @@
 SMEM = pl.BlockSpec(memory_space=pltpu.SMEM)
 VMEM = pl.BlockSpec(memory_space=pltpu.VMEM)
 ANY = pl.BlockSpec(memory_space=pl.ANY)
-COST = {"prepare": 4, "first": 4, "widen": 0.1, "repeat": 4, "near": 0.3, "far": 0.3, "turn": 10, "close": 5, "finish": 0.5}
+COST = {"prepare": 2, "first": 10, "widen": 0.1, "repeat": 1, "near": 0.3, "far": 0.3, "turn": 10, "close": 5, "finish": 0.5}
 
 
 def call(kernel, outs, in_specs, us, scratch=(), mib=8):
@@ -171,12 +171,12 @@
     lax.fori_loop(0, lse_rows.shape[1], step, 0)
 
 
-def near_kernel(idx_ref, q_rows, g_rows, low_ref, high_ref, lse_rows, delta_rows, live_ref, dq_ref, kv_ref):
+def near_kernel(q_rows, g_rows, low_ref, high_ref, far_ref, lse_rows, delta_rows, live_ref, dq_ref, kv_ref):
     keys = (low_ref[:, :HD], high_ref[:, :HD])
     values = (low_ref[:, HD:], high_ref[:, HD:])
 
     def write(rows, lanes, value):
-        dq_ref[rows, lanes] = value
+        dq_ref[0, rows, lanes] = (value + far_ref[rows, lanes]).astype(BF)
 
     attend(q_rows, g_rows, keys, values, live_ref[0], kv_ref, lse_rows, delta_rows, write)
 
@@ -190,7 +190,6 @@
     right_ref,
     left2_ref,
     right2_ref,
-    near_ref,
     lse_rows,
     delta_rows,
     live_ref,
@@ -208,7 +207,7 @@
     values = (left2_ref[:, HD:], upper[:, HD:])
 
     def write(rows, lanes, value):
-        dq_ref[0, rows, lanes] = (value + near_ref[rows, lanes]).astype(BF)
+        dq_ref[rows, lanes] = value
 
     attend(q_rows, g_rows, keys, values, live_ref[1], acc_ref, lse_rows, delta_rows, write)
     low_ref[:C] = acc_ref[0, :C].astype(BF)
@@ -291,15 +290,14 @@
         copy.wait()
 
 
-def repeat_kernel(mine_ref, theirs_ref, out_ref):
+def repeat_kernel(x_ref, out_ref):
     for i in range(out_ref.shape[0]):
-        out_ref[i, 0] = mine_ref[...]
-        out_ref[i, 1] = theirs_ref[...]
-
-
-def weight_kernel(scale, core_ref, x_ref, dv_ref, out_ref):
-    pieces, _, parts, tokens, width = x_ref.shape
-    each = out_ref.shape[0] // (2 * pieces)
+        out_ref[i] = x_ref[...]
+
+
+def weight_kernel(scale, x_ref, dv_ref, out_ref):
+    pieces, parts, tokens, width = x_ref.shape
+    each = out_ref.shape[0] // pieces
     rows = []
     for i in range(parts):
         lower, upper = dv_ref[i, :C].astype(F32), dv_ref[i, C : 2 * C].astype(F32)
@@ -311,11 +309,9 @@
         rows += [lower.astype(BF), upper.astype(BF)]
     dv = jnp.concatenate(rows, axis=0).T
     for i in range(pieces):
-        for j, core in enumerate((core_ref[0], 1 - core_ref[0])):
-            x = x_ref[i, j].reshape(parts * tokens, width)
-            flat = jnp.dot(dv, x, preferred_element_type=F32) * scale
-            flat = flat.T.astype(BF).reshape(each, width // each, HD)
-            out_ref[pl.ds((2 * i + core) * each, each)] = flat
+        x = x_ref[i].reshape(parts * tokens, width)
+        flat = jnp.dot(dv, x, preferred_element_type=F32) * scale
+        out_ref[i * each : (i + 1) * each] = flat.T.astype(BF).reshape(each, width // each, HD)
 
 
 def shift(value, by, wrap_half):
@@ -342,7 +338,7 @@
     rows = 2 * C
     groups = lax.axis_size(ROWS)
     steps = lax.axis_size("ctx_1")
-    pieces = lax.axis_size(TP)
+    pieces = lax.axis_size("tp_x")
     piece = layer_input.shape[2] // (groups * pieces)
     heads = width // HD
     group = min(4, heads)
@@ -359,7 +355,7 @@
         [pltpu.VMEM((rows, HD), BF), pltpu.VMEM((rows, HD), BF), pltpu.SemaphoreType.DMA((2,))],
         mib=56,
     )(place, key_heads, value_heads)
-    kv, part_of = lax.optimization_barrier((kv, lax.axis_index(TP).astype(jnp.int32).reshape(1)))
+    kv, part_of = lax.optimization_barrier((kv, lax.axis_index("tp_x").astype(jnp.int32).reshape(1)))
     cross = swap(cross, False)
     (chunks,) = call(
         chunk_kernel,
@@ -377,13 +373,12 @@
     low, high, send_low, send_high = call(
         at(widen_kernel, count), [pair] * 4, [SMEM] + [VMEM] * 4, COST["widen"]
     )(place, kv, cross, left, right)
-    _, mine = lax.optimization_barrier((send_low, mine))
     left2 = shift(send_low, 2, 1)
     right2 = shift(send_high, -2, 0)
-    theirs = lax.ppermute(mine, "core", [(0, 1), (1, 0)])
+    left2, mine = lax.optimization_barrier((left2, mine))
     (repeated,) = call(
-        repeat_kernel, [shape((pieces // 2, 2, groups, rows, piece), BF)], [VMEM] * 2, COST["repeat"]
-    )(mine, theirs)
+        repeat_kernel, [shape((pieces, groups, rows, piece), BF)], [VMEM], COST["repeat"]
+    )(mine)
     tokens = lax.all_to_all(repeated, "tp_x", 0, 0, tiled=True)
     docs, repeated = lax.optimization_barrier((doc_ids, repeated))
     q_rows, g_rows, lse_rows, delta_rows, live = call(
@@ -393,23 +388,23 @@
         COST["prepare"],
         mib=12,
     )(place, queries[0], out_grad[0], attn_out[0], log_sums[0], docs)
-    near_query, near_kv = call(
-        near_kernel,
-        [shape((rows, width), F32), shape((2, 128, 2 * HD), F32)],
-        [SMEM] + [VMEM] * 7,
-        COST["near"],
-        mib=12,
-    )(place, q_rows, g_rows, low, high, lse_rows, delta_rows, live)
-    query_grad, far_low, far_high = call(
+    far_query, far_low, far_high = call(
         at(far_kernel, count),
-        [shape((1, rows, width), BF), pair, pair],
-        [SMEM] + [VMEM] * 10,
+        [shape((rows, width), F32), pair, pair],
+        [SMEM] + [VMEM] * 9,
         COST["far"],
         [pltpu.VMEM((2, 128, 2 * HD), F32)],
         mib=12,
-    )(place, q_rows, g_rows, low, right, left2, right2, near_query, lse_rows, delta_rows, live)
+    )(place, q_rows, g_rows, low, right, left2, right2, lse_rows, delta_rows, live)
     low2 = shift(far_low, -2, 1)
     high2 = shift(far_high, 2, 0)
+    query_grad, near_kv = call(
+        near_kernel,
+        [shape((1, rows, width), BF), shape((2, 128, 2 * HD), F32)],
+        [VMEM] * 8,
+        COST["near"],
+        mib=12,
+    )(q_rows, g_rows, low, high, far_query, lse_rows, delta_rows, live)
     to_left, to_right = call(
         at(turn_kernel, count), [pair, three], [SMEM] + [VMEM] * 4, COST["turn"]
     )(place, near_kv, far_high, low2, high2)
@@ -427,10 +422,10 @@
     (part,) = call(
         at(weight_kernel, weight_scale),
         [shape((steps, piece * pieces // steps, HD), BF)],
-        [SMEM] + [VMEM] * 2,
+        [VMEM] * 2,
         1,
         mib=12,
-    )(lax.axis_index("core").astype(jnp.int32).reshape(1), tokens, everyone)
+    )(tokens, everyone)
     part, cross = lax.optimization_barrier((part, cross))
     parts = lax.all_to_all(part, "ctx_1", 0, 0, tiled=True)
     cross = swap(cross, True)

time: 125 us -> 118 us (0.944)
  the two profiles are of different devices: /device:TPU:10 before, /device:TPU:74 now
where the time goes in v6:
time: 118 us; the launch traced here: 117 us
  starting transfers between devices  48.3 us (41%)
  waiting for transfers between devices  31.1 us (26%)
  blocking collectives  20.6 us (17%)
  Pallas kernels  12.9 us (11%)
  local copies, waits for them, and re-layouts  2.41 us (2%)
    ppermute x8, starting transfers between devices, shift(): return lax.ppermute(value, CTX, pairs)  24.6 us
    all_to_all x1, blocking collectives, body(): everyone = lax.all_to_all(spread, ROWS, 0, 0, tiled=True)  20.6 us
    ppermute x8, waiting for transfers between devices, shift(): return lax.ppermute(value, CTX, pairs)  20.3 us
    all_to_all x1, waiting for transfers between devices, body(): parts = lax.all_to_all(part, 'ctx_1', 0, 0, tiled=True)  9.21 us
    all_to_all x1, starting transfers between devices, body(): mine = lax.all_to_all(chunks, ROWS, 0, 0, tiled=True)  8.62 us
    all_to_all x1, starting transfers between devices, body(): parts = lax.all_to_all(part, 'ctx_1', 0, 0, tiled=True)  5.27 us
    all_to_all x1, starting transfers between devices, body(): tokens = lax.all_to_all(repeated, 'tp_x', 0, 0, tiled=True)  4.97 us
    ppermute x2, starting transfers between devices, swap(): lax.ppermute(value, CTX, [(b, a) for a, b in pairs] if back else pairs)  4.83 us
  transfers between devices with their start and end apart: 13, of which 5 were waited for; matrix products, arithmetic and copies ran while one was open for 0% of the time, Pallas kernels for 9%

profile of v6, /device:TPU:74, one launch (start us, length us, event | category | flops | bytes accessed | tf_op | source)
XLA Modules:
  0.0 116.8 jit_solution(245031429241397225)
XLA Ops:
  0.6 1.6 %pack_kernel.1 = (bf16[128,256]{1,0:T(8,128)(2,1)}, bf16[64,256]{1,0:T(8,128)(2,1)}) custom-call(s32[1]{0:T(128)} %bitcast.idx_ref, bf16[1,128,128]{2,1,0:T(8,128)(2,1)} %k_ref.1, bf16[1,128,128]{2,1,0:T(8,128)(2,1)} %v_ref.1), custom_call_target="tpu_custom_call" | custom-call | flops 1000000000 | tf_op jit(solution)/shard_map/pack_kernel/pallas_call | solution.py:350
  2.2 1.3 %collective-permute-start = (bf16[64,256]{1,0:T(8,128)(2,1)}, bf16[64,256]{1,0:T(8,128)(2,1)S(1)}, u32[]{:S(2)}, u32[]{:S(2)}) collective-permute-start(bf16[64,256]{1,0:T(8,128)(2,1)} %get-tuple-element.40), channel_id=1, source_target_pairs={{104,232},{112,240},{120,248},{128,0},{136,8},{144,16},{105,233},{... | collective-permute-start | bytes 98312 | tf_op jit(solution)/shard_map/ppermute | solution.py:331
  4.5 8.6 %all-to-all-start = ((bf16[8,128,256]{2,1,0:T(8,128)(2,1)}), bf16[8,128,256]{2,1,0:T(8,128)(2,1)S(1)}, u32[]{:S(2)}, u32[]{:S(2)}) async-start(bf16[8,128,256]{2,1,0:T(8,128)(2,1)} %chunk_kernel.1), calls=%async_computation | async-start | bytes 1048576 | tf_op jit(solution)/shard_map/all_to_all | solution.py:367
  13.2 1.9 %collective-permute-start.2 = (bf16[192,256]{1,0:T(8,128)(2,1)S(1)}, bf16[192,256]{1,0:T(8,128)(2,1)S(1)}, u32[]{:S(2)}, u32[]{:S(2)}) collective-permute-start(bf16[192,256]{1,0:T(8,128)(2,1)S(1)} %get-tuple-element.42), channel_id=1, source_target_pairs={{0,120},{8,0},{16,8},{24,16},{32,24},{40,32},{48,40},{56,48},{64,5... | collective-permute-start | bytes 294920 | tf_op jit(solution)/shard_map/ppermute | solution.py:325
  15.1 4.3 %collective-permute-start.1 = (bf16[128,256]{1,0:T(8,128)(2,1)S(1)}, bf16[128,256]{1,0:T(8,128)(2,1)S(1)}, u32[]{:S(2)}, u32[]{:S(2)}) collective-permute-start(bf16[128,256]{1,0:T(8,128)(2,1)S(1)} %get-tuple-element.41), channel_id=1, source_target_pairs={{0,8},{8,16},{16,24},{24,32},{32,40},{40,48},{48,56},{56,64},{64,7... | collective-permute-start | bytes 196616 | tf_op jit(solution)/shard_map/ppermute | solution.py:325
  19.4 16.9 %collective-permute-done.1.left_ref = bf16[128,256]{1,0:T(8,128)(2,1)S(1)} collective-permute-done((bf16[128,256]{1,0:T(8,128)(2,1)S(1)}, bf16[128,256]{1,0:T(8,128)(2,1)S(1)}, u32[]{:S(2)}, u32[]{:S(2)}) %collective-permute-start.1) | collective-permute-done | bytes 65568 | tf_op jit(solution)/shard_map/ppermute | solution.py:325
  36.9 1.3 %collective-permute-start.3 = (bf16[128,256]{1,0:T(8,128)(2,1)S(1)}, bf16[128,256]{1,0:T(8,128)(2,1)S(1)}, u32[]{:S(2)}, u32[]{:S(2)}) collective-permute-start(bf16[128,256]{1,0:T(8,128)(2,1)S(1)} %get-tuple-element.43), channel_id=1, source_target_pairs={{0,16},{8,24},{16,32},{24,40},{32,48},{40,56},{48,64},{56,72},{64,... | collective-permute-start | bytes 196616 | tf_op jit(solution)/shard_map/ppermute | solution.py:325
  38.2 4.5 %collective-permute-start.4 = (bf16[128,256]{1,0:T(8,128)(2,1)}, bf16[128,256]{1,0:T(8,128)(2,1)S(1)}, u32[]{:S(2)}, u32[]{:S(2)}) collective-permute-start(bf16[128,256]{1,0:T(8,128)(2,1)} %get-tuple-element.52), channel_id=1, source_target_pairs={{0,112},{8,120},{16,0},{24,8},{32,16},{40,24},{48,32},{56,40},{64,... | collective-permute-start | bytes 196616 | tf_op jit(solution)/shard_map/ppermute | solution.py:325
  42.9 1.3 %copy-done = bf16[4,8,128,256]{3,2,1,0:T(8,128)(2,1)} copy-done((bf16[4,8,128,256]{3,2,1,0:T(8,128)(2,1)}, bf16[4,8,128,256]{3,2,1,0:T(8,128)(2,1)S(1)}, u32[]{:S(2)}) %copy-start) | copy-done | bytes 2097176
  44.3 5.0 %all-to-all-start.1 = ((bf16[4,8,128,256]{3,2,1,0:T(8,128)(2,1)}), bf16[4,8,128,256]{3,2,1,0:T(8,128)(2,1)S(1)}, u32[]{:S(2)}, u32[]{:S(2)}) async-start(bf16[4,8,128,256]{3,2,1,0:T(8,128)(2,1)} %copy-done), calls=%async_computation.1 | async-start | bytes 4194304 | tf_op jit(solution)/shard_map/all_to_all | solution.py:382
  50.3 1.3 %prepare_kernel.1 = (bf16[2,4,256,128]{3,2,1,0:T(8,128)(2,1)S(1)}, bf16[2,4,256,128]{3,2,1,0:T(8,128)(2,1)S(1)}, f32[2,4,256,128]{3,2,1,0:T(8,128)S(1)}, f32[2,4...) custom-call(s32[1]{0:T(128)} %bitcast.idx_ref, bf16[128,2048]{1,0:T(8,128)(2,1)S(1)} %bitcast.6, ...), custom_call_target="tpu_custom_call" | custom-call | flops 2000000000 | tf_op jit(solution)/shard_map/prepare_kernel/pallas_call | solution.py:384
  51.6 2.8 %far_kernel.1 = (f32[128,2048]{1,0:T(8,128)S(1)}, bf16[128,256]{1,0:T(8,128)(2,1)S(1)}, bf16[128,256]{1,0:T(8,128)(2,1)S(1)}) custom-call(s32[1]{0:T(128)} %bitcast.idx_ref, bf16[2,4,256,128]{3,2,1,0:T(8,128)(2,1)S(1)} %get-tuple-element.47.q_rows, bf16[2,4,256,128]{3,2,1,0:T(8,128)(2,1)S(1)} %get-tuple-element.48.g_rows, ...), custom_call_target="tpu_custom_call" | custom-call | flops 300000000 | tf_op jit(solution)/shard_map/far_kernel/pallas_call | solution.py:391
  54.4 1.3 %collective-permute-start.5 = (bf16[128,256]{1,0:T(8,128)(2,1)S(1)}, bf16[128,256]{1,0:T(8,128)(2,1)S(1)}, u32[]{:S(2)}, u32[]{:S(2)}) collective-permute-start(bf16[128,256]{1,0:T(8,128)(2,1)S(1)} %get-tuple-element.60), channel_id=1, source_target_pairs={{16,0},{24,8},{32,16},{40,24},{48,32},{56,40},{64,48},{72,56},{80,... | collective-permute-start | bytes 196616 | tf_op jit(solution)/shard_map/ppermute | solution.py:325
  55.7 5.4 %collective-permute-start.6 = (bf16[128,256]{1,0:T(8,128)(2,1)S(1)}, bf16[128,256]{1,0:T(8,128)(2,1)S(1)}, u32[]{:S(2)}, u32[]{:S(2)}) collective-permute-start(bf16[128,256]{1,0:T(8,128)(2,1)S(1)} %get-tuple-element.59.high_ref), channel_id=1, source_target_pairs={{0,16},{8,24},{16,32},{24,40},{32,48},{40,56},{48,64},{56,72},{64,... | collective-permute-start | bytes 196616 | tf_op jit(solution)/shard_map/ppermute | solution.py:325
  61.2 3.5 %near_kernel.1 = (bf16[1,128,2048]{2,1,0:T(8,128)(2,1)}, f32[2,128,256]{2,1,0:T(8,128)S(1)}) custom-call(bf16[2,4,256,128]{3,2,1,0:T(8,128)(2,1)S(1)} %get-tuple-element.47.q_rows, bf16[2,4,256,128]{3,2,1,0:T(8,128)(2,1)S(1)} %get-tuple-element.48.g_rows, bf16[128,256]{1,0:T(8,128)(2,1)S(1)} %get-tuple-element.49.near_low_ref.low_ref, ...), custom_call_target="tpu_custom_call" | custom-call | flops 300000000 | tf_op jit(solution)/shard_map/near_kernel/pallas_call | solution.py:401
  65.8 1.9 %collective-permute-start.8 = (bf16[192,256]{1,0:T(8,128)(2,1)S(1)}, bf16[192,256]{1,0:T(8,128)(2,1)S(1)}, u32[]{:S(2)}, u32[]{:S(2)}) collective-permute-start(bf16[192,256]{1,0:T(8,128)(2,1)S(1)} %get-tuple-element.61.right_ref), channel_id=1, source_target_pairs={{0,8},{8,16},{16,24},{24,32},{32,40},{40,48},{48,56},{56,64},{64,7... | collective-permute-start | bytes 294920 | tf_op jit(solution)/shard_map/ppermute | solution.py:325
  67.8 3.9 %collective-permute-start.7 = (bf16[128,256]{1,0:T(8,128)(2,1)S(1)}, bf16[128,256]{1,0:T(8,128)(2,1)S(1)}, u32[]{:S(2)}, u32[]{:S(2)}) collective-permute-start(bf16[128,256]{1,0:T(8,128)(2,1)S(1)} %get-tuple-element.62), channel_id=1, source_target_pairs={{8,0},{16,8},{24,16},{32,24},{40,32},{48,40},{56,48},{64,56},{72,6... | collective-permute-start | bytes 196616 | tf_op jit(solution)/shard_map/ppermute | solution.py:325
  71.7 2.2 %collective-permute-done.7.low1_ref = bf16[128,256]{1,0:T(8,128)(2,1)S(1)} collective-permute-done((bf16[128,256]{1,0:T(8,128)(2,1)S(1)}, bf16[128,256]{1,0:T(8,128)(2,1)S(1)}, u32[]{:S(2)}, u32[]{:S(2)}) %collective-permute-start.7) | collective-permute-done | bytes 65568 | tf_op jit(solution)/shard_map/ppermute | solution.py:325
  74.0 20.6 %all_to_all.20.dv_ref = bf16[8,192,128]{2,1,0:T(8,128)(2,1)S(1)} all-to-all(bf16[8,192,128]{2,1,0:T(8,128)(2,1)S(1)} %get-tuple-element.66), channel_id=1, replica_groups=mesh['dp'=4,'ctx_0'=2,'ctx_1'=16,'tp_x'=4,'core'=2] {'dp','ctx_0'}, dimensions={0} | all-to-all | bytes 786432 | tf_op jit(solution)/shard_map/all_to_all | solution.py:420
  94.6 1.3 %weight_kernel.1 = bf16[16,64,128]{2,1,0:T(8,128)(2,1)} custom-call(bf16[4,8,128,256]{3,2,1,0:T(8,128)(2,1)S(1)} %all-to-all-done.1.x_ref, bf16[8,192,128]{2,1,0:T(8,128)(2,1)S(1)} %all_to_all.20.dv_ref), custom_call_target="tpu_custom_call" | custom-call | flops 1000000000 | tf_op jit(solution)/shard_map/weight_kernel/pallas_call | solution.py:422
  95.9 5.3 %all-to-all-start.3 = ((bf16[16,64,128]{2,1,0:T(8,128)(2,1)}), bf16[16,64,128]{2,1,0:T(8,128)(2,1)S(1)}, u32[]{:S(2)}, u32[]{:S(2)}) async-start(bf16[16,64,128]{2,1,0:T(8,128)(2,1)} %weight_kernel.1), calls=%async_computation.3 | async-start | bytes 524288 | tf_op jit(solution)/shard_map/all_to_all | solution.py:430
  101.2 3.5 %collective-permute-start.9 = (bf16[64,256]{1,0:T(8,128)(2,1)S(1)}, bf16[64,256]{1,0:T(8,128)(2,1)S(1)}, u32[]{:S(2)}, u32[]{:S(2)}) collective-permute-start(bf16[64,256]{1,0:T(8,128)(2,1)S(1)} %get-tuple-element.68), channel_id=1, source_target_pairs={{232,104},{240,112},{248,120},{0,128},{8,136},{16,144},{233,105},{... | collective-permute-start | bytes 98312 | tf_op jit(solution)/shard_map/ppermute | solution.py:331
  104.7 1.6 %collective-permute-done.9.cross_ref = bf16[64,256]{1,0:T(8,128)(2,1)S(1)} collective-permute-done((bf16[64,256]{1,0:T(8,128)(2,1)S(1)}, bf16[64,256]{1,0:T(8,128)(2,1)S(1)}, u32[]{:S(2)}, u32[]{:S(2)}) %collective-permute-start.9) | collective-permute-done | bytes 32800 | tf_op jit(solution)/shard_map/ppermute | solution.py:331
  106.9 9.2 %all-to-all-done.3 = bf16[16,64,128]{2,1,0:T(8,128)(2,1)S(1)} async-done(((bf16[16,64,128]{2,1,0:T(8,128)(2,1)}), bf16[16,64,128]{2,1,0:T(8,128)(2,1)S(1)}, u32[]{:S(2)}, u32[]{:S(2)}) %all-to-all-start.3) | async-done | bytes 262176 | tf_op jit(solution)/shard_map/all_to_all | solution.py:430
  (32 shorter events, 5.4 us)
Async XLA Ops:
  0.6 2.9 %copy-start.1 = (bf16[1,128,8192]{2,1,0:T(8,128)(2,1)S(1)}, bf16[1,128,8192]{2,1,0:T(8,128)(2,1)}, u32[]{:S(2)}) copy-start(bf16[1,128,8192]{2,1,0:T(8,128)(2,1)} %x_ref.1) | copy-start | bytes 6291460
  2.2 10.9 %collective-permute-start = (bf16[64,256]{1,0:T(8,128)(2,1)}, bf16[64,256]{1,0:T(8,128)(2,1)S(1)}, u32[]{:S(2)}, u32[]{:S(2)}) collective-permute-start(bf16[64,256]{1,0:T(8,128)(2,1)} %get-tuple-element.40), channel_id=1, source_target_pairs={{104,232},{112,240},{120,248},{128,0},{136,8},{144,16},{105,233},{... | collective-permute-start | bytes 98312 | tf_op jit(solution)/shard_map/ppermute | solution.py:331
  3.6 9.6 %copy-start.7 = (bf16[128,256]{1,0:T(8,128)(2,1)S(1)}, bf16[128,256]{1,0:T(8,128)(2,1)}, u32[]{:S(2)}) copy-start(bf16[128,256]{1,0:T(8,128)(2,1)} %get-tuple-element.39.kv_ref) | copy-start | bytes 196612
  4.5 38.2 %all-to-all-start = ((bf16[8,128,256]{2,1,0:T(8,128)(2,1)}), bf16[8,128,256]{2,1,0:T(8,128)(2,1)S(1)}, u32[]{:S(2)}, u32[]{:S(2)}) async-start(bf16[8,128,256]{2,1,0:T(8,128)(2,1)} %chunk_kernel.1), calls=%async_computation | async-start | bytes 1048576 | tf_op jit(solution)/shard_map/all_to_all | solution.py:367
  13.2 23.1 %collective-permute-start.2 = (bf16[192,256]{1,0:T(8,128)(2,1)S(1)}, bf16[192,256]{1,0:T(8,128)(2,1)S(1)}, u32[]{:S(2)}, u32[]{:S(2)}) collective-permute-start(bf16[192,256]{1,0:T(8,128)(2,1)S(1)} %get-tuple-element.42), channel_id=1, source_target_pairs={{0,120},{8,0},{16,8},{24,16},{32,24},{40,32},{48,40},{56,48},{64,5... | collective-permute-start | bytes 294920 | tf_op jit(solution)/shard_map/ppermute | solution.py:325
  15.1 21.2 %collective-permute-start.1 = (bf16[128,256]{1,0:T(8,128)(2,1)S(1)}, bf16[128,256]{1,0:T(8,128)(2,1)S(1)}, u32[]{:S(2)}, u32[]{:S(2)}) collective-permute-start(bf16[128,256]{1,0:T(8,128)(2,1)S(1)} %get-tuple-element.41), channel_id=1, source_target_pairs={{0,8},{8,16},{16,24},{24,32},{32,40},{40,48},{48,56},{56,64},{64,7... | collective-permute-start | bytes 196616 | tf_op jit(solution)/shard_map/ppermute | solution.py:325
  36.9 5.8 %collective-permute-start.3 = (bf16[128,256]{1,0:T(8,128)(2,1)S(1)}, bf16[128,256]{1,0:T(8,128)(2,1)S(1)}, u32[]{:S(2)}, u32[]{:S(2)}) collective-permute-start(bf16[128,256]{1,0:T(8,128)(2,1)S(1)} %get-tuple-element.43), channel_id=1, source_target_pairs={{0,16},{8,24},{16,32},{24,40},{32,48},{40,56},{48,64},{56,72},{64,... | collective-permute-start | bytes 196616 | tf_op jit(solution)/shard_map/ppermute | solution.py:325
  38.2 13.4 %collective-permute-start.4 = (bf16[128,256]{1,0:T(8,128)(2,1)}, bf16[128,256]{1,0:T(8,128)(2,1)S(1)}, u32[]{:S(2)}, u32[]{:S(2)}) collective-permute-start(bf16[128,256]{1,0:T(8,128)(2,1)} %get-tuple-element.52), channel_id=1, source_target_pairs={{0,112},{8,120},{16,0},{24,8},{32,16},{40,24},{48,32},{56,40},{64,... | collective-permute-start | bytes 196616 | tf_op jit(solution)/shard_map/ppermute | solution.py:325
  42.9 1.4 %copy-start = (bf16[4,8,128,256]{3,2,1,0:T(8,128)(2,1)}, bf16[4,8,128,256]{3,2,1,0:T(8,128)(2,1)S(1)}, u32[]{:S(2)}) copy-start(bf16[4,8,128,256]{3,2,1,0:T(8,128)(2,1)S(1)} %repeat_kernel.1) | copy-start | bytes 6291460
  44.3 5.0 %copy-start.2 = (bf16[1,128,2048]{2,1,0:T(8,128)(2,1)S(1)}, bf16[1,128,2048]{2,1,0:T(8,128)(2,1)}, u32[]{:S(2)}) copy-start(bf16[1,128,2048]{2,1,0:T(8,128)(2,1)} %param.9) | copy-start | bytes 1572868
  44.3 5.0 %copy-start.3 = (bf16[1,128,2048]{2,1,0:T(8,128)(2,1)S(1)}, bf16[1,128,2048]{2,1,0:T(8,128)(2,1)}, u32[]{:S(2)}) copy-start(bf16[1,128,2048]{2,1,0:T(8,128)(2,1)} %param.13) | copy-start | bytes 1572868
  44.3 5.0 %copy-start.5 = (s32[1,4096]{1,0:T(1,128)S(1)}, s32[1,4096]{1,0:T(1,128)}, u32[]{:S(2)}) copy-start(s32[1,4096]{1,0:T(1,128)} %doc_ref) | copy-start | bytes 49156
  44.3 5.0 %copy-start.6 = (f32[1,16,128]{2,1,0:T(8,128)S(1)}, f32[1,16,128]{2,1,0:T(8,128)}, u32[]{:S(2)}) copy-start(f32[1,16,128]{2,1,0:T(8,128)} %param.14) | copy-start | bytes 24580
  44.3 29.7 %all-to-all-start.1 = ((bf16[4,8,128,256]{3,2,1,0:T(8,128)(2,1)}), bf16[4,8,128,256]{3,2,1,0:T(8,128)(2,1)S(1)}, u32[]{:S(2)}, u32[]{:S(2)}) async-start(bf16[4,8,128,256]{3,2,1,0:T(8,128)(2,1)} %copy-done), calls=%async_computation.1 | async-start | bytes 4194304 | tf_op jit(solution)/shard_map/all_to_all | solution.py:382
  49.3 1.0 copy-start.4
  54.4 10.2 %collective-permute-start.5 = (bf16[128,256]{1,0:T(8,128)(2,1)S(1)}, bf16[128,256]{1,0:T(8,128)(2,1)S(1)}, u32[]{:S(2)}, u32[]{:S(2)}) collective-permute-start(bf16[128,256]{1,0:T(8,128)(2,1)S(1)} %get-tuple-element.60), channel_id=1, source_target_pairs={{16,0},{24,8},{32,16},{40,24},{48,32},{56,40},{64,48},{72,56},{80,... | collective-permute-start | bytes 196616 | tf_op jit(solution)/shard_map/ppermute | solution.py:325
  55.7 10.1 %collective-permute-start.6 = (bf16[128,256]{1,0:T(8,128)(2,1)S(1)}, bf16[128,256]{1,0:T(8,128)(2,1)S(1)}, u32[]{:S(2)}, u32[]{:S(2)}) collective-permute-start(bf16[128,256]{1,0:T(8,128)(2,1)S(1)} %get-tuple-element.59.high_ref), channel_id=1, source_target_pairs={{0,16},{8,24},{16,32},{24,40},{32,48},{40,56},{48,64},{56,72},{64,... | collective-permute-start | bytes 196616 | tf_op jit(solution)/shard_map/ppermute | solution.py:325
  65.8 8.1 %collective-permute-start.8 = (bf16[192,256]{1,0:T(8,128)(2,1)S(1)}, bf16[192,256]{1,0:T(8,128)(2,1)S(1)}, u32[]{:S(2)}, u32[]{:S(2)}) collective-permute-start(bf16[192,256]{1,0:T(8,128)(2,1)S(1)} %get-tuple-element.61.right_ref), channel_id=1, source_target_pairs={{0,8},{8,16},{16,24},{24,32},{32,40},{40,48},{48,56},{56,64},{64,7... | collective-permute-start | bytes 294920 | tf_op jit(solution)/shard_map/ppermute | solution.py:325
  67.8 6.2 %collective-permute-start.7 = (bf16[128,256]{1,0:T(8,128)(2,1)S(1)}, bf16[128,256]{1,0:T(8,128)(2,1)S(1)}, u32[]{:S(2)}, u32[]{:S(2)}) collective-permute-start(bf16[128,256]{1,0:T(8,128)(2,1)S(1)} %get-tuple-element.62), channel_id=1, source_target_pairs={{8,0},{16,8},{24,16},{32,24},{40,32},{48,40},{56,48},{64,56},{72,6... | collective-permute-start | bytes 196616 | tf_op jit(solution)/shard_map/ppermute | solution.py:325
  95.9 20.2 %all-to-all-start.3 = ((bf16[16,64,128]{2,1,0:T(8,128)(2,1)}), bf16[16,64,128]{2,1,0:T(8,128)(2,1)S(1)}, u32[]{:S(2)}, u32[]{:S(2)}) async-start(bf16[16,64,128]{2,1,0:T(8,128)(2,1)} %weight_kernel.1), calls=%async_computation.3 | async-start | bytes 524288 | tf_op jit(solution)/shard_map/all_to_all | solution.py:430
  101.2 5.1 %collective-permute-start.9 = (bf16[64,256]{1,0:T(8,128)(2,1)S(1)}, bf16[64,256]{1,0:T(8,128)(2,1)S(1)}, u32[]{:S(2)}, u32[]{:S(2)}) collective-permute-start(bf16[64,256]{1,0:T(8,128)(2,1)S(1)} %get-tuple-element.68), channel_id=1, source_target_pairs={{232,104},{240,112},{248,120},{0,128},{8,136},{16,144},{233,105},{... | collective-permute-start | bytes 98312 | tf_op jit(solution)/shard_map/ppermute | solution.py:331
